TPU v7x, 32 devices: a whole 2x2x4 slice. The times are simulated.
32 devices in a mesh: groups: 2 (over x), src: 8 (over z, y), tgt: 2 (over core).
Axes of the slice: x: 2, y: 2, z: 4, core: 2. Of those that a mesh axis runs over, the one named last changes fastest.
Arguments:
- source_embed: bfloat16 [32768, 256], P(('groups', 'src')), parts along dimension 0, may hold values from -7 to 7
- target_embed: bfloat16 [32768, 256], P(('groups', 'tgt', 'src')), parts along dimension 0, may hold values from -6 to 6
- source_mass: float32 [32768], P(('groups', 'src')), parts along dimension 0, may hold values from 0.05 to 20
- target_mass: float32 [32768], P(('groups', 'tgt')), parts along dimension 0, may hold values from 0.05 to 20
- target_start: float32 [32768], P(('groups', 'tgt')), parts along dimension 0, may hold values from -3 to 11
- tile_list: int32 [16, 2, 2, 128], P(('groups', 'src'), 'tgt'), parts along dimension 0, may hold values from 0 to 63, as said below
- tile_count: int32 [16, 2], P(('groups', 'src'), 'tgt'), parts along dimension 0, may hold values from 25 to 128, as said below
Outputs:
- source_potential: float32 [32768], P(('groups', 'src')), parts along dimension 0
- target_potential: float32 [32768], P(('groups', 'tgt')), parts along dimension 0
There are 2 independent parts, one for each index of `groups`. A program takes and returns all parts, laid end to end along the dimension named above; each array names one. Nothing has to cross between parts.
Inputs may be any that keep to these rules, and one draw needn't show every extreme that they name: `tile_list`: entry [s, t, 0, k] is a row block among the 16 blocks of src index s, entry [s, t, 1, k] a column block among the 64 blocks of tgt index t. The 128 tiles of a device are distinct; its first 16 are (r, (r + s * 16) mod 64) for r = 0 .. 15, so every row and every column of the whole has support. `tile_count`: number of live tiles of a device, which are the first ones of its list; in every part one device holds 128.
All inputs are finite; a program needn't handle non-finite values.
Results may differ from a plain program's by a relative error of at most 0.0004.
Values may be sent and summed in bfloat16 or wider, within the bound.
No kernel may reach another device: no remote copies, remote signals or barrier semaphores. Data moves between devices by JAX's collectives and lax.ppermute only.
A program may use at most 64 MiB of HBM per device.

v0:
```python
import math

import jax
import jax.numpy as jnp
from jax import lax
from jax.experimental import pallas as pl
from jax.experimental.pallas import tpu as pltpu
from jax.sharding import PartitionSpec as P

TILE = 128
EPSILON = 0.05
FLOOR = -1e30
MAKE_UNROLL = 16
READ_UNROLL = 8
PADDING = max(MAKE_UNROLL, READ_UNROLL)
VMEM_LIMIT = 4 * 1024 * 1024


def hop(value, src_mask, tgt_mask=0):
    cores = lax.axis_size("tgt")
    total = lax.axis_size("src") * cores
    flip = src_mask * cores + tgt_mask
    return lax.ppermute(value, ("src", "tgt"), [(i, i ^ flip) for i in range(total)])


def half_norms(rows):
    wide = rows.astype(jnp.float32)
    return 0.5 * jnp.sum(wide * wide, axis=-1).reshape(-1, TILE)


def share_kernel(side, source, first, second, share, sems):
    begin = lax.axis_index("tgt") * side
    move = pltpu.make_async_copy(source.at[pl.ds(begin, side)], share, sems.at[0])
    move.start()
    move.wait()


def list_kernel(half, src_rows, col_blocks, slots, own, peer, ids):
    upper = lax.axis_index("src") // half
    listed = own.shape[3]

    def scan(refs, shift):
        def step(k, found):
            col = refs[0, 0, 1, k] - upper * col_blocks
            ids[found] = refs[0, 0, 0, k] + shift * src_rows
            ids[slots + found] = col
            return found + ((col >= 0) & (col < col_blocks)).astype(jnp.int32)

        return step

    found = lax.fori_loop(0, listed, scan(own, upper), 0, unroll=8)
    found = lax.fori_loop(0, listed, scan(peer, 1 - upper), found, unroll=8)
    for extra in range(PADDING):
        ids[found + extra] = 0
        ids[slots + found + extra] = 0
    ids[2 * slots] = found


def merge_logs(parts):
    peak = parts[0]
    for part in parts[1:]:
        peak = jnp.maximum(peak, part)
    return peak + jnp.log2(sum(jnp.exp2(part - peak) for part in parts))


def spread_out(potential, spread):
    turned = jnp.transpose(potential)
    for block in range(potential.shape[0]):
        spread[block] = jnp.broadcast_to(turned[:, block : block + 1], (TILE, TILE))


def clear(peaks, sums):
    peaks[...] = jnp.full(peaks.shape, FLOOR, jnp.float32)
    sums[...] = jnp.zeros(sums.shape, jnp.float32)


def sweep(unroll, count, scores_of, known_of, reduced_of, spread, peaks, sums):
    dummy = peaks.shape[0] - 1

    def merge(carry):
        for place, peak, summed in carry:
            old_peak = peaks[place]
            old_sum = sums[place]
            top = jnp.maximum(old_peak, peak)
            peaks[place] = top
            sums[place] = old_sum * jnp.exp2(old_peak - top) + summed * jnp.exp2(peak - top)

    def turn(index, carry):
        merge(carry)
        fresh = []
        for lane in range(unroll):
            slot = index * unroll + lane
            scores = (scores_of(slot) + spread[known_of(slot)]).reshape(TILE // 8, 8, TILE)
            peak = jnp.max(scores, axis=0)
            summed = jnp.sum(jnp.exp2(scores - peak[None]), axis=0)
            fresh.append((jnp.where(slot < count, reduced_of(slot), dummy), peak, summed))
        return tuple(fresh)

    nothing = tuple(
        (jnp.int32(dummy), jnp.full((8, TILE), FLOOR, jnp.float32), jnp.zeros((8, TILE), jnp.float32))
        for lane in range(unroll)
    )
    merge(lax.fori_loop(0, (count + unroll - 1) // unroll, turn, nothing))


def log_sums(peaks, sums):
    top = peaks[0 : peaks.shape[0] - 1]
    peak = jnp.max(top, axis=1)
    summed = jnp.sum(sums[0 : top.shape[0]] * jnp.exp2(top - peak[:, None, :]), axis=1)
    live = summed > 0.0
    return jnp.where(live, peak + jnp.log2(jnp.where(live, summed, 1.0)), FLOOR)


def first_kernel(scale, half, slots, places, ids_any, start, mass, *refs):
    n_src, n_tgt, n_norm = places
    norm_parts, refs = refs[: len(n_norm)], refs[len(n_norm) :]
    src_pieces, refs = refs[: len(n_src)], refs[len(n_src) :]
    tgt_pieces, refs = refs[: len(n_tgt)], refs[len(n_tgt) :]
    out, by_col, src, tgt, norms, ids, spread, peaks, sums, sems = refs
    moves = [pltpu.make_async_copy(ids_any, ids, sems.at[0])]
    position = lax.axis_index("src")
    meta = (position // half, lax.axis_index("tgt"), position % half)
    for pieces, places_of, held in ((src_pieces, n_src, src), (tgt_pieces, n_tgt, tgt)):
        for ref, place in zip(pieces, places_of):
            begin = pl.multiple_of(place(meta), ref.shape[0])
            moves.append(
                pltpu.make_async_copy(ref, held.at[pl.ds(begin, ref.shape[0])], sems.at[len(moves)])
            )
    for move in moves:
        move.start()
    clear(peaks, sums)
    for ref, place in zip(norm_parts, n_norm):
        begin = pl.multiple_of(place(meta), ref.shape[0])
        norms[pl.ds(begin, ref.shape[0])] = ref[...]
    spread_out(start[...] - scale * norms[...], spread)
    for move in moves:
        move.wait()

    def scores_of(slot):
        products = scale * lax.dot_general(
            tgt[ids[slots + slot]],
            src[ids[slot]],
            (((1,), (1,)), ((), ())),
            preferred_element_type=jnp.float32,
        )
        by_col[slot] = products
        return products

    sweep(
        MAKE_UNROLL,
        ids[2 * slots],
        scores_of,
        lambda slot: ids[slots + slot],
        lambda slot: ids[slot],
        spread,
        peaks,
        sums,
    )
    own = mass.shape[0]
    out[0 : 2 * own] = log_sums(peaks, sums)
    out[2 * own :] = jnp.log2(mass[...])


def pass_kernel(scale, half, slots, row_pass, n_parts, makes, has_out, ids_any, *refs):
    parts, refs = refs[:n_parts], refs[n_parts:]
    mass, refs = refs[0], refs[1:]
    if makes:
        src, tgt, out, products, pair, refs = *refs[:5], refs[5:]
    else:
        products, out, refs = *refs[:2], refs[2:]
    if has_out:
        extra, refs = refs[0], refs[1:]
    ids, spread, peaks, sums, sem = refs
    move = pltpu.make_async_copy(ids_any, ids, sem)
    move.start()
    clear(peaks, sums)
    if makes:
        own = mass.shape[0] // 3
        upper = lax.axis_index("src") // half
        pair[pl.ds(pl.multiple_of(upper * own, own), own)] = mass[2 * own :]
        pair[pl.ds(pl.multiple_of((1 - upper) * own, own), own)] = parts[1][2 * own :]
        potential = pair[...] - merge_logs([part[0 : 2 * own] for part in parts])
    else:
        potential = mass[...] - merge_logs([part[...] for part in parts])
    if has_out:
        extra[...] = potential
    spread_out(potential, spread)
    move.wait()
    known, reduced = (slots, 0) if row_pass else (0, slots)

    def scores_of(slot):
        if makes:
            products[slot] = scale * lax.dot_general(
                src[ids[slot]],
                tgt[ids[slots + slot]],
                (((1,), (1,)), ((), ())),
                preferred_element_type=jnp.float32,
            )
        return products[slot]

    sweep(
        MAKE_UNROLL if makes else READ_UNROLL,
        ids[2 * slots],
        scores_of,
        lambda slot: ids[known + slot],
        lambda slot: ids[reduced + slot],
        spread,
        peaks,
        sums,
    )
    out[...] = log_sums(peaks, sums)


def finish_kernel(scale, to_unit, parts_count, *refs):
    parts, (mass, norms, out) = refs[:parts_count], refs[parts_count:]
    potential = mass[...] - merge_logs([part[...] for part in parts])
    out[...] = (potential / scale + norms[...]) / to_unit


def shards(
    source_embed, target_embed, source_mass, target_mass, target_start, tile_list, tile_count
):
    width = source_embed.shape[1]
    shard_count = lax.axis_size("src")
    half = shard_count // 2
    src_index = lax.axis_index("src")
    upper = src_index // half
    scale = 2.0 / (width * EPSILON) * math.log2(math.e)
    to_unit = 0.5 * width

    source_blocks = source_embed.reshape(-1, TILE, width)
    target_blocks = target_embed.reshape(-1, TILE, width)
    src_rows = source_blocks.shape[0]
    own_cols = target_blocks.shape[0]
    col_blocks = own_cols * half
    side = src_rows // lax.axis_size("tgt")
    listed = tile_list.shape[3]
    slots = 2 * listed + PADDING

    smem = pl.BlockSpec(memory_space=pltpu.SMEM)
    vmem = pl.BlockSpec(memory_space=pltpu.VMEM)
    anywhere = pl.BlockSpec(memory_space=pl.ANY)
    params = pltpu.CompilerParams(vmem_limit_bytes=VMEM_LIMIT)

    peer_list = hop(tile_list, half)
    peer_count = hop(tile_count, half)

    def live_list(tiles, count):
        live = lax.broadcasted_iota(jnp.int32, tiles.shape, 3) < count[0, 0]
        return jnp.where(live, tiles, -1)

    share = pl.pallas_call(
        lambda *refs: share_kernel(side, *refs),
        out_shape=jax.ShapeDtypeStruct((side, TILE, width), source_embed.dtype),
        in_specs=[anywhere] * 3,
        out_specs=vmem,
        scratch_shapes=[pltpu.SemaphoreType.DMA((1,))],
        compiler_params=params,
        name="outgoing",
    )(source_blocks, tile_count, tile_count)
    direct = hop(share, half)
    held = {0: target_blocks}
    for slot in range(1, half):
        low = slot & -slot
        held[slot] = hop(held[slot ^ low], low)
    swapped = hop(direct, 0, 1)
    ids_size = -(-(2 * slots + 1) // 1024) * 1024
    ids = pl.pallas_call(
        lambda *refs: list_kernel(half, src_rows, col_blocks, slots, *refs),
        out_shape=jax.ShapeDtypeStruct((ids_size,), jnp.int32),
        in_specs=[smem] * 2,
        out_specs=smem,
        compiler_params=params,
        name="tile_lists",
    )(live_list(tile_list, tile_count), live_list(peer_list, peer_count))
    ids_scratch = pltpu.SMEM((ids_size,), jnp.int32)

    log_half = jnp.log2(
        lax.dynamic_slice_in_dim(target_mass.reshape(-1, TILE), upper * col_blocks, col_blocks)
    )
    start = (scale * to_unit) * lax.dynamic_slice_in_dim(
        target_start.reshape(-1, TILE), upper * col_blocks, col_blocks
    )
    source_norms = half_norms(source_blocks)

    src_pieces = [source_blocks, direct, swapped]
    src_places = [
        lambda meta: meta[0] * src_rows,
        lambda meta: (1 - meta[0]) * src_rows + meta[1] * side,
        lambda meta: (1 - meta[0]) * src_rows + (1 - meta[1]) * side,
    ]
    tgt_pieces, tgt_places, norm_parts = [], [], []
    for slot in range(half):
        tgt_pieces.append(held[slot])
        norm_parts.append(half_norms(held[slot]))
        tgt_places.append(lambda meta, slot=slot: (meta[2] ^ slot) * own_cols)

    def accumulators(known, reduced):
        return [
            ids_scratch,
            pltpu.VMEM((known, TILE, TILE), jnp.float32),
            pltpu.VMEM((reduced + 1, 8, TILE), jnp.float32),
            pltpu.VMEM((reduced + 1, 8, TILE), jnp.float32),
        ]

    moves = 1 + len(src_pieces) + len(tgt_pieces)
    rows, by_col, src, tgt, target_norms = pl.pallas_call(
        lambda *refs: first_kernel(scale, half, slots, (src_places, tgt_places, tgt_places), *refs),
        out_shape=[
            jax.ShapeDtypeStruct((3 * src_rows, TILE), jnp.float32),
            jax.ShapeDtypeStruct((slots, TILE, TILE), jnp.float32),
            jax.ShapeDtypeStruct((2 * src_rows, TILE, width), jnp.bfloat16),
            jax.ShapeDtypeStruct((col_blocks, TILE, width), jnp.bfloat16),
            jax.ShapeDtypeStruct((col_blocks, TILE), jnp.float32),
        ],
        in_specs=[anywhere, vmem, vmem]
        + [vmem] * len(norm_parts)
        + [anywhere] * (len(src_pieces) + len(tgt_pieces)),
        out_specs=[vmem] * 5,
        scratch_shapes=accumulators(col_blocks, 2 * src_rows) + [pltpu.SemaphoreType.DMA((moves,))],
        compiler_params=params,
        name="first_row_pass",
    )(ids, start, source_mass.reshape(src_rows, TILE), *norm_parts, *src_pieces, *tgt_pieces)

    def run(row_pass, parts, mass, given, has_out):
        known, reduced = (col_blocks, 2 * src_rows) if row_pass else (2 * src_rows, col_blocks)
        makes = len(given) == 2
        out_shape = [jax.ShapeDtypeStruct((reduced, TILE), jnp.float32)]
        if makes:
            out_shape.append(jax.ShapeDtypeStruct((slots, TILE, TILE), jnp.float32))
            out_shape.append(jax.ShapeDtypeStruct((known, TILE), jnp.float32))
        if has_out:
            out_shape.append(jax.ShapeDtypeStruct((known, TILE), jnp.float32))
        return pl.pallas_call(
            lambda *refs: pass_kernel(scale, half, slots, row_pass, len(parts), makes, has_out, *refs),
            out_shape=out_shape,
            in_specs=[anywhere] + [vmem] * (len(parts) + 1 + len(given)),
            out_specs=[vmem] * len(out_shape),
            scratch_shapes=accumulators(known, reduced) + [pltpu.SemaphoreType.DMA],
            compiler_params=params,
            name="row_pass" if row_pass else "column_pass",
        )(ids, *parts, mass, *given)

    def share_rows(part):
        return [part, hop(part, half), hop(part, half, 1), hop(part, 0, 1)]

    def share_columns(part):
        return [part] + [hop(part, mask) for mask in range(1, half)]

    columns, by_row, log_pair = run(False, share_rows(rows), rows, [src, tgt], False)
    rows = run(True, share_columns(columns), log_half, [by_col], False)[0]
    columns, source_final = run(False, share_rows(rows), log_pair, [by_row], True)
    gathered = share_columns(columns)
    target_final = pl.pallas_call(
        lambda *refs: finish_kernel(scale, to_unit, len(gathered), *refs),
        out_shape=jax.ShapeDtypeStruct((col_blocks, TILE), jnp.float32),
        in_specs=[vmem] * (len(gathered) + 2),
        out_specs=vmem,
        compiler_params=params,
        name="finish",
    )(*gathered, log_half, target_norms)
    other = hop(target_final, half)
    target_pot = jnp.where(
        upper == 0, jnp.concatenate([target_final, other]), jnp.concatenate([other, target_final])
    )
    own_final = lax.dynamic_slice_in_dim(source_final, upper * src_rows, src_rows)
    source_pot = (own_final / scale + source_norms) / to_unit
    return (source_pot.reshape(-1), target_pot.reshape(-1))


def solution(mesh):
    return jax.shard_map(
        shards,
        mesh=mesh,
        in_specs=(
            P(("groups", "src"), None),
            P(("groups", "tgt", "src"), None),
            P(("groups", "src")),
            P(("groups", "tgt")),
            P(("groups", "tgt")),
            P(("groups", "src"), "tgt", None, None),
            P(("groups", "src"), "tgt"),
        ),
        out_specs=(P(("groups", "src")), P(("groups", "tgt"))),
        check_vma=False,
    )
```

profile of v0, /device:TPU:0, one launch (start us, length us, event | category | flops | bytes accessed | tf_op | source)
XLA Modules:
  0.0 78.2 jit_solution(17412208098714322977)
XLA Ops:
  0.6 0.0 copy-start.7
  0.6 3.1 %collective-permute-start.3 = (bf16[8,128,256]{2,1,0:T(8,128)(2,1)}, bf16[8,128,256]{2,1,0:T(8,128)(2,1)S(1)}, u32[]{:S(2)}, u32[]{:S(2)}) collective-permute-start(bf16[8,128,256]{2,1,0:T(8,128)(2,1)} %bitcast.22), channel_id=1, source_target_pairs={{0,4},{1,5},{2,6},{3,7},{4,0},{5,1},{6,2},{7,3},{8,12},{9,13},{10,... | collective-permute-start | bytes 1572872 | tf_op jit(solution)/shard_map/ppermute | solution.py:23
  3.7 1.5 %collective-permute-start.2 = (bf16[8,128,256]{2,1,0:T(8,128)(2,1)}, bf16[8,128,256]{2,1,0:T(8,128)(2,1)S(1)}, u32[]{:S(2)}, u32[]{:S(2)}) collective-permute-start(bf16[8,128,256]{2,1,0:T(8,128)(2,1)} %bitcast.23), channel_id=1, source_target_pairs={{0,2},{1,3},{2,0},{3,1},{4,6},{5,7},{6,4},{7,5},{8,10},{9,11},{10,... | collective-permute-start | bytes 1572872 | tf_op jit(solution)/shard_map/ppermute | solution.py:23
  5.2 2.6 %collective-permute-start.1 = (s32[1,1,2,128]{3,2,1,0:T(2,128)}, s32[1,1,2,128]{3,2,1,0:T(2,128)S(1)}, u32[]{:S(2)}, u32[]{:S(2)}) collective-permute-start(s32[1,1,2,128]{3,2,1,0:T(2,128)} %param.12), channel_id=1, source_target_pairs={{0,8},{1,9},{2,10},{3,11},{4,12},{5,13},{6,14},{7,15},{8,0},{9,1},... | collective-permute-start | bytes 3080 | tf_op jit(solution)/shard_map/ppermute | solution.py:23
  7.8 0.3 collective-permute-start
  8.9 0.0 copy-start
  8.9 1.2 %copy-done = bf16[2048,256]{1,0:T(8,128)(2,1)S(1)} copy-done((bf16[2048,256]{1,0:T(8,128)(2,1)S(1)}, bf16[2048,256]{1,0:T(8,128)(2,1)}, u32[]{:S(2)}) %copy-start) | copy-done | bytes 1048600
  10.1 0.9 %outgoing.1 = bf16[8,128,256]{2,1,0:T(8,128)(2,1)} custom-call(bf16[16,128,256]{2,1,0:T(8,128)(2,1)S(1)} %bitcast.20, s32[1,1]{1,0:T(1,128)} %copy.9.refs_1_.refs_2_, s32[1,1]{1,0:T(1,128)} %copy.9.refs_1_.refs_2_), custom_call_target="tpu_custom_call" | custom-call | tf_op jit(solution)/shard_map/outgoing/pallas_call | solution.py:252
  11.0 2.7 %collective-permute-start.5 = (bf16[8,128,256]{2,1,0:T(8,128)(2,1)}, bf16[8,128,256]{2,1,0:T(8,128)(2,1)S(1)}, u32[]{:S(2)}, u32[]{:S(2)}) collective-permute-start(bf16[8,128,256]{2,1,0:T(8,128)(2,1)} %outgoing.1), channel_id=1, source_target_pairs={{0,8},{1,9},{2,10},{3,11},{4,12},{5,13},{6,14},{7,15},{8,0},{9,1},... | collective-permute-start | bytes 1572872 | tf_op jit(solution)/shard_map/ppermute | solution.py:23
  13.6 1.3 %multiply_reduce_fusion.4 = f32[1024]{0:T(1024)S(1)} fusion(bf16[1024,256]{1,0:T(8,128)(2,1)} %param.8), kind=kLoop, calls=%fused_computation.4 | loop fusion | flops 785408 | bytes 528384 | tf_op jit(solution)/shard_map/reduce_sum | solution.py:28
  14.9 0.0 copy-done.7
  14.9 0.0 copy-done.5
  15.0 1.4 %collective-permute-done = s32[1,1]{1,0:T(1,128)} collective-permute-done((s32[1,1]{1,0:T(1,128)}, s32[1,1]{1,0:T(1,128)}, u32[]{:S(2)}, u32[]{:S(2)}) %collective-permute-start) | collective-permute-done | bytes 36 | tf_op jit(solution)/shard_map/ppermute | solution.py:23
  16.4 0.6 iota_compare_fusion
  16.9 0.0 collective-permute-done.1
  17.0 2.7 %tile_lists.1.refs_0_ = s32[1024]{0:T(1024)S(1)} custom-call(s32[1,1,2,128]{3,2,1,0:T(2,128)S(1)} %broadcast_select_fusion.1.refs_0_, s32[1,1,2,128]{3,2,1,0:T(2,128)S(1)} %broadcast_select_fusion.refs_1_), custom_call_target="tpu_custom_call" | custom-call | tf_op jit(solution)/shard_map/tile_lists/pallas_call | solution.py:268
  19.7 0.9 %collective-permute-done.3.refs_12_ = bf16[8,128,256]{2,1,0:T(8,128)(2,1)S(1)} collective-permute-done((bf16[8,128,256]{2,1,0:T(8,128)(2,1)}, bf16[8,128,256]{2,1,0:T(8,128)(2,1)S(1)}, u32[]{:S(2)}, u32[]{:S(2)}) %collective-permute-start.3) | collective-permute-done | bytes 524320 | tf_op jit(solution)/shard_map/ppermute | solution.py:23
  20.6 2.7 %collective-permute-start.4 = (bf16[8,128,256]{2,1,0:T(8,128)(2,1)S(1)}, bf16[8,128,256]{2,1,0:T(8,128)(2,1)S(1)}, u32[]{:S(2)}, u32[]{:S(2)}) collective-permute-start(bf16[8,128,256]{2,1,0:T(8,128)(2,1)S(1)} %collective-permute-done.3.refs_12_), channel_id=1, source_target_pairs={{0,2},{1,3},{2,0},{3,1},{4,6},{5,7},{6,4},{7,5},{8,10},{9,11},{10,... | collective-permute-start | bytes 1572872 | tf_op jit(solution)/shard_map/ppermute | solution.py:23
  23.3 12.7 %collective-permute-done.5.refs_8_ = bf16[8,128,256]{2,1,0:T(8,128)(2,1)S(1)} collective-permute-done((bf16[8,128,256]{2,1,0:T(8,128)(2,1)}, bf16[8,128,256]{2,1,0:T(8,128)(2,1)S(1)}, u32[]{:S(2)}, u32[]{:S(2)}) %collective-permute-start.5) | collective-permute-done | bytes 524320 | tf_op jit(solution)/shard_map/ppermute | solution.py:23
  36.0 0.0 collective-permute-start.6
  36.0 0.2 multiply_reduce_fusion.2
  36.2 0.0 collective-permute-done.2.refs_11_
  36.2 0.2 multiply_reduce_fusion.3
  36.5 0.0 collective-permute-done.4.refs_13_
  36.5 0.2 multiply_reduce_fusion.1
  36.7 1.2 %collective-permute-done.6.refs_9_ = bf16[8,128,256]{2,1,0:T(8,128)(2,1)S(1)} collective-permute-done((bf16[8,128,256]{2,1,0:T(8,128)(2,1)S(1)}, bf16[8,128,256]{2,1,0:T(8,128)(2,1)S(1)}, u32[]{:S(2)}, u32[]{:S(2)}) %collective-permute-start.6) | collective-permute-done | bytes 524320 | tf_op jit(solution)/shard_map/ppermute | solution.py:23
  37.9 0.0 copy-done.1
  37.9 0.0 copy-done.3
  37.9 0.0 copy-done.4
  37.9 3.9 %first_row_pass.1 = (f32[48,128]{1,0:T(8,128)S(1)}, f32[272,128,128]{2,1,0:T(8,128)S(1)}, bf16[32,128,256]{2,1,0:T(8,128)(2,1)S(1)}, bf16[32,128,256]{2,1,0:T(8,128)(2,1)S(1)}, f32[32,128]{1,0:T(8,128)S(1)}) custom-call(s32[1024]{0:T(1024)S(1)} %tile_lists.1.refs_0_, f32[32,128]{1,0:T(8,128)S(1)} %dynamic-slice_multiply_fusion.refs_1_, ...), custom_call_target="tpu_custom_call" | custom-call | tf_op jit(solution)/shard_map/first_row_pass/pallas_call | solution.py:307
  41.8 0.1 collective-permute-start.7
  41.9 2.9 %collective-permute-start.8 = (f32[48,128]{1,0:T(8,128)S(1)}, f32[48,128]{1,0:T(8,128)S(1)}, u32[]{:S(2)}, u32[]{:S(2)}) collective-permute-start(f32[48,128]{1,0:T(8,128)S(1)} %get-tuple-element.12.refs_1_.refs_5_), channel_id=1, source_target_pairs={{0,9},{1,8},{2,11},{3,10},{4,13},{5,12},{6,15},{7,14},{8,1},{9,0},... | collective-permute-start | bytes 73736 | tf_op jit(solution)/shard_map/ppermute | solution.py:23
  44.8 0.2 collective-permute-start.9
  45.0 1.9 %collective-permute-done.7.refs_2_ = f32[48,128]{1,0:T(8,128)S(1)} collective-permute-done((f32[48,128]{1,0:T(8,128)S(1)}, f32[48,128]{1,0:T(8,128)S(1)}, u32[]{:S(2)}, u32[]{:S(2)}) %collective-permute-start.7) | collective-permute-done | bytes 24608 | tf_op jit(solution)/shard_map/ppermute | solution.py:23
  46.8 0.0 collective-permute-done.8.refs_3_
  46.8 0.0 collective-permute-done.9.refs_4_
  46.8 3.6 %column_pass.2 = (f32[32,128]{1,0:T(8,128)S(1)}, f32[272,128,128]{2,1,0:T(8,128)S(1)}, f32[32,128]{1,0:T(8,128)S(1)}) custom-call(s32[1024]{0:T(1024)S(1)} %tile_lists.1.refs_0_, f32[48,128]{1,0:T(8,128)S(1)} %get-tuple-element.12.refs_1_.refs_5_, f32[48,128]{1,0:T(8,128)S(1)} %collective-permute-done.7.refs_2_, ...), custom_call_target="tpu_custom_call" | custom-call | tf_op jit(solution)/shard_map/column_pass/pallas_call | solution.py:334
  50.4 0.4 collective-permute-start.10
  50.8 1.1 %collective-permute-start.11 = (f32[32,128]{1,0:T(8,128)S(1)}, f32[32,128]{1,0:T(8,128)S(1)}, u32[]{:S(2)}, u32[]{:S(2)}) collective-permute-start(f32[32,128]{1,0:T(8,128)S(1)} %get-tuple-element.15.refs_1_), channel_id=1, source_target_pairs={{0,4},{1,5},{2,6},{3,7},{4,0},{5,1},{6,2},{7,3},{8,12},{9,13},{10,... | collective-permute-start | bytes 49160 | tf_op jit(solution)/shard_map/ppermute | solution.py:23
  52.0 2.0 %collective-permute-start.12 = (f32[32,128]{1,0:T(8,128)S(1)}, f32[32,128]{1,0:T(8,128)S(1)}, u32[]{:S(2)}, u32[]{:S(2)}) collective-permute-start(f32[32,128]{1,0:T(8,128)S(1)} %get-tuple-element.15.refs_1_), channel_id=1, source_target_pairs={{0,6},{1,7},{2,4},{3,5},{4,2},{5,3},{6,0},{7,1},{8,14},{9,15},{10,... | collective-permute-start | bytes 49160 | tf_op jit(solution)/shard_map/ppermute | solution.py:23
  54.0 0.0 copy-done.6
  54.0 0.2 collective-permute-done.10.refs_2_
  54.2 0.3 collective-permute-done.11.refs_3_
  54.6 2.0 %collective-permute-done.12.refs_4_ = f32[32,128]{1,0:T(8,128)S(1)} collective-permute-done((f32[32,128]{1,0:T(8,128)S(1)}, f32[32,128]{1,0:T(8,128)S(1)}, u32[]{:S(2)}, u32[]{:S(2)}) %collective-permute-start.12) | collective-permute-done | bytes 16416 | tf_op jit(solution)/shard_map/ppermute | solution.py:23
  56.6 2.2 %row_pass.1.refs_1_ = f32[32,128]{1,0:T(8,128)S(1)} custom-call(s32[1024]{0:T(1024)S(1)} %tile_lists.1.refs_0_, f32[32,128]{1,0:T(8,128)S(1)} %get-tuple-element.15.refs_1_, f32[32,128]{1,0:T(8,128)S(1)} %collective-permute-done.10.refs_2_, f32[32,128]{1,0:T(8,128)S(1)} %collective-permute-done.11.refs_3_, f32[32,128]{1,0:T(8,128)S(1)} %collective-permute-done.12.refs_4_, ...), custom_call_target="tpu_custom_call" | custom-call | tf_op jit(solution)/shard_map/row_pass/pallas_call | solution.py:334
  58.8 0.5 collective-permute-start.13
  59.3 0.6 collective-permute-start.14
  59.9 2.0 %collective-permute-start.15 = (f32[32,128]{1,0:T(8,128)S(1)}, f32[32,128]{1,0:T(8,128)S(1)}, u32[]{:S(2)}, u32[]{:S(2)}) collective-permute-start(f32[32,128]{1,0:T(8,128)S(1)} %row_pass.1.refs_1_), channel_id=1, source_target_pairs={{0,1},{1,0},{2,3},{3,2},{4,5},{5,4},{6,7},{7,6},{8,9},{9,8},{10,11... | collective-permute-start | bytes 49160 | tf_op jit(solution)/shard_map/ppermute | solution.py:23
  61.9 1.8 %collective-permute-done.13.refs_2_ = f32[32,128]{1,0:T(8,128)S(1)} collective-permute-done((f32[32,128]{1,0:T(8,128)S(1)}, f32[32,128]{1,0:T(8,128)S(1)}, u32[]{:S(2)}, u32[]{:S(2)}) %collective-permute-start.13) | collective-permute-done | bytes 16416 | tf_op jit(solution)/shard_map/ppermute | solution.py:23
  63.7 0.0 collective-permute-done.14.refs_3_
  63.7 0.0 collective-permute-done.15.refs_4_
  63.7 2.2 %column_pass.3 = (f32[32,128]{1,0:T(8,128)S(1)}, f32[32,128]{1,0:T(8,128)S(1)}) custom-call(s32[1024]{0:T(1024)S(1)} %tile_lists.1.refs_0_, f32[32,128]{1,0:T(8,128)S(1)} %row_pass.1.refs_1_, f32[32,128]{1,0:T(8,128)S(1)} %collective-permute-done.13.refs_2_, f32[32,128]{1,0:T(8,128)S(1)} %collective-permute-done.14.refs_3_, ...), custom_call_target="tpu_custom_call" | custom-call | tf_op jit(solution)/shard_map/column_pass/pallas_call | solution.py:334
  65.8 1.6 %collective-permute-start.16 = (f32[32,128]{1,0:T(8,128)S(1)}, f32[32,128]{1,0:T(8,128)S(1)}, u32[]{:S(2)}, u32[]{:S(2)}) collective-permute-start(f32[32,128]{1,0:T(8,128)S(1)} %get-tuple-element.20.refs_0_), channel_id=1, source_target_pairs={{0,2},{1,3},{2,0},{3,1},{4,6},{5,7},{6,4},{7,5},{8,10},{9,11},{10,... | collective-permute-start | bytes 49160 | tf_op jit(solution)/shard_map/ppermute | solution.py:23
  67.4 0.8 %collective-permute-start.17 = (f32[32,128]{1,0:T(8,128)S(1)}, f32[32,128]{1,0:T(8,128)S(1)}, u32[]{:S(2)}, u32[]{:S(2)}) collective-permute-start(f32[32,128]{1,0:T(8,128)S(1)} %get-tuple-element.20.refs_0_), channel_id=1, source_target_pairs={{0,4},{1,5},{2,6},{3,7},{4,0},{5,1},{6,2},{7,3},{8,12},{9,13},{10,... | collective-permute-start | bytes 49160 | tf_op jit(solution)/shard_map/ppermute | solution.py:23
  68.2 1.2 %collective-permute-start.18 = (f32[32,128]{1,0:T(8,128)S(1)}, f32[32,128]{1,0:T(8,128)S(1)}, u32[]{:S(2)}, u32[]{:S(2)}) collective-permute-start(f32[32,128]{1,0:T(8,128)S(1)} %get-tuple-element.20.refs_0_), channel_id=1, source_target_pairs={{0,6},{1,7},{2,4},{3,5},{4,2},{5,3},{6,0},{7,1},{8,14},{9,15},{10,... | collective-permute-start | bytes 49160 | tf_op jit(solution)/shard_map/ppermute | solution.py:23
  69.4 0.0 copy-done.2
  69.4 0.3 multiply_reduce_fusion
  69.8 0.0 collective-permute-done.16.refs_1_
  69.8 1.4 %collective-permute-done.17.refs_2_ = f32[32,128]{1,0:T(8,128)S(1)} collective-permute-done((f32[32,128]{1,0:T(8,128)S(1)}, f32[32,128]{1,0:T(8,128)S(1)}, u32[]{:S(2)}, u32[]{:S(2)}) %collective-permute-start.17) | collective-permute-done | bytes 16416 | tf_op jit(solution)/shard_map/ppermute | solution.py:23
  71.2 1.7 %collective-permute-done.18.refs_3_ = f32[32,128]{1,0:T(8,128)S(1)} collective-permute-done((f32[32,128]{1,0:T(8,128)S(1)}, f32[32,128]{1,0:T(8,128)S(1)}, u32[]{:S(2)}, u32[]{:S(2)}) %collective-permute-start.18) | collective-permute-done | bytes 16416 | tf_op jit(solution)/shard_map/ppermute | solution.py:23
  72.9 1.8 %collective-permute-start.19 = (f32[32,128]{1,0:T(8,128)S(1)}, f32[32,128]{1,0:T(8,128)S(1)}, u32[]{:S(2)}, u32[]{:S(2)}) collective-permute-start(f32[32,128]{1,0:T(8,128)S(1)} %finish.1), channel_id=1, source_target_pairs={{0,8},{1,9},{2,10},{3,11},{4,12},{5,13},{6,14},{7,15},{8,0},{9,1},... | collective-permute-start | bytes 49160 | tf_op jit(solution)/shard_map/ppermute | solution.py:23
  74.7 0.6 fusion.2
  75.3 2.3 %collective-permute-done.19 = f32[32,128]{1,0:T(8,128)S(1)} collective-permute-done((f32[32,128]{1,0:T(8,128)S(1)}, f32[32,128]{1,0:T(8,128)S(1)}, u32[]{:S(2)}, u32[]{:S(2)}) %collective-permute-start.19) | collective-permute-done | bytes 16416 | tf_op jit(solution)/shard_map/ppermute | solution.py:23
  77.6 0.6 fusion
  (16 shorter events, 0.1 us)
Async XLA Ops:
  0.6 14.3 %copy-start.7 = (s32[1,1,2,128]{3,2,1,0:T(2,128)S(1)}, s32[1,1,2,128]{3,2,1,0:T(2,128)}, u32[]{:S(2)}) copy-start(s32[1,1,2,128]{3,2,1,0:T(2,128)} %param.12) | copy-start | bytes 3076
  0.6 19.9 %collective-permute-start.3 = (bf16[8,128,256]{2,1,0:T(8,128)(2,1)}, bf16[8,128,256]{2,1,0:T(8,128)(2,1)S(1)}, u32[]{:S(2)}, u32[]{:S(2)}) collective-permute-start(bf16[8,128,256]{2,1,0:T(8,128)(2,1)} %bitcast.22), channel_id=1, source_target_pairs={{0,4},{1,5},{2,6},{3,7},{4,0},{5,1},{6,2},{7,3},{8,12},{9,13},{10,... | collective-permute-start | bytes 1572872 | tf_op jit(solution)/shard_map/ppermute | solution.py:23
  3.7 32.5 %collective-permute-start.2 = (bf16[8,128,256]{2,1,0:T(8,128)(2,1)}, bf16[8,128,256]{2,1,0:T(8,128)(2,1)S(1)}, u32[]{:S(2)}, u32[]{:S(2)}) collective-permute-start(bf16[8,128,256]{2,1,0:T(8,128)(2,1)} %bitcast.23), channel_id=1, source_target_pairs={{0,2},{1,3},{2,0},{3,1},{4,6},{5,7},{6,4},{7,5},{8,10},{9,11},{10,... | collective-permute-start | bytes 1572872 | tf_op jit(solution)/shard_map/ppermute | solution.py:23
  5.2 11.7 %collective-permute-start.1 = (s32[1,1,2,128]{3,2,1,0:T(2,128)}, s32[1,1,2,128]{3,2,1,0:T(2,128)S(1)}, u32[]{:S(2)}, u32[]{:S(2)}) collective-permute-start(s32[1,1,2,128]{3,2,1,0:T(2,128)} %param.12), channel_id=1, source_target_pairs={{0,8},{1,9},{2,10},{3,11},{4,12},{5,13},{6,14},{7,15},{8,0},{9,1},... | collective-permute-start | bytes 3080 | tf_op jit(solution)/shard_map/ppermute | solution.py:23
  7.8 8.5 %collective-permute-start = (s32[1,1]{1,0:T(1,128)}, s32[1,1]{1,0:T(1,128)}, u32[]{:S(2)}, u32[]{:S(2)}) collective-permute-start(s32[1,1]{1,0:T(1,128)} %param.13), channel_id=1, source_target_pairs={{0,8},{1,9},{2,10},{3,11},{4,12},{5,13},{6,14},{7,15},{8,0},{9,1},... | collective-permute-start | bytes 20 | tf_op jit(solution)/shard_map/ppermute | solution.py:23
  8.9 1.2 %copy-start = (bf16[2048,256]{1,0:T(8,128)(2,1)S(1)}, bf16[2048,256]{1,0:T(8,128)(2,1)}, u32[]{:S(2)}) copy-start(bf16[2048,256]{1,0:T(8,128)(2,1)} %param.7) | copy-start | bytes 3145732
  10.1 4.9 %copy-start.5 = (f32[8192]{0:T(1024)S(1)}, f32[8192]{0:T(1024)}, u32[]{:S(2)}) copy-start(f32[8192]{0:T(1024)} %param.11) | copy-start | bytes 98308
  10.1 27.8 %copy-start.1 = (bf16[2048,256]{1,0:T(8,128)(2,1)S(1)}, bf16[2048,256]{1,0:T(8,128)(2,1)}, u32[]{:S(2)}) copy-start(bf16[2048,256]{1,0:T(8,128)(2,1)} %param.7) | copy-start | bytes 3145732
  10.1 27.8 %copy-start.3 = (bf16[1024,256]{1,0:T(8,128)(2,1)S(1)}, bf16[1024,256]{1,0:T(8,128)(2,1)}, u32[]{:S(2)}) copy-start(bf16[1024,256]{1,0:T(8,128)(2,1)} %param.8) | copy-start | bytes 1572868
  10.1 27.8 %copy-start.4 = (f32[2048]{0:T(1024)S(1)}, f32[2048]{0:T(1024)}, u32[]{:S(2)}) copy-start(f32[2048]{0:T(1024)} %param.9) | copy-start | bytes 24580
  11.0 25.0 %collective-permute-start.5 = (bf16[8,128,256]{2,1,0:T(8,128)(2,1)}, bf16[8,128,256]{2,1,0:T(8,128)(2,1)S(1)}, u32[]{:S(2)}, u32[]{:S(2)}) collective-permute-start(bf16[8,128,256]{2,1,0:T(8,128)(2,1)} %outgoing.1), channel_id=1, source_target_pairs={{0,8},{1,9},{2,10},{3,11},{4,12},{5,13},{6,14},{7,15},{8,0},{9,1},... | collective-permute-start | bytes 1572872 | tf_op jit(solution)/shard_map/ppermute | solution.py:23
  20.6 15.9 %collective-permute-start.4 = (bf16[8,128,256]{2,1,0:T(8,128)(2,1)S(1)}, bf16[8,128,256]{2,1,0:T(8,128)(2,1)S(1)}, u32[]{:S(2)}, u32[]{:S(2)}) collective-permute-start(bf16[8,128,256]{2,1,0:T(8,128)(2,1)S(1)} %collective-permute-done.3.refs_12_), channel_id=1, source_target_pairs={{0,2},{1,3},{2,0},{3,1},{4,6},{5,7},{6,4},{7,5},{8,10},{9,11},{10,... | collective-permute-start | bytes 1572872 | tf_op jit(solution)/shard_map/ppermute | solution.py:23
  36.0 1.9 %collective-permute-start.6 = (bf16[8,128,256]{2,1,0:T(8,128)(2,1)S(1)}, bf16[8,128,256]{2,1,0:T(8,128)(2,1)S(1)}, u32[]{:S(2)}, u32[]{:S(2)}) collective-permute-start(bf16[8,128,256]{2,1,0:T(8,128)(2,1)S(1)} %collective-permute-done.5.refs_8_), channel_id=1, source_target_pairs={{0,1},{1,0},{2,3},{3,2},{4,5},{5,4},{6,7},{7,6},{8,9},{9,8},{10,11... | collective-permute-start | bytes 1572872 | tf_op jit(solution)/shard_map/ppermute | solution.py:23
  41.8 5.0 %collective-permute-start.7 = (f32[48,128]{1,0:T(8,128)S(1)}, f32[48,128]{1,0:T(8,128)S(1)}, u32[]{:S(2)}, u32[]{:S(2)}) collective-permute-start(f32[48,128]{1,0:T(8,128)S(1)} %get-tuple-element.12.refs_1_.refs_5_), channel_id=1, source_target_pairs={{0,8},{1,9},{2,10},{3,11},{4,12},{5,13},{6,14},{7,15},{8,0},{9,1},... | collective-permute-start | bytes 73736 | tf_op jit(solution)/shard_map/ppermute | solution.py:23
  41.9 4.9 %collective-permute-start.8 = (f32[48,128]{1,0:T(8,128)S(1)}, f32[48,128]{1,0:T(8,128)S(1)}, u32[]{:S(2)}, u32[]{:S(2)}) collective-permute-start(f32[48,128]{1,0:T(8,128)S(1)} %get-tuple-element.12.refs_1_.refs_5_), channel_id=1, source_target_pairs={{0,9},{1,8},{2,11},{3,10},{4,13},{5,12},{6,15},{7,14},{8,1},{9,0},... | collective-permute-start | bytes 73736 | tf_op jit(solution)/shard_map/ppermute | solution.py:23
  44.8 2.0 %collective-permute-start.9 = (f32[48,128]{1,0:T(8,128)S(1)}, f32[48,128]{1,0:T(8,128)S(1)}, u32[]{:S(2)}, u32[]{:S(2)}) collective-permute-start(f32[48,128]{1,0:T(8,128)S(1)} %get-tuple-element.12.refs_1_.refs_5_), channel_id=1, source_target_pairs={{0,1},{1,0},{2,3},{3,2},{4,5},{5,4},{6,7},{7,6},{8,9},{9,8},{10,11... | collective-permute-start | bytes 73736 | tf_op jit(solution)/shard_map/ppermute | solution.py:23
  46.8 7.2 %copy-start.6 = (f32[8192]{0:T(1024)S(1)}, f32[8192]{0:T(1024)}, u32[]{:S(2)}) copy-start(f32[8192]{0:T(1024)} %param.10) | copy-start | bytes 98308
  50.4 3.8 %collective-permute-start.10 = (f32[32,128]{1,0:T(8,128)S(1)}, f32[32,128]{1,0:T(8,128)S(1)}, u32[]{:S(2)}, u32[]{:S(2)}) collective-permute-start(f32[32,128]{1,0:T(8,128)S(1)} %get-tuple-element.15.refs_1_), channel_id=1, source_target_pairs={{0,2},{1,3},{2,0},{3,1},{4,6},{5,7},{6,4},{7,5},{8,10},{9,11},{10,... | collective-permute-start | bytes 49160 | tf_op jit(solution)/shard_map/ppermute | solution.py:23
  50.8 3.7 %collective-permute-start.11 = (f32[32,128]{1,0:T(8,128)S(1)}, f32[32,128]{1,0:T(8,128)S(1)}, u32[]{:S(2)}, u32[]{:S(2)}) collective-permute-start(f32[32,128]{1,0:T(8,128)S(1)} %get-tuple-element.15.refs_1_), channel_id=1, source_target_pairs={{0,4},{1,5},{2,6},{3,7},{4,0},{5,1},{6,2},{7,3},{8,12},{9,13},{10,... | collective-permute-start | bytes 49160 | tf_op jit(solution)/shard_map/ppermute | solution.py:23
  52.0 4.6 %collective-permute-start.12 = (f32[32,128]{1,0:T(8,128)S(1)}, f32[32,128]{1,0:T(8,128)S(1)}, u32[]{:S(2)}, u32[]{:S(2)}) collective-permute-start(f32[32,128]{1,0:T(8,128)S(1)} %get-tuple-element.15.refs_1_), channel_id=1, source_target_pairs={{0,6},{1,7},{2,4},{3,5},{4,2},{5,3},{6,0},{7,1},{8,14},{9,15},{10,... | collective-permute-start | bytes 49160 | tf_op jit(solution)/shard_map/ppermute | solution.py:23
  58.8 4.9 %collective-permute-start.13 = (f32[32,128]{1,0:T(8,128)S(1)}, f32[32,128]{1,0:T(8,128)S(1)}, u32[]{:S(2)}, u32[]{:S(2)}) collective-permute-start(f32[32,128]{1,0:T(8,128)S(1)} %row_pass.1.refs_1_), channel_id=1, source_target_pairs={{0,8},{1,9},{2,10},{3,11},{4,12},{5,13},{6,14},{7,15},{8,0},{9,1},... | collective-permute-start | bytes 49160 | tf_op jit(solution)/shard_map/ppermute | solution.py:23
  59.3 4.3 %collective-permute-start.14 = (f32[32,128]{1,0:T(8,128)S(1)}, f32[32,128]{1,0:T(8,128)S(1)}, u32[]{:S(2)}, u32[]{:S(2)}) collective-permute-start(f32[32,128]{1,0:T(8,128)S(1)} %row_pass.1.refs_1_), channel_id=1, source_target_pairs={{0,9},{1,8},{2,11},{3,10},{4,13},{5,12},{6,15},{7,14},{8,1},{9,0},... | collective-permute-start | bytes 49160 | tf_op jit(solution)/shard_map/ppermute | solution.py:23
  59.9 3.7 %collective-permute-start.15 = (f32[32,128]{1,0:T(8,128)S(1)}, f32[32,128]{1,0:T(8,128)S(1)}, u32[]{:S(2)}, u32[]{:S(2)}) collective-permute-start(f32[32,128]{1,0:T(8,128)S(1)} %row_pass.1.refs_1_), channel_id=1, source_target_pairs={{0,1},{1,0},{2,3},{3,2},{4,5},{5,4},{6,7},{7,6},{8,9},{9,8},{10,11... | collective-permute-start | bytes 49160 | tf_op jit(solution)/shard_map/ppermute | solution.py:23
  63.7 5.7 %copy-start.2 = (bf16[2048,256]{1,0:T(8,128)(2,1)S(1)}, bf16[2048,256]{1,0:T(8,128)(2,1)}, u32[]{:S(2)}) copy-start(bf16[2048,256]{1,0:T(8,128)(2,1)} %param.7) | copy-start | bytes 3145732
  65.8 3.9 %collective-permute-start.16 = (f32[32,128]{1,0:T(8,128)S(1)}, f32[32,128]{1,0:T(8,128)S(1)}, u32[]{:S(2)}, u32[]{:S(2)}) collective-permute-start(f32[32,128]{1,0:T(8,128)S(1)} %get-tuple-element.20.refs_0_), channel_id=1, source_target_pairs={{0,2},{1,3},{2,0},{3,1},{4,6},{5,7},{6,4},{7,5},{8,10},{9,11},{10,... | collective-permute-start | bytes 49160 | tf_op jit(solution)/shard_map/ppermute | solution.py:23
  67.4 3.7 %collective-permute-start.17 = (f32[32,128]{1,0:T(8,128)S(1)}, f32[32,128]{1,0:T(8,128)S(1)}, u32[]{:S(2)}, u32[]{:S(2)}) collective-permute-start(f32[32,128]{1,0:T(8,128)S(1)} %get-tuple-element.20.refs_0_), channel_id=1, source_target_pairs={{0,4},{1,5},{2,6},{3,7},{4,0},{5,1},{6,2},{7,3},{8,12},{9,13},{10,... | collective-permute-start | bytes 49160 | tf_op jit(solution)/shard_map/ppermute | solution.py:23
  68.2 4.6 %collective-permute-start.18 = (f32[32,128]{1,0:T(8,128)S(1)}, f32[32,128]{1,0:T(8,128)S(1)}, u32[]{:S(2)}, u32[]{:S(2)}) collective-permute-start(f32[32,128]{1,0:T(8,128)S(1)} %get-tuple-element.20.refs_0_), channel_id=1, source_target_pairs={{0,6},{1,7},{2,4},{3,5},{4,2},{5,3},{6,0},{7,1},{8,14},{9,15},{10,... | collective-permute-start | bytes 49160 | tf_op jit(solution)/shard_map/ppermute | solution.py:23
  72.9 4.7 %collective-permute-start.19 = (f32[32,128]{1,0:T(8,128)S(1)}, f32[32,128]{1,0:T(8,128)S(1)}, u32[]{:S(2)}, u32[]{:S(2)}) collective-permute-start(f32[32,128]{1,0:T(8,128)S(1)} %finish.1), channel_id=1, source_target_pairs={{0,8},{1,9},{2,10},{3,11},{4,12},{5,13},{6,14},{7,15},{8,0},{9,1},... | collective-permute-start | bytes 49160 | tf_op jit(solution)/shard_map/ppermute | solution.py:23
where the time goes:
time: 78.7 us; the launch traced here: 78.2 us
  starting transfers between devices  28 us (36%)
  waiting for transfers between devices  27.8 us (35%)
  Pallas kernels  15.5 us (20%)
  other arithmetic  4.05 us (5%)
  between operations  1.6 us (2%)
  local copies, waits for them, and re-layouts  1.25 us (2%)
    ppermute x20, starting transfers between devices, hop(): lax.ppermute(value, ('src', 'tgt'), [(i, i ^ flip) for i in range(total)])  28 us
    ppermute x20, waiting for transfers between devices, hop(): lax.ppermute(value, ('src', 'tgt'), [(i, i ^ flip) for i in range(total)])  27.8 us
    pallas_call x3, Pallas kernels, run(): pl.pallas_call(lambda *refs: pass_kernel(scale, half, slots, row_pass, le...  7.92 us
    pallas_call x1, Pallas kernels, shards(): pl.pallas_call(lambda *refs: first_kernel(scale, half, slots, (src_places...  3.92 us
    pallas_call x1, Pallas kernels, shards(): pl.pallas_call(lambda *refs: list_kernel(half, src_rows, col_blocks, slot...  2.73 us
    reduce_sum x5, other arithmetic, half_norms(): return 0.5 * jnp.sum(wide * wide, axis=-1).reshape(-1, TILE)  2.23 us
  transfers between devices with their start and end apart: 20, of which 12 were waited for; matrix products, arithmetic and copies ran while one was open for 4% of the time, Pallas kernels for 5%

commit v1 on v0

--- a/solution.py
+++ b/solution.py
@@ -10,10 +10,10 @@
 TILE = 128
 EPSILON = 0.05
 FLOOR = -1e30
-MAKE_UNROLL = 16
+MAKE_UNROLL = 20
 READ_UNROLL = 8
 PADDING = max(MAKE_UNROLL, READ_UNROLL)
-VMEM_LIMIT = 4 * 1024 * 1024
+VMEM_LIMIT = 3 * 1024 * 1024
 
 
 def hop(value, src_mask, tgt_mask=0):
@@ -28,28 +28,40 @@
     return 0.5 * jnp.sum(wide * wide, axis=-1).reshape(-1, TILE)
 
 
-def share_kernel(side, source, first, second, share, sems):
+def share_kernel(side, source, share, sems):
     begin = lax.axis_index("tgt") * side
     move = pltpu.make_async_copy(source.at[pl.ds(begin, side)], share, sems.at[0])
     move.start()
     move.wait()
 
 
-def list_kernel(half, src_rows, col_blocks, slots, own, peer, ids):
-    upper = lax.axis_index("src") // half
+def list_kernel(half, src_rows, own_cols, slots, own, peer, ids):
+    position = lax.axis_index("src")
+    upper = position // half
+    col_blocks = half * own_cols
+    late = ((position % half) ^ (half - 1)) * own_cols
     listed = own.shape[3]
 
-    def scan(refs, shift):
+    def scan(refs, shift, wanted):
         def step(k, found):
             col = refs[0, 0, 1, k] - upper * col_blocks
             ids[found] = refs[0, 0, 0, k] + shift * src_rows
             ids[slots + found] = col
-            return found + ((col >= 0) & (col < col_blocks)).astype(jnp.int32)
+            return found + wanted(col).astype(jnp.int32)
 
         return step
 
-    found = lax.fori_loop(0, listed, scan(own, upper), 0, unroll=8)
-    found = lax.fori_loop(0, listed, scan(peer, 1 - upper), found, unroll=8)
+    def is_late(col):
+        return (col >= late) & (col < late + own_cols)
+
+    def is_here(col):
+        return (col >= 0) & (col < col_blocks)
+
+    early = scan(own, upper, lambda col: is_here(col) & jnp.logical_not(is_late(col)))
+    found = lax.fori_loop(0, listed, early, 0, unroll=8)
+    ids[2 * slots + 1] = found
+    found = lax.fori_loop(0, listed, scan(own, upper, is_late), found, unroll=8)
+    found = lax.fori_loop(0, listed, scan(peer, 1 - upper, is_here), found, unroll=8)
     for extra in range(PADDING):
         ids[found + extra] = 0
         ids[slots + found + extra] = 0
@@ -63,10 +75,10 @@
     return peak + jnp.log2(sum(jnp.exp2(part - peak) for part in parts))
 
 
-def spread_out(potential, spread):
+def spread_out(potential, spread, begin=0):
     turned = jnp.transpose(potential)
     for block in range(potential.shape[0]):
-        spread[block] = jnp.broadcast_to(turned[:, block : block + 1], (TILE, TILE))
+        spread[begin + block] = jnp.broadcast_to(turned[:, block : block + 1], (TILE, TILE))
 
 
 def clear(peaks, sums):
@@ -74,7 +86,7 @@
     sums[...] = jnp.zeros(sums.shape, jnp.float32)
 
 
-def sweep(unroll, count, scores_of, known_of, reduced_of, spread, peaks, sums):
+def sweep(unroll, begin, count, scores_of, known_of, reduced_of, spread, peaks, sums):
     dummy = peaks.shape[0] - 1
 
     def merge(carry):
@@ -89,7 +101,7 @@
         merge(carry)
         fresh = []
         for lane in range(unroll):
-            slot = index * unroll + lane
+            slot = begin + index * unroll + lane
             scores = (scores_of(slot) + spread[known_of(slot)]).reshape(TILE // 8, 8, TILE)
             peak = jnp.max(scores, axis=0)
             summed = jnp.sum(jnp.exp2(scores - peak[None]), axis=0)
@@ -100,7 +112,7 @@
         (jnp.int32(dummy), jnp.full((8, TILE), FLOOR, jnp.float32), jnp.zeros((8, TILE), jnp.float32))
         for lane in range(unroll)
     )
-    merge(lax.fori_loop(0, (count + unroll - 1) // unroll, turn, nothing))
+    merge(lax.fori_loop(0, (count - begin + unroll - 1) // unroll, turn, nothing))
 
 
 def log_sums(peaks, sums):
@@ -111,28 +123,39 @@
     return jnp.where(live, peak + jnp.log2(jnp.where(live, summed, 1.0)), FLOOR)
 
 
-def first_kernel(scale, half, slots, places, ids_any, start, mass, *refs):
-    n_src, n_tgt, n_norm = places
-    norm_parts, refs = refs[: len(n_norm)], refs[len(n_norm) :]
-    src_pieces, refs = refs[: len(n_src)], refs[len(n_src) :]
-    tgt_pieces, refs = refs[: len(n_tgt)], refs[len(n_tgt) :]
-    out, by_col, src, tgt, norms, ids, spread, peaks, sums, sems = refs
-    moves = [pltpu.make_async_copy(ids_any, ids, sems.at[0])]
-    position = lax.axis_index("src")
-    meta = (position // half, lax.axis_index("tgt"), position % half)
-    for pieces, places_of, held in ((src_pieces, n_src, src), (tgt_pieces, n_tgt, tgt)):
+def gather_parts(meta, groups, sems, first_sem):
+    moves = []
+    for pieces, places_of, whole in groups:
         for ref, place in zip(pieces, places_of):
             begin = pl.multiple_of(place(meta), ref.shape[0])
             moves.append(
-                pltpu.make_async_copy(ref, held.at[pl.ds(begin, ref.shape[0])], sems.at[len(moves)])
+                pltpu.make_async_copy(
+                    ref, whole.at[pl.ds(begin, ref.shape[0])], sems.at[first_sem + len(moves)]
+                )
             )
+    return moves
+
+
+def first_kernel(scale, half, slots, late, places, ids_any, start, *refs):
+    n_src, n_tgt = places
+    norm_parts, refs = refs[: len(n_tgt)], refs[len(n_tgt) :]
+    src_pieces, refs = refs[: len(n_src)], refs[len(n_src) :]
+    tgt_pieces, refs = refs[: len(n_tgt)], refs[len(n_tgt) :]
+    if late:
+        mass, out, refs = refs[0], refs[8], refs[9:]
+    by_col, src, tgt, norms, spread, peaks, sums, ids, sems = refs
+    position = lax.axis_index("src")
+    meta = (position // half, lax.axis_index("tgt"), position % half)
+    moves = [pltpu.make_async_copy(ids_any, ids, sems.at[0])]
+    moves += gather_parts(meta, ((src_pieces, n_src, src), (tgt_pieces, n_tgt, tgt)), sems, 1)
     for move in moves:
         move.start()
-    clear(peaks, sums)
-    for ref, place in zip(norm_parts, n_norm):
+    if not late:
+        clear(peaks, sums)
+    for ref, place in zip(norm_parts, n_tgt):
         begin = pl.multiple_of(place(meta), ref.shape[0])
         norms[pl.ds(begin, ref.shape[0])] = ref[...]
-    spread_out(start[...] - scale * norms[...], spread)
+        spread_out(start[pl.ds(begin, ref.shape[0])] - scale * ref[...], spread, begin)
     for move in moves:
         move.wait()
 
@@ -143,12 +166,13 @@
             (((1,), (1,)), ((), ())),
             preferred_element_type=jnp.float32,
         )
-        by_col[slot] = products
+        by_col[jnp.minimum(slot, by_col.shape[0] - 1)] = products
         return products
 
     sweep(
         MAKE_UNROLL,
-        ids[2 * slots],
+        ids[2 * slots + 1] if late else 0,
+        ids[2 * slots] if late else ids[2 * slots + 1],
         scores_of,
         lambda slot: ids[slots + slot],
         lambda slot: ids[slot],
@@ -156,9 +180,10 @@
         peaks,
         sums,
     )
-    own = mass.shape[0]
-    out[0 : 2 * own] = log_sums(peaks, sums)
-    out[2 * own :] = jnp.log2(mass[...])
+    if late:
+        own = mass.shape[0]
+        out[0 : 2 * own] = log_sums(peaks, sums)
+        out[2 * own :] = jnp.log2(mass[...])
 
 
 def pass_kernel(scale, half, slots, row_pass, n_parts, makes, has_out, ids_any, *refs):
@@ -189,17 +214,20 @@
     known, reduced = (slots, 0) if row_pass else (0, slots)
 
     def scores_of(slot):
-        if makes:
-            products[slot] = scale * lax.dot_general(
-                src[ids[slot]],
-                tgt[ids[slots + slot]],
-                (((1,), (1,)), ((), ())),
-                preferred_element_type=jnp.float32,
-            )
-        return products[slot]
+        if not makes:
+            return products[jnp.minimum(slot, products.shape[0] - 1)]
+        made = scale * lax.dot_general(
+            src[ids[slot]],
+            tgt[ids[slots + slot]],
+            (((1,), (1,)), ((), ())),
+            preferred_element_type=jnp.float32,
+        )
+        products[jnp.minimum(slot, products.shape[0] - 1)] = made
+        return made
 
     sweep(
         MAKE_UNROLL if makes else READ_UNROLL,
+        0,
         ids[2 * slots],
         scores_of,
         lambda slot: ids[known + slot],
@@ -252,21 +280,20 @@
     share = pl.pallas_call(
         lambda *refs: share_kernel(side, *refs),
         out_shape=jax.ShapeDtypeStruct((side, TILE, width), source_embed.dtype),
-        in_specs=[anywhere] * 3,
+        in_specs=[anywhere],
         out_specs=vmem,
         scratch_shapes=[pltpu.SemaphoreType.DMA((1,))],
         compiler_params=params,
         name="outgoing",
-    )(source_blocks, tile_count, tile_count)
+    )(source_blocks)
     direct = hop(share, half)
     held = {0: target_blocks}
     for slot in range(1, half):
         low = slot & -slot
         held[slot] = hop(held[slot ^ low], low)
-    swapped = hop(direct, 0, 1)
-    ids_size = -(-(2 * slots + 1) // 1024) * 1024
+    ids_size = -(-(2 * slots + 2) // 1024) * 1024
     ids = pl.pallas_call(
-        lambda *refs: list_kernel(half, src_rows, col_blocks, slots, *refs),
+        lambda *refs: list_kernel(half, src_rows, own_cols, slots, *refs),
         out_shape=jax.ShapeDtypeStruct((ids_size,), jnp.int32),
         in_specs=[smem] * 2,
         out_specs=smem,
@@ -283,7 +310,7 @@
     )
     source_norms = half_norms(source_blocks)
 
-    src_pieces = [source_blocks, direct, swapped]
+    src_pieces = [source_blocks]
     src_places = [
         lambda meta: meta[0] * src_rows,
         lambda meta: (1 - meta[0]) * src_rows + meta[1] * side,
@@ -303,31 +330,53 @@
             pltpu.VMEM((reduced + 1, 8, TILE), jnp.float32),
         ]
 
-    moves = 1 + len(src_pieces) + len(tgt_pieces)
-    rows, by_col, src, tgt, target_norms = pl.pallas_call(
-        lambda *refs: first_kernel(scale, half, slots, (src_places, tgt_places, tgt_places), *refs),
-        out_shape=[
-            jax.ShapeDtypeStruct((3 * src_rows, TILE), jnp.float32),
-            jax.ShapeDtypeStruct((slots, TILE, TILE), jnp.float32),
-            jax.ShapeDtypeStruct((2 * src_rows, TILE, width), jnp.bfloat16),
-            jax.ShapeDtypeStruct((col_blocks, TILE, width), jnp.bfloat16),
-            jax.ShapeDtypeStruct((col_blocks, TILE), jnp.float32),
-        ],
-        in_specs=[anywhere, vmem, vmem]
-        + [vmem] * len(norm_parts)
-        + [anywhere] * (len(src_pieces) + len(tgt_pieces)),
-        out_specs=[vmem] * 5,
-        scratch_shapes=accumulators(col_blocks, 2 * src_rows) + [pltpu.SemaphoreType.DMA((moves,))],
-        compiler_params=params,
-        name="first_row_pass",
-    )(ids, start, source_mass.reshape(src_rows, TILE), *norm_parts, *src_pieces, *tgt_pieces)
+    shared = [
+        jax.ShapeDtypeStruct((2 * listed + 1, TILE, TILE), jnp.float32),
+        jax.ShapeDtypeStruct((2 * src_rows, TILE, width), jnp.bfloat16),
+        jax.ShapeDtypeStruct((col_blocks, TILE, width), jnp.bfloat16),
+        jax.ShapeDtypeStruct((col_blocks, TILE), jnp.float32),
+        jax.ShapeDtypeStruct((col_blocks, TILE, TILE), jnp.float32),
+        jax.ShapeDtypeStruct((2 * src_rows + 1, 8, TILE), jnp.float32),
+        jax.ShapeDtypeStruct((2 * src_rows + 1, 8, TILE), jnp.float32),
+    ]
+
+    def first(late, given):
+        srcs = slice(1, None) if late else slice(0, 1)
+        tgts = slice(half - 1, None) if late else slice(0, half - 1)
+        pieces = src_pieces[srcs] + tgt_pieces[tgts]
+        norms = norm_parts[tgts]
+        inputs = [ids, start, *norms, *pieces, *given]
+        out_shape = shared
+        if late:
+            out_shape = [jax.ShapeDtypeStruct((3 * src_rows, TILE), jnp.float32)] + shared
+        return pl.pallas_call(
+            lambda *refs: first_kernel(
+                scale, half, slots, late, (src_places[srcs], tgt_places[tgts]), *refs
+            ),
+            out_shape=out_shape,
+            in_specs=[anywhere] + [vmem] * (1 + len(norms)) + [anywhere] * len(pieces) + [vmem] * len(given),
+            out_specs=[vmem] * len(out_shape),
+            scratch_shapes=[ids_scratch, pltpu.SemaphoreType.DMA((1 + len(pieces),))],
+            input_output_aliases=(
+                {len(inputs) - len(shared) + i: 1 + i for i in range(len(shared))} if late else {}
+            ),
+            compiler_params=params,
+            name="late_row_pass" if late else "early_row_pass",
+        )(*inputs)
+
+    kept = list(first(False, []))
+    direct, kept[5] = lax.optimization_barrier((direct, kept[5]))
+    src_pieces[1:] = [direct, hop(direct, 0, 1)]
+    rows, by_col, src, tgt, target_norms = first(
+        True, [source_mass.reshape(src_rows, TILE), *kept]
+    )[:5]
 
     def run(row_pass, parts, mass, given, has_out):
         known, reduced = (col_blocks, 2 * src_rows) if row_pass else (2 * src_rows, col_blocks)
         makes = len(given) == 2
         out_shape = [jax.ShapeDtypeStruct((reduced, TILE), jnp.float32)]
         if makes:
-            out_shape.append(jax.ShapeDtypeStruct((slots, TILE, TILE), jnp.float32))
+            out_shape.append(jax.ShapeDtypeStruct((2 * listed + 1, TILE, TILE), jnp.float32))
             out_shape.append(jax.ShapeDtypeStruct((known, TILE), jnp.float32))
         if has_out:
             out_shape.append(jax.ShapeDtypeStruct((known, TILE), jnp.float32))

time: 78.7 us -> 77.7 us (0.987)
  waiting for transfers between devices: 27.8 us -> 24.1 us
  starting transfers between devices: 28 us -> 30.3 us
    ppermute x20, waiting for transfers between devices: 27.8 us -> 24.1 us  [hop(): lax.ppermute(value, ('src', 'tgt'), [(i, i ^ flip) for i in range(total)])]
    ppermute x20, starting transfers between devices: 28 us -> 30.3 us  [hop(): lax.ppermute(value, ('src', 'tgt'), [(i, i ^ flip) for i in range(total)])]
    pallas_call x2 -> x3, Pallas kernels: 6.66 us -> 7.99 us  [the longest x2 4.31 us: first(): pl.pallas_call(lambda *refs: first_kernel(scale, half, slots, late, (src_...]
    pallas_call x3, Pallas kernels: 7.92 us -> 7.02 us  [run(): pl.pallas_call(lambda *refs: pass_kernel(scale, half, slots, row_pass, le...]
  transfers between devices with their start and end apart: 20 -> 20, of which waited for: 12 -> 12; matrix products, arithmetic and copies ran while one was open for 4% -> 4% of each run, Pallas kernels for 5% -> 9%
where the time goes in v1:
time: 77.7 us; the launch traced here: 77.1 us
  starting transfers between devices  30.3 us (39%)
  waiting for transfers between devices  24.1 us (31%)
  Pallas kernels  15.9 us (20%)
  other arithmetic  4.05 us (5%)
  between operations  1.58 us (2%)
  local copies, waits for them, and re-layouts  1.25 us (2%)
    ppermute x20, starting transfers between devices, hop(): lax.ppermute(value, ('src', 'tgt'), [(i, i ^ flip) for i in range(total)])  30.3 us
    ppermute x20, waiting for transfers between devices, hop(): lax.ppermute(value, ('src', 'tgt'), [(i, i ^ flip) for i in range(total)])  24.1 us
    pallas_call x3, Pallas kernels, run(): pl.pallas_call(lambda *refs: pass_kernel(scale, half, slots, row_pass, le...  7.02 us
    pallas_call x2, Pallas kernels, first(): pl.pallas_call(lambda *refs: first_kernel(scale, half, slots, late, (src_...  4.31 us
    pallas_call x1, Pallas kernels, shards(): pl.pallas_call(lambda *refs: list_kernel(half, src_rows, own_cols, slots,...  3.68 us
    reduce_sum x5, other arithmetic, half_norms(): return 0.5 * jnp.sum(wide * wide, axis=-1).reshape(-1, TILE)  2.23 us
  transfers between devices with their start and end apart: 20, of which 12 were waited for; matrix products, arithmetic and copies ran while one was open for 4% of the time, Pallas kernels for 9%

profile of v1, /device:TPU:0, one launch (start us, length us, event | category | flops | bytes accessed | tf_op | source)
XLA Modules:
  0.0 77.1 jit_solution(313601574937398760)
XLA Ops:
  0.6 0.0 copy-start.6
  0.6 3.1 %collective-permute-start.2 = (bf16[8,128,256]{2,1,0:T(8,128)(2,1)}, bf16[8,128,256]{2,1,0:T(8,128)(2,1)S(1)}, u32[]{:S(2)}, u32[]{:S(2)}) collective-permute-start(bf16[8,128,256]{2,1,0:T(8,128)(2,1)} %bitcast.22), channel_id=1, source_target_pairs={{0,4},{1,5},{2,6},{3,7},{4,0},{5,1},{6,2},{7,3},{8,12},{9,13},{10,... | collective-permute-start | bytes 1572872 | tf_op jit(solution)/shard_map/ppermute | solution.py:23
  3.7 1.5 %collective-permute-start.5 = (bf16[8,128,256]{2,1,0:T(8,128)(2,1)}, bf16[8,128,256]{2,1,0:T(8,128)(2,1)S(1)}, u32[]{:S(2)}, u32[]{:S(2)}) collective-permute-start(bf16[8,128,256]{2,1,0:T(8,128)(2,1)} %bitcast.23), channel_id=1, source_target_pairs={{0,2},{1,3},{2,0},{3,1},{4,6},{5,7},{6,4},{7,5},{8,10},{9,11},{10,... | collective-permute-start | bytes 1572872 | tf_op jit(solution)/shard_map/ppermute | solution.py:23
  5.2 2.6 %collective-permute-start.1 = (s32[1,1,2,128]{3,2,1,0:T(2,128)}, s32[1,1,2,128]{3,2,1,0:T(2,128)S(1)}, u32[]{:S(2)}, u32[]{:S(2)}) collective-permute-start(s32[1,1,2,128]{3,2,1,0:T(2,128)} %param.12), channel_id=1, source_target_pairs={{0,8},{1,9},{2,10},{3,11},{4,12},{5,13},{6,14},{7,15},{8,0},{9,1},... | collective-permute-start | bytes 3080 | tf_op jit(solution)/shard_map/ppermute | solution.py:23
  7.8 0.3 collective-permute-start
  8.2 1.2 %copy-done = bf16[2048,256]{1,0:T(8,128)(2,1)S(1)} copy-done((bf16[2048,256]{1,0:T(8,128)(2,1)S(1)}, bf16[2048,256]{1,0:T(8,128)(2,1)}, u32[]{:S(2)}) %copy-start) | copy-done | bytes 1048600
  9.4 0.8 %outgoing.1 = bf16[8,128,256]{2,1,0:T(8,128)(2,1)} custom-call(bf16[16,128,256]{2,1,0:T(8,128)(2,1)S(1)} %bitcast.20), custom_call_target="tpu_custom_call" | custom-call | tf_op jit(solution)/shard_map/outgoing/pallas_call | solution.py:280
  10.3 2.7 %collective-permute-start.4 = (bf16[8,128,256]{2,1,0:T(8,128)(2,1)}, bf16[8,128,256]{2,1,0:T(8,128)(2,1)S(1)}, u32[]{:S(2)}, u32[]{:S(2)}) collective-permute-start(bf16[8,128,256]{2,1,0:T(8,128)(2,1)} %outgoing.1), channel_id=1, source_target_pairs={{0,8},{1,9},{2,10},{3,11},{4,12},{5,13},{6,14},{7,15},{8,0},{9,1},... | collective-permute-start | bytes 1572872 | tf_op jit(solution)/shard_map/ppermute | solution.py:23
  13.6 1.3 %multiply_reduce_fusion.3 = f32[1024]{0:T(1024)S(1)} fusion(bf16[1024,256]{1,0:T(8,128)(2,1)} %param.8), kind=kLoop, calls=%fused_computation.3 | loop fusion | flops 785408 | bytes 528384 | tf_op jit(solution)/shard_map/reduce_sum | solution.py:28
  14.9 0.0 copy-done.4
  14.9 0.0 copy-done.6
  14.9 1.5 %collective-permute-done = s32[1,1]{1,0:T(1,128)} collective-permute-done((s32[1,1]{1,0:T(1,128)}, s32[1,1]{1,0:T(1,128)}, u32[]{:S(2)}, u32[]{:S(2)}) %collective-permute-start) | collective-permute-done | bytes 36 | tf_op jit(solution)/shard_map/ppermute | solution.py:23
  16.4 0.6 iota_compare_fusion
  16.9 0.0 collective-permute-done.1
  17.0 3.7 %tile_lists.1.refs_0_ = s32[1024]{0:T(1024)S(1)} custom-call(s32[1,1,2,128]{3,2,1,0:T(2,128)S(1)} %broadcast_select_fusion.1.refs_0_, s32[1,1,2,128]{3,2,1,0:T(2,128)S(1)} %broadcast_select_fusion.refs_1_), custom_call_target="tpu_custom_call" | custom-call | tf_op jit(solution)/shard_map/tile_lists/pallas_call | solution.py:295
  20.6 0.0 copy-start.3
  20.7 0.6 collective-permute-done.2.refs_8_
  21.3 2.7 %collective-permute-start.3 = (bf16[8,128,256]{2,1,0:T(8,128)(2,1)S(1)}, bf16[8,128,256]{2,1,0:T(8,128)(2,1)S(1)}, u32[]{:S(2)}, u32[]{:S(2)}) collective-permute-start(bf16[8,128,256]{2,1,0:T(8,128)(2,1)S(1)} %collective-permute-done.2.refs_8_), channel_id=1, source_target_pairs={{0,2},{1,3},{2,0},{3,1},{4,6},{5,7},{6,4},{7,5},{8,10},{9,11},{10,... | collective-permute-start | bytes 1572872 | tf_op jit(solution)/shard_map/ppermute | solution.py:23
  24.0 0.2 multiply_reduce_fusion.1
  24.2 0.0 collective-permute-done.5.refs_7_
  24.2 0.2 multiply_reduce_fusion.2
  24.4 0.0 copy-done.1
  24.4 0.0 copy-done.2
  24.5 2.3 %early_row_pass.1 = (f32[257,128,128]{2,1,0:T(8,128)S(1)}, bf16[32,128,256]{2,1,0:T(8,128)(2,1)S(1)}, bf16[32,128,256]{2,1,0:T(8,128)(2,1)S(1)}, f32[32,128]{1,0...) custom-call(s32[1024]{0:T(1024)S(1)} %tile_lists.1.refs_0_, ...), custom_call_target="tpu_custom_call" | custom-call | tf_op jit(solution)/shard_map/early_row_pass/pallas_call | solution.py:352
  26.7 8.6 %collective-permute-done.4.refs_3_ = bf16[8,128,256]{2,1,0:T(8,128)(2,1)S(1)} collective-permute-done((bf16[8,128,256]{2,1,0:T(8,128)(2,1)}, bf16[8,128,256]{2,1,0:T(8,128)(2,1)S(1)}, u32[]{:S(2)}, u32[]{:S(2)}) %collective-permute-start.4) | collective-permute-done | bytes 524320 | tf_op jit(solution)/shard_map/ppermute | solution.py:23
  35.3 0.0 collective-permute-start.6
  35.3 0.0 collective-permute-done.3.refs_5_
  35.3 0.2 multiply_reduce_fusion.4
  35.5 1.7 %collective-permute-done.6.refs_4_ = bf16[8,128,256]{2,1,0:T(8,128)(2,1)S(1)} collective-permute-done((bf16[8,128,256]{2,1,0:T(8,128)(2,1)S(1)}, bf16[8,128,256]{2,1,0:T(8,128)(2,1)S(1)}, u32[]{:S(2)}, u32[]{:S(2)}) %collective-permute-start.6) | collective-permute-done | bytes 524320 | tf_op jit(solution)/shard_map/ppermute | solution.py:23
  37.2 0.0 copy-done.3
  37.2 2.0 %late_row_pass.1 = (f32[48,128]{1,0:T(8,128)S(1)}, f32[257,128,128]{2,1,0:T(8,128)S(1)}, bf16[32,128,256]{2,1,0:T(8,128)(2,1)S(1)}, bf16[32,128,256]{2,1,0:T(8,1...) custom-call(s32[1024]{0:T(1024)S(1)} %tile_lists.1.refs_0_, ...), custom_call_target="tpu_custom_call", output_to_operand_aliasing={{1}: (7, {}), {2}: (8, {}), {3}: (9, {}), {4}: (10, {}), {5... | custom-call | tf_op jit(solution)/shard_map/late_row_pass/pallas_call | solution.py:352
  39.2 0.1 collective-permute-start.7
  39.3 2.4 %collective-permute-start.8 = (f32[48,128]{1,0:T(8,128)S(1)}, f32[48,128]{1,0:T(8,128)S(1)}, u32[]{:S(2)}, u32[]{:S(2)}) collective-permute-start(f32[48,128]{1,0:T(8,128)S(1)} %get-tuple-element.30.refs_1_.refs_5_), channel_id=1, source_target_pairs={{0,9},{1,8},{2,11},{3,10},{4,13},{5,12},{6,15},{7,14},{8,1},{9,0},... | collective-permute-start | bytes 73736 | tf_op jit(solution)/shard_map/ppermute | solution.py:23
  41.7 0.6 collective-permute-start.9
  42.4 1.9 %collective-permute-done.7.refs_2_ = f32[48,128]{1,0:T(8,128)S(1)} collective-permute-done((f32[48,128]{1,0:T(8,128)S(1)}, f32[48,128]{1,0:T(8,128)S(1)}, u32[]{:S(2)}, u32[]{:S(2)}) %collective-permute-start.7) | collective-permute-done | bytes 24608 | tf_op jit(solution)/shard_map/ppermute | solution.py:23
  44.3 0.0 collective-permute-done.8.refs_3_
  44.3 0.0 collective-permute-done.9.refs_4_
  44.3 2.9 %column_pass.2 = (f32[32,128]{1,0:T(8,128)S(1)}, f32[257,128,128]{2,1,0:T(8,128)S(1)}, f32[32,128]{1,0:T(8,128)S(1)}) custom-call(s32[1024]{0:T(1024)S(1)} %tile_lists.1.refs_0_, f32[48,128]{1,0:T(8,128)S(1)} %get-tuple-element.30.refs_1_.refs_5_, f32[48,128]{1,0:T(8,128)S(1)} %collective-permute-done.7.refs_2_, ...), custom_call_target="tpu_custom_call" | custom-call | tf_op jit(solution)/shard_map/column_pass/pallas_call | solution.py:383
  47.2 3.9 %collective-permute-start.10 = (f32[32,128]{1,0:T(8,128)S(1)}, f32[32,128]{1,0:T(8,128)S(1)}, u32[]{:S(2)}, u32[]{:S(2)}) collective-permute-start(f32[32,128]{1,0:T(8,128)S(1)} %get-tuple-element.33.refs_1_), channel_id=1, source_target_pairs={{0,2},{1,3},{2,0},{3,1},{4,6},{5,7},{6,4},{7,5},{8,10},{9,11},{10,... | collective-permute-start | bytes 49160 | tf_op jit(solution)/shard_map/ppermute | solution.py:23
  51.1 0.0 collective-permute-start.11
  51.1 1.5 %collective-permute-start.12 = (f32[32,128]{1,0:T(8,128)S(1)}, f32[32,128]{1,0:T(8,128)S(1)}, u32[]{:S(2)}, u32[]{:S(2)}) collective-permute-start(f32[32,128]{1,0:T(8,128)S(1)} %get-tuple-element.33.refs_1_), channel_id=1, source_target_pairs={{0,6},{1,7},{2,4},{3,5},{4,2},{5,3},{6,0},{7,1},{8,14},{9,15},{10,... | collective-permute-start | bytes 49160 | tf_op jit(solution)/shard_map/ppermute | solution.py:23
  52.7 0.0 copy-done.5
  52.7 0.2 collective-permute-done.10.refs_2_
  52.8 2.0 %collective-permute-done.11.refs_3_ = f32[32,128]{1,0:T(8,128)S(1)} collective-permute-done((f32[32,128]{1,0:T(8,128)S(1)}, f32[32,128]{1,0:T(8,128)S(1)}, u32[]{:S(2)}, u32[]{:S(2)}) %collective-permute-start.11) | collective-permute-done | bytes 16416 | tf_op jit(solution)/shard_map/ppermute | solution.py:23
  54.9 0.9 %collective-permute-done.12.refs_4_ = f32[32,128]{1,0:T(8,128)S(1)} collective-permute-done((f32[32,128]{1,0:T(8,128)S(1)}, f32[32,128]{1,0:T(8,128)S(1)}, u32[]{:S(2)}, u32[]{:S(2)}) %collective-permute-start.12) | collective-permute-done | bytes 16416 | tf_op jit(solution)/shard_map/ppermute | solution.py:23
  55.8 2.1 %row_pass.1.refs_1_ = f32[32,128]{1,0:T(8,128)S(1)} custom-call(s32[1024]{0:T(1024)S(1)} %tile_lists.1.refs_0_, f32[32,128]{1,0:T(8,128)S(1)} %get-tuple-element.33.refs_1_, f32[32,128]{1,0:T(8,128)S(1)} %collective-permute-done.10.refs_2_, f32[32,128]{1,0:T(8,128)S(1)} %collective-permute-done.11.refs_3_, f32[32,128]{1,0:T(8,128)S(1)} %collective-permute-done.12.refs_4_, ...), custom_call_target="tpu_custom_call" | custom-call | tf_op jit(solution)/shard_map/row_pass/pallas_call | solution.py:383
  57.9 0.5 collective-permute-start.13
  58.3 0.0 collective-permute-start.14
  58.3 2.6 %collective-permute-start.15 = (f32[32,128]{1,0:T(8,128)S(1)}, f32[32,128]{1,0:T(8,128)S(1)}, u32[]{:S(2)}, u32[]{:S(2)}) collective-permute-start(f32[32,128]{1,0:T(8,128)S(1)} %row_pass.1.refs_1_), channel_id=1, source_target_pairs={{0,1},{1,0},{2,3},{3,2},{4,5},{5,4},{6,7},{7,6},{8,9},{9,8},{10,11... | collective-permute-start | bytes 49160 | tf_op jit(solution)/shard_map/ppermute | solution.py:23
  61.0 1.6 %collective-permute-done.13.refs_2_ = f32[32,128]{1,0:T(8,128)S(1)} collective-permute-done((f32[32,128]{1,0:T(8,128)S(1)}, f32[32,128]{1,0:T(8,128)S(1)}, u32[]{:S(2)}, u32[]{:S(2)}) %collective-permute-start.13) | collective-permute-done | bytes 16416 | tf_op jit(solution)/shard_map/ppermute | solution.py:23
  62.6 0.0 collective-permute-done.14.refs_3_
  62.6 0.0 collective-permute-done.15.refs_4_
  62.6 2.1 %column_pass.3 = (f32[32,128]{1,0:T(8,128)S(1)}, f32[32,128]{1,0:T(8,128)S(1)}) custom-call(s32[1024]{0:T(1024)S(1)} %tile_lists.1.refs_0_, f32[32,128]{1,0:T(8,128)S(1)} %row_pass.1.refs_1_, f32[32,128]{1,0:T(8,128)S(1)} %collective-permute-done.13.refs_2_, f32[32,128]{1,0:T(8,128)S(1)} %collective-permute-done.14.refs_3_, ...), custom_call_target="tpu_custom_call" | custom-call | tf_op jit(solution)/shard_map/column_pass/pallas_call | solution.py:383
  64.6 2.5 %collective-permute-start.16 = (f32[32,128]{1,0:T(8,128)S(1)}, f32[32,128]{1,0:T(8,128)S(1)}, u32[]{:S(2)}, u32[]{:S(2)}) collective-permute-start(f32[32,128]{1,0:T(8,128)S(1)} %get-tuple-element.38.refs_0_), channel_id=1, source_target_pairs={{0,2},{1,3},{2,0},{3,1},{4,6},{5,7},{6,4},{7,5},{8,10},{9,11},{10,... | collective-permute-start | bytes 49160 | tf_op jit(solution)/shard_map/ppermute | solution.py:23
  67.1 0.0 collective-permute-start.17
  67.1 1.5 %collective-permute-start.18 = (f32[32,128]{1,0:T(8,128)S(1)}, f32[32,128]{1,0:T(8,128)S(1)}, u32[]{:S(2)}, u32[]{:S(2)}) collective-permute-start(f32[32,128]{1,0:T(8,128)S(1)} %get-tuple-element.38.refs_0_), channel_id=1, source_target_pairs={{0,6},{1,7},{2,4},{3,5},{4,2},{5,3},{6,0},{7,1},{8,14},{9,15},{10,... | collective-permute-start | bytes 49160 | tf_op jit(solution)/shard_map/ppermute | solution.py:23
  68.7 0.3 multiply_reduce_fusion
  69.0 0.0 collective-permute-done.16.refs_1_
  69.1 1.8 %collective-permute-done.17.refs_2_ = f32[32,128]{1,0:T(8,128)S(1)} collective-permute-done((f32[32,128]{1,0:T(8,128)S(1)}, f32[32,128]{1,0:T(8,128)S(1)}, u32[]{:S(2)}, u32[]{:S(2)}) %collective-permute-start.17) | collective-permute-done | bytes 16416 | tf_op jit(solution)/shard_map/ppermute | solution.py:23
  70.9 0.9 %collective-permute-done.18.refs_3_ = f32[32,128]{1,0:T(8,128)S(1)} collective-permute-done((f32[32,128]{1,0:T(8,128)S(1)}, f32[32,128]{1,0:T(8,128)S(1)}, u32[]{:S(2)}, u32[]{:S(2)}) %collective-permute-start.18) | collective-permute-done | bytes 16416 | tf_op jit(solution)/shard_map/ppermute | solution.py:23
  71.8 1.7 %collective-permute-start.19 = (f32[32,128]{1,0:T(8,128)S(1)}, f32[32,128]{1,0:T(8,128)S(1)}, u32[]{:S(2)}, u32[]{:S(2)}) collective-permute-start(f32[32,128]{1,0:T(8,128)S(1)} %finish.1), channel_id=1, source_target_pairs={{0,8},{1,9},{2,10},{3,11},{4,12},{5,13},{6,14},{7,15},{8,0},{9,1},... | collective-permute-start | bytes 49160 | tf_op jit(solution)/shard_map/ppermute | solution.py:23
  73.5 0.6 fusion.2
  74.1 2.4 %collective-permute-done.19 = f32[32,128]{1,0:T(8,128)S(1)} collective-permute-done((f32[32,128]{1,0:T(8,128)S(1)}, f32[32,128]{1,0:T(8,128)S(1)}, u32[]{:S(2)}, u32[]{:S(2)}) %collective-permute-start.19) | collective-permute-done | bytes 16416 | tf_op jit(solution)/shard_map/ppermute | solution.py:23
  76.5 0.6 fusion
  (15 shorter events, 0.1 us)
Async XLA Ops:
  0.6 14.3 %copy-start.6 = (s32[1,1,2,128]{3,2,1,0:T(2,128)S(1)}, s32[1,1,2,128]{3,2,1,0:T(2,128)}, u32[]{:S(2)}) copy-start(s32[1,1,2,128]{3,2,1,0:T(2,128)} %param.12) | copy-start | bytes 3076
  0.6 20.6 %collective-permute-start.2 = (bf16[8,128,256]{2,1,0:T(8,128)(2,1)}, bf16[8,128,256]{2,1,0:T(8,128)(2,1)S(1)}, u32[]{:S(2)}, u32[]{:S(2)}) collective-permute-start(bf16[8,128,256]{2,1,0:T(8,128)(2,1)} %bitcast.22), channel_id=1, source_target_pairs={{0,4},{1,5},{2,6},{3,7},{4,0},{5,1},{6,2},{7,3},{8,12},{9,13},{10,... | collective-permute-start | bytes 1572872 | tf_op jit(solution)/shard_map/ppermute | solution.py:23
  3.7 20.5 %collective-permute-start.5 = (bf16[8,128,256]{2,1,0:T(8,128)(2,1)}, bf16[8,128,256]{2,1,0:T(8,128)(2,1)S(1)}, u32[]{:S(2)}, u32[]{:S(2)}) collective-permute-start(bf16[8,128,256]{2,1,0:T(8,128)(2,1)} %bitcast.23), channel_id=1, source_target_pairs={{0,2},{1,3},{2,0},{3,1},{4,6},{5,7},{6,4},{7,5},{8,10},{9,11},{10,... | collective-permute-start | bytes 1572872 | tf_op jit(solution)/shard_map/ppermute | solution.py:23
  5.2 11.7 %collective-permute-start.1 = (s32[1,1,2,128]{3,2,1,0:T(2,128)}, s32[1,1,2,128]{3,2,1,0:T(2,128)S(1)}, u32[]{:S(2)}, u32[]{:S(2)}) collective-permute-start(s32[1,1,2,128]{3,2,1,0:T(2,128)} %param.12), channel_id=1, source_target_pairs={{0,8},{1,9},{2,10},{3,11},{4,12},{5,13},{6,14},{7,15},{8,0},{9,1},... | collective-permute-start | bytes 3080 | tf_op jit(solution)/shard_map/ppermute | solution.py:23
  7.8 8.5 %collective-permute-start = (s32[1,1]{1,0:T(1,128)}, s32[1,1]{1,0:T(1,128)}, u32[]{:S(2)}, u32[]{:S(2)}) collective-permute-start(s32[1,1]{1,0:T(1,128)} %param.13), channel_id=1, source_target_pairs={{0,8},{1,9},{2,10},{3,11},{4,12},{5,13},{6,14},{7,15},{8,0},{9,1},... | collective-permute-start | bytes 20 | tf_op jit(solution)/shard_map/ppermute | solution.py:23
  8.2 1.2 %copy-start = (bf16[2048,256]{1,0:T(8,128)(2,1)S(1)}, bf16[2048,256]{1,0:T(8,128)(2,1)}, u32[]{:S(2)}) copy-start(bf16[2048,256]{1,0:T(8,128)(2,1)} %param.7) | copy-start | bytes 3145732
  9.4 5.5 %copy-start.4 = (f32[8192]{0:T(1024)S(1)}, f32[8192]{0:T(1024)}, u32[]{:S(2)}) copy-start(f32[8192]{0:T(1024)} %param.11) | copy-start | bytes 98308
  9.4 15.0 %copy-start.1 = (bf16[2048,256]{1,0:T(8,128)(2,1)S(1)}, bf16[2048,256]{1,0:T(8,128)(2,1)}, u32[]{:S(2)}) copy-start(bf16[2048,256]{1,0:T(8,128)(2,1)} %param.7) | copy-start | bytes 3145732
  9.4 15.0 %copy-start.2 = (bf16[1024,256]{1,0:T(8,128)(2,1)S(1)}, bf16[1024,256]{1,0:T(8,128)(2,1)}, u32[]{:S(2)}) copy-start(bf16[1024,256]{1,0:T(8,128)(2,1)} %param.8) | copy-start | bytes 1572868
  10.3 25.0 %collective-permute-start.4 = (bf16[8,128,256]{2,1,0:T(8,128)(2,1)}, bf16[8,128,256]{2,1,0:T(8,128)(2,1)S(1)}, u32[]{:S(2)}, u32[]{:S(2)}) collective-permute-start(bf16[8,128,256]{2,1,0:T(8,128)(2,1)} %outgoing.1), channel_id=1, source_target_pairs={{0,8},{1,9},{2,10},{3,11},{4,12},{5,13},{6,14},{7,15},{8,0},{9,1},... | collective-permute-start | bytes 1572872 | tf_op jit(solution)/shard_map/ppermute | solution.py:23
  20.6 16.6 %copy-start.3 = (f32[2048]{0:T(1024)S(1)}, f32[2048]{0:T(1024)}, u32[]{:S(2)}) copy-start(f32[2048]{0:T(1024)} %param.9) | copy-start | bytes 24580
  21.3 14.0 %collective-permute-start.3 = (bf16[8,128,256]{2,1,0:T(8,128)(2,1)S(1)}, bf16[8,128,256]{2,1,0:T(8,128)(2,1)S(1)}, u32[]{:S(2)}, u32[]{:S(2)}) collective-permute-start(bf16[8,128,256]{2,1,0:T(8,128)(2,1)S(1)} %collective-permute-done.2.refs_8_), channel_id=1, source_target_pairs={{0,2},{1,3},{2,0},{3,1},{4,6},{5,7},{6,4},{7,5},{8,10},{9,11},{10,... | collective-permute-start | bytes 1572872 | tf_op jit(solution)/shard_map/ppermute | solution.py:23
  35.3 1.9 %collective-permute-start.6 = (bf16[8,128,256]{2,1,0:T(8,128)(2,1)S(1)}, bf16[8,128,256]{2,1,0:T(8,128)(2,1)S(1)}, u32[]{:S(2)}, u32[]{:S(2)}) collective-permute-start(bf16[8,128,256]{2,1,0:T(8,128)(2,1)S(1)} %collective-permute-done.4.refs_3_), channel_id=1, source_target_pairs={{0,1},{1,0},{2,3},{3,2},{4,5},{5,4},{6,7},{7,6},{8,9},{9,8},{10,11... | collective-permute-start | bytes 1572872 | tf_op jit(solution)/shard_map/ppermute | solution.py:23
  39.2 5.1 %collective-permute-start.7 = (f32[48,128]{1,0:T(8,128)S(1)}, f32[48,128]{1,0:T(8,128)S(1)}, u32[]{:S(2)}, u32[]{:S(2)}) collective-permute-start(f32[48,128]{1,0:T(8,128)S(1)} %get-tuple-element.30.refs_1_.refs_5_), channel_id=1, source_target_pairs={{0,8},{1,9},{2,10},{3,11},{4,12},{5,13},{6,14},{7,15},{8,0},{9,1},... | collective-permute-start | bytes 73736 | tf_op jit(solution)/shard_map/ppermute | solution.py:23
  39.3 5.0 %collective-permute-start.8 = (f32[48,128]{1,0:T(8,128)S(1)}, f32[48,128]{1,0:T(8,128)S(1)}, u32[]{:S(2)}, u32[]{:S(2)}) collective-permute-start(f32[48,128]{1,0:T(8,128)S(1)} %get-tuple-element.30.refs_1_.refs_5_), channel_id=1, source_target_pairs={{0,9},{1,8},{2,11},{3,10},{4,13},{5,12},{6,15},{7,14},{8,1},{9,0},... | collective-permute-start | bytes 73736 | tf_op jit(solution)/shard_map/ppermute | solution.py:23
  41.7 2.6 %collective-permute-start.9 = (f32[48,128]{1,0:T(8,128)S(1)}, f32[48,128]{1,0:T(8,128)S(1)}, u32[]{:S(2)}, u32[]{:S(2)}) collective-permute-start(f32[48,128]{1,0:T(8,128)S(1)} %get-tuple-element.30.refs_1_.refs_5_), channel_id=1, source_target_pairs={{0,1},{1,0},{2,3},{3,2},{4,5},{5,4},{6,7},{7,6},{8,9},{9,8},{10,11... | collective-permute-start | bytes 73736 | tf_op jit(solution)/shard_map/ppermute | solution.py:23
  44.3 8.4 %copy-start.5 = (f32[8192]{0:T(1024)S(1)}, f32[8192]{0:T(1024)}, u32[]{:S(2)}) copy-start(f32[8192]{0:T(1024)} %param.10) | copy-start | bytes 98308
  47.2 5.6 %collective-permute-start.10 = (f32[32,128]{1,0:T(8,128)S(1)}, f32[32,128]{1,0:T(8,128)S(1)}, u32[]{:S(2)}, u32[]{:S(2)}) collective-permute-start(f32[32,128]{1,0:T(8,128)S(1)} %get-tuple-element.33.refs_1_), channel_id=1, source_target_pairs={{0,2},{1,3},{2,0},{3,1},{4,6},{5,7},{6,4},{7,5},{8,10},{9,11},{10,... | collective-permute-start | bytes 49160 | tf_op jit(solution)/shard_map/ppermute | solution.py:23
  51.1 3.7 %collective-permute-start.11 = (f32[32,128]{1,0:T(8,128)S(1)}, f32[32,128]{1,0:T(8,128)S(1)}, u32[]{:S(2)}, u32[]{:S(2)}) collective-permute-start(f32[32,128]{1,0:T(8,128)S(1)} %get-tuple-element.33.refs_1_), channel_id=1, source_target_pairs={{0,4},{1,5},{2,6},{3,7},{4,0},{5,1},{6,2},{7,3},{8,12},{9,13},{10,... | collective-permute-start | bytes 49160 | tf_op jit(solution)/shard_map/ppermute | solution.py:23
  51.1 4.6 %collective-permute-start.12 = (f32[32,128]{1,0:T(8,128)S(1)}, f32[32,128]{1,0:T(8,128)S(1)}, u32[]{:S(2)}, u32[]{:S(2)}) collective-permute-start(f32[32,128]{1,0:T(8,128)S(1)} %get-tuple-element.33.refs_1_), channel_id=1, source_target_pairs={{0,6},{1,7},{2,4},{3,5},{4,2},{5,3},{6,0},{7,1},{8,14},{9,15},{10,... | collective-permute-start | bytes 49160 | tf_op jit(solution)/shard_map/ppermute | solution.py:23
  57.9 4.7 %collective-permute-start.13 = (f32[32,128]{1,0:T(8,128)S(1)}, f32[32,128]{1,0:T(8,128)S(1)}, u32[]{:S(2)}, u32[]{:S(2)}) collective-permute-start(f32[32,128]{1,0:T(8,128)S(1)} %row_pass.1.refs_1_), channel_id=1, source_target_pairs={{0,8},{1,9},{2,10},{3,11},{4,12},{5,13},{6,14},{7,15},{8,0},{9,1},... | collective-permute-start | bytes 49160 | tf_op jit(solution)/shard_map/ppermute | solution.py:23
  58.3 4.2 %collective-permute-start.14 = (f32[32,128]{1,0:T(8,128)S(1)}, f32[32,128]{1,0:T(8,128)S(1)}, u32[]{:S(2)}, u32[]{:S(2)}) collective-permute-start(f32[32,128]{1,0:T(8,128)S(1)} %row_pass.1.refs_1_), channel_id=1, source_target_pairs={{0,9},{1,8},{2,11},{3,10},{4,13},{5,12},{6,15},{7,14},{8,1},{9,0},... | collective-permute-start | bytes 49160 | tf_op jit(solution)/shard_map/ppermute | solution.py:23
  58.3 4.2 %collective-permute-start.15 = (f32[32,128]{1,0:T(8,128)S(1)}, f32[32,128]{1,0:T(8,128)S(1)}, u32[]{:S(2)}, u32[]{:S(2)}) collective-permute-start(f32[32,128]{1,0:T(8,128)S(1)} %row_pass.1.refs_1_), channel_id=1, source_target_pairs={{0,1},{1,0},{2,3},{3,2},{4,5},{5,4},{6,7},{7,6},{8,9},{9,8},{10,11... | collective-permute-start | bytes 49160 | tf_op jit(solution)/shard_map/ppermute | solution.py:23
  64.6 4.4 %collective-permute-start.16 = (f32[32,128]{1,0:T(8,128)S(1)}, f32[32,128]{1,0:T(8,128)S(1)}, u32[]{:S(2)}, u32[]{:S(2)}) collective-permute-start(f32[32,128]{1,0:T(8,128)S(1)} %get-tuple-element.38.refs_0_), channel_id=1, source_target_pairs={{0,2},{1,3},{2,0},{3,1},{4,6},{5,7},{6,4},{7,5},{8,10},{9,11},{10,... | collective-permute-start | bytes 49160 | tf_op jit(solution)/shard_map/ppermute | solution.py:23
  67.1 3.7 %collective-permute-start.17 = (f32[32,128]{1,0:T(8,128)S(1)}, f32[32,128]{1,0:T(8,128)S(1)}, u32[]{:S(2)}, u32[]{:S(2)}) collective-permute-start(f32[32,128]{1,0:T(8,128)S(1)} %get-tuple-element.38.refs_0_), channel_id=1, source_target_pairs={{0,4},{1,5},{2,6},{3,7},{4,0},{5,1},{6,2},{7,3},{8,12},{9,13},{10,... | collective-permute-start | bytes 49160 | tf_op jit(solution)/shard_map/ppermute | solution.py:23
  67.1 4.6 %collective-permute-start.18 = (f32[32,128]{1,0:T(8,128)S(1)}, f32[32,128]{1,0:T(8,128)S(1)}, u32[]{:S(2)}, u32[]{:S(2)}) collective-permute-start(f32[32,128]{1,0:T(8,128)S(1)} %get-tuple-element.38.refs_0_), channel_id=1, source_target_pairs={{0,6},{1,7},{2,4},{3,5},{4,2},{5,3},{6,0},{7,1},{8,14},{9,15},{10,... | collective-permute-start | bytes 49160 | tf_op jit(solution)/shard_map/ppermute | solution.py:23
  71.8 4.7 %collective-permute-start.19 = (f32[32,128]{1,0:T(8,128)S(1)}, f32[32,128]{1,0:T(8,128)S(1)}, u32[]{:S(2)}, u32[]{:S(2)}) collective-permute-start(f32[32,128]{1,0:T(8,128)S(1)} %finish.1), channel_id=1, source_target_pairs={{0,8},{1,9},{2,10},{3,11},{4,12},{5,13},{6,14},{7,15},{8,0},{9,1},... | collective-permute-start | bytes 49160 | tf_op jit(solution)/shard_map/ppermute | solution.py:23

commit v2 on v1

--- a/solution.py
+++ b/solution.py
@@ -12,6 +12,7 @@
 FLOOR = -1e30
 MAKE_UNROLL = 20
 READ_UNROLL = 8
+TURN_UNROLL = 16
 PADDING = max(MAKE_UNROLL, READ_UNROLL)
 VMEM_LIMIT = 3 * 1024 * 1024
 
@@ -186,11 +187,11 @@
         out[2 * own :] = jnp.log2(mass[...])
 
 
-def pass_kernel(scale, half, slots, row_pass, n_parts, makes, has_out, ids_any, *refs):
+def pass_kernel(half, slots, row_pass, n_parts, makes, has_out, ids_any, *refs):
     parts, refs = refs[:n_parts], refs[n_parts:]
     mass, refs = refs[0], refs[1:]
     if makes:
-        src, tgt, out, products, pair, refs = *refs[:5], refs[5:]
+        turned, out, products, pair, refs = *refs[:4], refs[4:]
     else:
         products, out, refs = *refs[:2], refs[2:]
     if has_out:
@@ -216,17 +217,13 @@
     def scores_of(slot):
         if not makes:
             return products[jnp.minimum(slot, products.shape[0] - 1)]
-        made = scale * lax.dot_general(
-            src[ids[slot]],
-            tgt[ids[slots + slot]],
-            (((1,), (1,)), ((), ())),
-            preferred_element_type=jnp.float32,
-        )
-        products[jnp.minimum(slot, products.shape[0] - 1)] = made
+        place = jnp.minimum(slot, products.shape[0] - 1)
+        made = jnp.transpose(turned[place])
+        products[place] = made
         return made
 
     sweep(
-        MAKE_UNROLL if makes else READ_UNROLL,
+        TURN_UNROLL if makes else READ_UNROLL,
         0,
         ids[2 * slots],
         scores_of,
@@ -371,9 +368,8 @@
         True, [source_mass.reshape(src_rows, TILE), *kept]
     )[:5]
 
-    def run(row_pass, parts, mass, given, has_out):
+    def run(row_pass, parts, mass, products, makes, has_out):
         known, reduced = (col_blocks, 2 * src_rows) if row_pass else (2 * src_rows, col_blocks)
-        makes = len(given) == 2
         out_shape = [jax.ShapeDtypeStruct((reduced, TILE), jnp.float32)]
         if makes:
             out_shape.append(jax.ShapeDtypeStruct((2 * listed + 1, TILE, TILE), jnp.float32))
@@ -381,14 +377,14 @@
         if has_out:
             out_shape.append(jax.ShapeDtypeStruct((known, TILE), jnp.float32))
         return pl.pallas_call(
-            lambda *refs: pass_kernel(scale, half, slots, row_pass, len(parts), makes, has_out, *refs),
+            lambda *refs: pass_kernel(half, slots, row_pass, len(parts), makes, has_out, *refs),
             out_shape=out_shape,
-            in_specs=[anywhere] + [vmem] * (len(parts) + 1 + len(given)),
+            in_specs=[anywhere] + [vmem] * (len(parts) + 2),
             out_specs=[vmem] * len(out_shape),
             scratch_shapes=accumulators(known, reduced) + [pltpu.SemaphoreType.DMA],
             compiler_params=params,
             name="row_pass" if row_pass else "column_pass",
-        )(ids, *parts, mass, *given)
+        )(ids, *parts, mass, products)
 
     def share_rows(part):
         return [part, hop(part, half), hop(part, half, 1), hop(part, 0, 1)]
@@ -396,9 +392,9 @@
     def share_columns(part):
         return [part] + [hop(part, mask) for mask in range(1, half)]
 
-    columns, by_row, log_pair = run(False, share_rows(rows), rows, [src, tgt], False)
-    rows = run(True, share_columns(columns), log_half, [by_col], False)[0]
-    columns, source_final = run(False, share_rows(rows), log_pair, [by_row], True)
+    columns, by_row, log_pair = run(False, share_rows(rows), rows, by_col, True, False)
+    rows = run(True, share_columns(columns), log_half, by_col, False, False)[0]
+    columns, source_final = run(False, share_rows(rows), log_pair, by_row, False, True)
     gathered = share_columns(columns)
     target_final = pl.pallas_call(
         lambda *refs: finish_kernel(scale, to_unit, len(gathered), *refs),

time: 77.7 us -> 76.8 us (0.988)
  starting transfers between devices: 30.3 us -> 27.4 us
  waiting for transfers between devices: 24.1 us -> 26.2 us
    ppermute x20, starting transfers between devices: 30.3 us -> 27.4 us  [hop(): lax.ppermute(value, ('src', 'tgt'), [(i, i ^ flip) for i in range(total)])]
    ppermute x20, waiting for transfers between devices: 24.1 us -> 26.2 us  [hop(): lax.ppermute(value, ('src', 'tgt'), [(i, i ^ flip) for i in range(total)])]
  transfers between devices with their start and end apart: 20 -> 20, of which waited for: 12 -> 13; matrix products, arithmetic and copies ran while one was open for 4% -> 4% of each run, Pallas kernels for 9% -> 9%
where the time goes in v2:
time: 76.8 us; the launch traced here: 76.3 us
  starting transfers between devices  27.4 us (36%)
  waiting for transfers between devices  26.2 us (34%)
  Pallas kernels  15.7 us (20%)
  other arithmetic  4.05 us (5%)
  between operations  1.58 us (2%)
  local copies, waits for them, and re-layouts  1.25 us (2%)
    ppermute x20, starting transfers between devices, hop(): lax.ppermute(value, ('src', 'tgt'), [(i, i ^ flip) for i in range(total)])  27.4 us
    ppermute x20, waiting for transfers between devices, hop(): lax.ppermute(value, ('src', 'tgt'), [(i, i ^ flip) for i in range(total)])  26.2 us
    pallas_call x3, Pallas kernels, run(): pl.pallas_call(lambda *refs: pass_kernel(half, slots, row_pass, len(parts...  6.75 us
    pallas_call x2, Pallas kernels, first(): pl.pallas_call(lambda *refs: first_kernel(scale, half, slots, late, (src_...  4.45 us
    pallas_call x1, Pallas kernels, shards(): pl.pallas_call(lambda *refs: list_kernel(half, src_rows, own_cols, slots,...  3.68 us
    reduce_sum x5, other arithmetic, half_norms(): return 0.5 * jnp.sum(wide * wide, axis=-1).reshape(-1, TILE)  2.23 us
  transfers between devices with their start and end apart: 20, of which 13 were waited for; matrix products, arithmetic and copies ran while one was open for 4% of the time, Pallas kernels for 9%

profile of v2, /device:TPU:0, one launch (start us, length us, event | category | flops | bytes accessed | tf_op | source)
XLA Modules:
  0.0 76.3 jit_solution(12685006621091313262)
XLA Ops:
  0.6 0.0 copy-start.6
  0.6 3.1 %collective-permute-start.2 = (bf16[8,128,256]{2,1,0:T(8,128)(2,1)}, bf16[8,128,256]{2,1,0:T(8,128)(2,1)S(1)}, u32[]{:S(2)}, u32[]{:S(2)}) collective-permute-start(bf16[8,128,256]{2,1,0:T(8,128)(2,1)} %bitcast.22), channel_id=1, source_target_pairs={{0,4},{1,5},{2,6},{3,7},{4,0},{5,1},{6,2},{7,3},{8,12},{9,13},{10,... | collective-permute-start | bytes 1572872 | tf_op jit(solution)/shard_map/ppermute | solution.py:24
  3.7 1.5 %collective-permute-start.5 = (bf16[8,128,256]{2,1,0:T(8,128)(2,1)}, bf16[8,128,256]{2,1,0:T(8,128)(2,1)S(1)}, u32[]{:S(2)}, u32[]{:S(2)}) collective-permute-start(bf16[8,128,256]{2,1,0:T(8,128)(2,1)} %bitcast.23), channel_id=1, source_target_pairs={{0,2},{1,3},{2,0},{3,1},{4,6},{5,7},{6,4},{7,5},{8,10},{9,11},{10,... | collective-permute-start | bytes 1572872 | tf_op jit(solution)/shard_map/ppermute | solution.py:24
  5.2 2.6 %collective-permute-start.1 = (s32[1,1,2,128]{3,2,1,0:T(2,128)}, s32[1,1,2,128]{3,2,1,0:T(2,128)S(1)}, u32[]{:S(2)}, u32[]{:S(2)}) collective-permute-start(s32[1,1,2,128]{3,2,1,0:T(2,128)} %param.12), channel_id=1, source_target_pairs={{0,8},{1,9},{2,10},{3,11},{4,12},{5,13},{6,14},{7,15},{8,0},{9,1},... | collective-permute-start | bytes 3080 | tf_op jit(solution)/shard_map/ppermute | solution.py:24
  7.8 0.3 collective-permute-start
  8.2 1.2 %copy-done = bf16[2048,256]{1,0:T(8,128)(2,1)S(1)} copy-done((bf16[2048,256]{1,0:T(8,128)(2,1)S(1)}, bf16[2048,256]{1,0:T(8,128)(2,1)}, u32[]{:S(2)}) %copy-start) | copy-done | bytes 1048600
  9.4 0.8 %outgoing.1 = bf16[8,128,256]{2,1,0:T(8,128)(2,1)} custom-call(bf16[16,128,256]{2,1,0:T(8,128)(2,1)S(1)} %bitcast.20), custom_call_target="tpu_custom_call" | custom-call | tf_op jit(solution)/shard_map/outgoing/pallas_call | solution.py:277
  10.3 2.7 %collective-permute-start.4 = (bf16[8,128,256]{2,1,0:T(8,128)(2,1)}, bf16[8,128,256]{2,1,0:T(8,128)(2,1)S(1)}, u32[]{:S(2)}, u32[]{:S(2)}) collective-permute-start(bf16[8,128,256]{2,1,0:T(8,128)(2,1)} %outgoing.1), channel_id=1, source_target_pairs={{0,8},{1,9},{2,10},{3,11},{4,12},{5,13},{6,14},{7,15},{8,0},{9,1},... | collective-permute-start | bytes 1572872 | tf_op jit(solution)/shard_map/ppermute | solution.py:24
  13.6 1.3 %multiply_reduce_fusion.3 = f32[1024]{0:T(1024)S(1)} fusion(bf16[1024,256]{1,0:T(8,128)(2,1)} %param.8), kind=kLoop, calls=%fused_computation.3 | loop fusion | flops 785408 | bytes 528384 | tf_op jit(solution)/shard_map/reduce_sum | solution.py:29
  14.9 0.0 copy-done.4
  14.9 0.0 copy-done.6
  14.9 1.5 %collective-permute-done = s32[1,1]{1,0:T(1,128)} collective-permute-done((s32[1,1]{1,0:T(1,128)}, s32[1,1]{1,0:T(1,128)}, u32[]{:S(2)}, u32[]{:S(2)}) %collective-permute-start) | collective-permute-done | bytes 36 | tf_op jit(solution)/shard_map/ppermute | solution.py:24
  16.4 0.6 iota_compare_fusion
  16.9 0.0 collective-permute-done.1
  17.0 3.7 %tile_lists.1.refs_0_ = s32[1024]{0:T(1024)S(1)} custom-call(s32[1,1,2,128]{3,2,1,0:T(2,128)S(1)} %broadcast_select_fusion.1.refs_0_, s32[1,1,2,128]{3,2,1,0:T(2,128)S(1)} %broadcast_select_fusion.refs_1_), custom_call_target="tpu_custom_call" | custom-call | tf_op jit(solution)/shard_map/tile_lists/pallas_call | solution.py:292
  20.6 0.0 copy-start.3
  20.7 0.6 collective-permute-done.2.refs_8_
  21.3 2.7 %collective-permute-start.3 = (bf16[8,128,256]{2,1,0:T(8,128)(2,1)S(1)}, bf16[8,128,256]{2,1,0:T(8,128)(2,1)S(1)}, u32[]{:S(2)}, u32[]{:S(2)}) collective-permute-start(bf16[8,128,256]{2,1,0:T(8,128)(2,1)S(1)} %collective-permute-done.2.refs_8_), channel_id=1, source_target_pairs={{0,2},{1,3},{2,0},{3,1},{4,6},{5,7},{6,4},{7,5},{8,10},{9,11},{10,... | collective-permute-start | bytes 1572872 | tf_op jit(solution)/shard_map/ppermute | solution.py:24
  24.0 0.2 multiply_reduce_fusion.1
  24.2 0.0 collective-permute-done.5.refs_7_
  24.2 0.2 multiply_reduce_fusion.2
  24.4 0.0 copy-done.1
  24.4 0.0 copy-done.2
  24.5 2.3 %early_row_pass.1 = (f32[257,128,128]{2,1,0:T(8,128)S(1)}, bf16[32,128,256]{2,1,0:T(8,128)(2,1)S(1)}, bf16[32,128,256]{2,1,0:T(8,128)(2,1)S(1)}, f32[32,128]{1,0...) custom-call(s32[1024]{0:T(1024)S(1)} %tile_lists.1.refs_0_, ...), custom_call_target="tpu_custom_call" | custom-call | tf_op jit(solution)/shard_map/early_row_pass/pallas_call | solution.py:349
  26.8 8.5 %collective-permute-done.4.refs_3_ = bf16[8,128,256]{2,1,0:T(8,128)(2,1)S(1)} collective-permute-done((bf16[8,128,256]{2,1,0:T(8,128)(2,1)}, bf16[8,128,256]{2,1,0:T(8,128)(2,1)S(1)}, u32[]{:S(2)}, u32[]{:S(2)}) %collective-permute-start.4) | collective-permute-done | bytes 524320 | tf_op jit(solution)/shard_map/ppermute | solution.py:24
  35.3 0.0 collective-permute-start.6
  35.3 0.0 collective-permute-done.3.refs_5_
  35.3 0.2 multiply_reduce_fusion.4
  35.5 1.7 %collective-permute-done.6.refs_4_ = bf16[8,128,256]{2,1,0:T(8,128)(2,1)S(1)} collective-permute-done((bf16[8,128,256]{2,1,0:T(8,128)(2,1)S(1)}, bf16[8,128,256]{2,1,0:T(8,128)(2,1)S(1)}, u32[]{:S(2)}, u32[]{:S(2)}) %collective-permute-start.6) | collective-permute-done | bytes 524320 | tf_op jit(solution)/shard_map/ppermute | solution.py:24
  37.2 0.0 copy-done.3
  37.2 2.1 %late_row_pass.1 = (f32[48,128]{1,0:T(8,128)S(1)}, f32[257,128,128]{2,1,0:T(8,128)S(1)}, bf16[32,128,256]{2,1,0:T(8,128)(2,1)S(1)}, bf16[32,128,256]{2,1,0:T(8,1...) custom-call(s32[1024]{0:T(1024)S(1)} %tile_lists.1.refs_0_, ...), custom_call_target="tpu_custom_call", output_to_operand_aliasing={{1}: (7, {}), {2}: (8, {}), {3}: (9, {}), {4}: (10, {}), {5... | custom-call | tf_op jit(solution)/shard_map/late_row_pass/pallas_call | solution.py:349
  39.3 0.1 collective-permute-start.7
  39.4 2.4 %collective-permute-start.8 = (f32[48,128]{1,0:T(8,128)S(1)}, f32[48,128]{1,0:T(8,128)S(1)}, u32[]{:S(2)}, u32[]{:S(2)}) collective-permute-start(f32[48,128]{1,0:T(8,128)S(1)} %get-tuple-element.28.refs_1_.refs_5_), channel_id=1, source_target_pairs={{0,9},{1,8},{2,11},{3,10},{4,13},{5,12},{6,15},{7,14},{8,1},{9,0},... | collective-permute-start | bytes 73736 | tf_op jit(solution)/shard_map/ppermute | solution.py:24
  41.8 0.7 collective-permute-start.9
  42.4 2.0 %collective-permute-done.7.refs_2_ = f32[48,128]{1,0:T(8,128)S(1)} collective-permute-done((f32[48,128]{1,0:T(8,128)S(1)}, f32[48,128]{1,0:T(8,128)S(1)}, u32[]{:S(2)}, u32[]{:S(2)}) %collective-permute-start.7) | collective-permute-done | bytes 24608 | tf_op jit(solution)/shard_map/ppermute | solution.py:24
  44.4 0.0 collective-permute-done.8.refs_3_
  44.4 0.0 collective-permute-done.9.refs_4_
  44.4 2.6 %column_pass.2 = (f32[32,128]{1,0:T(8,128)S(1)}, f32[257,128,128]{2,1,0:T(8,128)S(1)}, f32[32,128]{1,0:T(8,128)S(1)}) custom-call(s32[1024]{0:T(1024)S(1)} %tile_lists.1.refs_0_, f32[48,128]{1,0:T(8,128)S(1)} %get-tuple-element.28.refs_1_.refs_5_, f32[48,128]{1,0:T(8,128)S(1)} %collective-permute-done.7.refs_2_, ...), custom_call_target="tpu_custom_call" | custom-call | tf_op jit(solution)/shard_map/column_pass/pallas_call | solution.py:379
  47.1 0.7 collective-permute-start.10
  47.8 2.2 %collective-permute-start.11 = (f32[32,128]{1,0:T(8,128)S(1)}, f32[32,128]{1,0:T(8,128)S(1)}, u32[]{:S(2)}, u32[]{:S(2)}) collective-permute-start(f32[32,128]{1,0:T(8,128)S(1)} %get-tuple-element.30.refs_1_), channel_id=1, source_target_pairs={{0,4},{1,5},{2,6},{3,7},{4,0},{5,1},{6,2},{7,3},{8,12},{9,13},{10,... | collective-permute-start | bytes 49160 | tf_op jit(solution)/shard_map/ppermute | solution.py:24
  50.0 0.6 collective-permute-start.12
  50.6 0.0 copy-done.5
  50.6 0.2 collective-permute-done.10.refs_2_
  50.9 0.9 %collective-permute-done.11.refs_3_ = f32[32,128]{1,0:T(8,128)S(1)} collective-permute-done((f32[32,128]{1,0:T(8,128)S(1)}, f32[32,128]{1,0:T(8,128)S(1)}, u32[]{:S(2)}, u32[]{:S(2)}) %collective-permute-start.11) | collective-permute-done | bytes 16416 | tf_op jit(solution)/shard_map/ppermute | solution.py:24
  51.8 2.9 %collective-permute-done.12.refs_4_ = f32[32,128]{1,0:T(8,128)S(1)} collective-permute-done((f32[32,128]{1,0:T(8,128)S(1)}, f32[32,128]{1,0:T(8,128)S(1)}, u32[]{:S(2)}, u32[]{:S(2)}) %collective-permute-start.12) | collective-permute-done | bytes 16416 | tf_op jit(solution)/shard_map/ppermute | solution.py:24
  54.7 2.1 %row_pass.1.refs_1_ = f32[32,128]{1,0:T(8,128)S(1)} custom-call(s32[1024]{0:T(1024)S(1)} %tile_lists.1.refs_0_, f32[32,128]{1,0:T(8,128)S(1)} %get-tuple-element.30.refs_1_, f32[32,128]{1,0:T(8,128)S(1)} %collective-permute-done.10.refs_2_, f32[32,128]{1,0:T(8,128)S(1)} %collective-permute-done.11.refs_3_, f32[32,128]{1,0:T(8,128)S(1)} %collective-permute-done.12.refs_4_, ...), custom_call_target="tpu_custom_call" | custom-call | tf_op jit(solution)/shard_map/row_pass/pallas_call | solution.py:379
  56.7 1.4 %collective-permute-start.13 = (f32[32,128]{1,0:T(8,128)S(1)}, f32[32,128]{1,0:T(8,128)S(1)}, u32[]{:S(2)}, u32[]{:S(2)}) collective-permute-start(f32[32,128]{1,0:T(8,128)S(1)} %row_pass.1.refs_1_), channel_id=1, source_target_pairs={{0,8},{1,9},{2,10},{3,11},{4,12},{5,13},{6,14},{7,15},{8,0},{9,1},... | collective-permute-start | bytes 49160 | tf_op jit(solution)/shard_map/ppermute | solution.py:24
  58.2 0.0 collective-permute-start.14
  58.2 1.7 %collective-permute-start.15 = (f32[32,128]{1,0:T(8,128)S(1)}, f32[32,128]{1,0:T(8,128)S(1)}, u32[]{:S(2)}, u32[]{:S(2)}) collective-permute-start(f32[32,128]{1,0:T(8,128)S(1)} %row_pass.1.refs_1_), channel_id=1, source_target_pairs={{0,1},{1,0},{2,3},{3,2},{4,5},{5,4},{6,7},{7,6},{8,9},{9,8},{10,11... | collective-permute-start | bytes 49160 | tf_op jit(solution)/shard_map/ppermute | solution.py:24
  59.8 1.6 %collective-permute-done.13.refs_2_ = f32[32,128]{1,0:T(8,128)S(1)} collective-permute-done((f32[32,128]{1,0:T(8,128)S(1)}, f32[32,128]{1,0:T(8,128)S(1)}, u32[]{:S(2)}, u32[]{:S(2)}) %collective-permute-start.13) | collective-permute-done | bytes 16416 | tf_op jit(solution)/shard_map/ppermute | solution.py:24
  61.4 1.0 %collective-permute-done.14.refs_3_ = f32[32,128]{1,0:T(8,128)S(1)} collective-permute-done((f32[32,128]{1,0:T(8,128)S(1)}, f32[32,128]{1,0:T(8,128)S(1)}, u32[]{:S(2)}, u32[]{:S(2)}) %collective-permute-start.14) | collective-permute-done | bytes 16416 | tf_op jit(solution)/shard_map/ppermute | solution.py:24
  62.5 0.0 collective-permute-done.15.refs_4_
  62.5 2.1 %column_pass.3 = (f32[32,128]{1,0:T(8,128)S(1)}, f32[32,128]{1,0:T(8,128)S(1)}) custom-call(s32[1024]{0:T(1024)S(1)} %tile_lists.1.refs_0_, f32[32,128]{1,0:T(8,128)S(1)} %row_pass.1.refs_1_, f32[32,128]{1,0:T(8,128)S(1)} %collective-permute-done.13.refs_2_, f32[32,128]{1,0:T(8,128)S(1)} %collective-permute-done.14.refs_3_, ...), custom_call_target="tpu_custom_call" | custom-call | tf_op jit(solution)/shard_map/column_pass/pallas_call | solution.py:379
  64.5 0.1 collective-permute-start.16
  64.6 1.5 %collective-permute-start.17 = (f32[32,128]{1,0:T(8,128)S(1)}, f32[32,128]{1,0:T(8,128)S(1)}, u32[]{:S(2)}, u32[]{:S(2)}) collective-permute-start(f32[32,128]{1,0:T(8,128)S(1)} %get-tuple-element.34.refs_0_), channel_id=1, source_target_pairs={{0,4},{1,5},{2,6},{3,7},{4,0},{5,1},{6,2},{7,3},{8,12},{9,13},{10,... | collective-permute-start | bytes 49160 | tf_op jit(solution)/shard_map/ppermute | solution.py:24
  66.1 2.0 %collective-permute-start.18 = (f32[32,128]{1,0:T(8,128)S(1)}, f32[32,128]{1,0:T(8,128)S(1)}, u32[]{:S(2)}, u32[]{:S(2)}) collective-permute-start(f32[32,128]{1,0:T(8,128)S(1)} %get-tuple-element.34.refs_0_), channel_id=1, source_target_pairs={{0,6},{1,7},{2,4},{3,5},{4,2},{5,3},{6,0},{7,1},{8,14},{9,15},{10,... | collective-permute-start | bytes 49160 | tf_op jit(solution)/shard_map/ppermute | solution.py:24
  68.1 0.3 multiply_reduce_fusion
  68.4 0.0 collective-permute-done.16.refs_1_
  68.5 0.1 collective-permute-done.17.refs_2_
  68.5 2.2 %collective-permute-done.18.refs_3_ = f32[32,128]{1,0:T(8,128)S(1)} collective-permute-done((f32[32,128]{1,0:T(8,128)S(1)}, f32[32,128]{1,0:T(8,128)S(1)}, u32[]{:S(2)}, u32[]{:S(2)}) %collective-permute-start.18) | collective-permute-done | bytes 16416 | tf_op jit(solution)/shard_map/ppermute | solution.py:24
  70.8 1.2 %collective-permute-start.19 = (f32[32,128]{1,0:T(8,128)S(1)}, f32[32,128]{1,0:T(8,128)S(1)}, u32[]{:S(2)}, u32[]{:S(2)}) collective-permute-start(f32[32,128]{1,0:T(8,128)S(1)} %finish.1), channel_id=1, source_target_pairs={{0,8},{1,9},{2,10},{3,11},{4,12},{5,13},{6,14},{7,15},{8,0},{9,1},... | collective-permute-start | bytes 49160 | tf_op jit(solution)/shard_map/ppermute | solution.py:24
  72.0 0.6 fusion.2
  72.6 3.1 %collective-permute-done.19 = f32[32,128]{1,0:T(8,128)S(1)} collective-permute-done((f32[32,128]{1,0:T(8,128)S(1)}, f32[32,128]{1,0:T(8,128)S(1)}, u32[]{:S(2)}, u32[]{:S(2)}) %collective-permute-start.19) | collective-permute-done | bytes 16416 | tf_op jit(solution)/shard_map/ppermute | solution.py:24
  75.7 0.6 fusion
  (15 shorter events, 0.1 us)
Async XLA Ops:
  0.6 14.3 %copy-start.6 = (s32[1,1,2,128]{3,2,1,0:T(2,128)S(1)}, s32[1,1,2,128]{3,2,1,0:T(2,128)}, u32[]{:S(2)}) copy-start(s32[1,1,2,128]{3,2,1,0:T(2,128)} %param.12) | copy-start | bytes 3076
  0.6 20.6 %collective-permute-start.2 = (bf16[8,128,256]{2,1,0:T(8,128)(2,1)}, bf16[8,128,256]{2,1,0:T(8,128)(2,1)S(1)}, u32[]{:S(2)}, u32[]{:S(2)}) collective-permute-start(bf16[8,128,256]{2,1,0:T(8,128)(2,1)} %bitcast.22), channel_id=1, source_target_pairs={{0,4},{1,5},{2,6},{3,7},{4,0},{5,1},{6,2},{7,3},{8,12},{9,13},{10,... | collective-permute-start | bytes 1572872 | tf_op jit(solution)/shard_map/ppermute | solution.py:24
  3.7 20.5 %collective-permute-start.5 = (bf16[8,128,256]{2,1,0:T(8,128)(2,1)}, bf16[8,128,256]{2,1,0:T(8,128)(2,1)S(1)}, u32[]{:S(2)}, u32[]{:S(2)}) collective-permute-start(bf16[8,128,256]{2,1,0:T(8,128)(2,1)} %bitcast.23), channel_id=1, source_target_pairs={{0,2},{1,3},{2,0},{3,1},{4,6},{5,7},{6,4},{7,5},{8,10},{9,11},{10,... | collective-permute-start | bytes 1572872 | tf_op jit(solution)/shard_map/ppermute | solution.py:24
  5.2 11.7 %collective-permute-start.1 = (s32[1,1,2,128]{3,2,1,0:T(2,128)}, s32[1,1,2,128]{3,2,1,0:T(2,128)S(1)}, u32[]{:S(2)}, u32[]{:S(2)}) collective-permute-start(s32[1,1,2,128]{3,2,1,0:T(2,128)} %param.12), channel_id=1, source_target_pairs={{0,8},{1,9},{2,10},{3,11},{4,12},{5,13},{6,14},{7,15},{8,0},{9,1},... | collective-permute-start | bytes 3080 | tf_op jit(solution)/shard_map/ppermute | solution.py:24
  7.8 8.5 %collective-permute-start = (s32[1,1]{1,0:T(1,128)}, s32[1,1]{1,0:T(1,128)}, u32[]{:S(2)}, u32[]{:S(2)}) collective-permute-start(s32[1,1]{1,0:T(1,128)} %param.13), channel_id=1, source_target_pairs={{0,8},{1,9},{2,10},{3,11},{4,12},{5,13},{6,14},{7,15},{8,0},{9,1},... | collective-permute-start | bytes 20 | tf_op jit(solution)/shard_map/ppermute | solution.py:24
  8.2 1.2 %copy-start = (bf16[2048,256]{1,0:T(8,128)(2,1)S(1)}, bf16[2048,256]{1,0:T(8,128)(2,1)}, u32[]{:S(2)}) copy-start(bf16[2048,256]{1,0:T(8,128)(2,1)} %param.7) | copy-start | bytes 3145732
  9.4 5.5 %copy-start.4 = (f32[8192]{0:T(1024)S(1)}, f32[8192]{0:T(1024)}, u32[]{:S(2)}) copy-start(f32[8192]{0:T(1024)} %param.11) | copy-start | bytes 98308
  9.4 15.0 %copy-start.1 = (bf16[2048,256]{1,0:T(8,128)(2,1)S(1)}, bf16[2048,256]{1,0:T(8,128)(2,1)}, u32[]{:S(2)}) copy-start(bf16[2048,256]{1,0:T(8,128)(2,1)} %param.7) | copy-start | bytes 3145732
  9.4 15.0 %copy-start.2 = (bf16[1024,256]{1,0:T(8,128)(2,1)S(1)}, bf16[1024,256]{1,0:T(8,128)(2,1)}, u32[]{:S(2)}) copy-start(bf16[1024,256]{1,0:T(8,128)(2,1)} %param.8) | copy-start | bytes 1572868
  10.3 25.0 %collective-permute-start.4 = (bf16[8,128,256]{2,1,0:T(8,128)(2,1)}, bf16[8,128,256]{2,1,0:T(8,128)(2,1)S(1)}, u32[]{:S(2)}, u32[]{:S(2)}) collective-permute-start(bf16[8,128,256]{2,1,0:T(8,128)(2,1)} %outgoing.1), channel_id=1, source_target_pairs={{0,8},{1,9},{2,10},{3,11},{4,12},{5,13},{6,14},{7,15},{8,0},{9,1},... | collective-permute-start | bytes 1572872 | tf_op jit(solution)/shard_map/ppermute | solution.py:24
  20.6 16.6 %copy-start.3 = (f32[2048]{0:T(1024)S(1)}, f32[2048]{0:T(1024)}, u32[]{:S(2)}) copy-start(f32[2048]{0:T(1024)} %param.9) | copy-start | bytes 24580
  21.3 14.0 %collective-permute-start.3 = (bf16[8,128,256]{2,1,0:T(8,128)(2,1)S(1)}, bf16[8,128,256]{2,1,0:T(8,128)(2,1)S(1)}, u32[]{:S(2)}, u32[]{:S(2)}) collective-permute-start(bf16[8,128,256]{2,1,0:T(8,128)(2,1)S(1)} %collective-permute-done.2.refs_8_), channel_id=1, source_target_pairs={{0,2},{1,3},{2,0},{3,1},{4,6},{5,7},{6,4},{7,5},{8,10},{9,11},{10,... | collective-permute-start | bytes 1572872 | tf_op jit(solution)/shard_map/ppermute | solution.py:24
  35.3 1.9 %collective-permute-start.6 = (bf16[8,128,256]{2,1,0:T(8,128)(2,1)S(1)}, bf16[8,128,256]{2,1,0:T(8,128)(2,1)S(1)}, u32[]{:S(2)}, u32[]{:S(2)}) collective-permute-start(bf16[8,128,256]{2,1,0:T(8,128)(2,1)S(1)} %collective-permute-done.4.refs_3_), channel_id=1, source_target_pairs={{0,1},{1,0},{2,3},{3,2},{4,5},{5,4},{6,7},{7,6},{8,9},{9,8},{10,11... | collective-permute-start | bytes 1572872 | tf_op jit(solution)/shard_map/ppermute | solution.py:24
  39.3 5.1 %collective-permute-start.7 = (f32[48,128]{1,0:T(8,128)S(1)}, f32[48,128]{1,0:T(8,128)S(1)}, u32[]{:S(2)}, u32[]{:S(2)}) collective-permute-start(f32[48,128]{1,0:T(8,128)S(1)} %get-tuple-element.28.refs_1_.refs_5_), channel_id=1, source_target_pairs={{0,8},{1,9},{2,10},{3,11},{4,12},{5,13},{6,14},{7,15},{8,0},{9,1},... | collective-permute-start | bytes 73736 | tf_op jit(solution)/shard_map/ppermute | solution.py:24
  39.4 5.0 %collective-permute-start.8 = (f32[48,128]{1,0:T(8,128)S(1)}, f32[48,128]{1,0:T(8,128)S(1)}, u32[]{:S(2)}, u32[]{:S(2)}) collective-permute-start(f32[48,128]{1,0:T(8,128)S(1)} %get-tuple-element.28.refs_1_.refs_5_), channel_id=1, source_target_pairs={{0,9},{1,8},{2,11},{3,10},{4,13},{5,12},{6,15},{7,14},{8,1},{9,0},... | collective-permute-start | bytes 73736 | tf_op jit(solution)/shard_map/ppermute | solution.py:24
  41.8 2.6 %collective-permute-start.9 = (f32[48,128]{1,0:T(8,128)S(1)}, f32[48,128]{1,0:T(8,128)S(1)}, u32[]{:S(2)}, u32[]{:S(2)}) collective-permute-start(f32[48,128]{1,0:T(8,128)S(1)} %get-tuple-element.28.refs_1_.refs_5_), channel_id=1, source_target_pairs={{0,1},{1,0},{2,3},{3,2},{4,5},{5,4},{6,7},{7,6},{8,9},{9,8},{10,11... | collective-permute-start | bytes 73736 | tf_op jit(solution)/shard_map/ppermute | solution.py:24
  44.4 6.2 %copy-start.5 = (f32[8192]{0:T(1024)S(1)}, f32[8192]{0:T(1024)}, u32[]{:S(2)}) copy-start(f32[8192]{0:T(1024)} %param.10) | copy-start | bytes 98308
  47.1 3.8 %collective-permute-start.10 = (f32[32,128]{1,0:T(8,128)S(1)}, f32[32,128]{1,0:T(8,128)S(1)}, u32[]{:S(2)}, u32[]{:S(2)}) collective-permute-start(f32[32,128]{1,0:T(8,128)S(1)} %get-tuple-element.30.refs_1_), channel_id=1, source_target_pairs={{0,2},{1,3},{2,0},{3,1},{4,6},{5,7},{6,4},{7,5},{8,10},{9,11},{10,... | collective-permute-start | bytes 49160 | tf_op jit(solution)/shard_map/ppermute | solution.py:24
  47.8 4.0 %collective-permute-start.11 = (f32[32,128]{1,0:T(8,128)S(1)}, f32[32,128]{1,0:T(8,128)S(1)}, u32[]{:S(2)}, u32[]{:S(2)}) collective-permute-start(f32[32,128]{1,0:T(8,128)S(1)} %get-tuple-element.30.refs_1_), channel_id=1, source_target_pairs={{0,4},{1,5},{2,6},{3,7},{4,0},{5,1},{6,2},{7,3},{8,12},{9,13},{10,... | collective-permute-start | bytes 49160 | tf_op jit(solution)/shard_map/ppermute | solution.py:24
  50.0 4.6 %collective-permute-start.12 = (f32[32,128]{1,0:T(8,128)S(1)}, f32[32,128]{1,0:T(8,128)S(1)}, u32[]{:S(2)}, u32[]{:S(2)}) collective-permute-start(f32[32,128]{1,0:T(8,128)S(1)} %get-tuple-element.30.refs_1_), channel_id=1, source_target_pairs={{0,6},{1,7},{2,4},{3,5},{4,2},{5,3},{6,0},{7,1},{8,14},{9,15},{10,... | collective-permute-start | bytes 49160 | tf_op jit(solution)/shard_map/ppermute | solution.py:24
  56.7 4.7 %collective-permute-start.13 = (f32[32,128]{1,0:T(8,128)S(1)}, f32[32,128]{1,0:T(8,128)S(1)}, u32[]{:S(2)}, u32[]{:S(2)}) collective-permute-start(f32[32,128]{1,0:T(8,128)S(1)} %row_pass.1.refs_1_), channel_id=1, source_target_pairs={{0,8},{1,9},{2,10},{3,11},{4,12},{5,13},{6,14},{7,15},{8,0},{9,1},... | collective-permute-start | bytes 49160 | tf_op jit(solution)/shard_map/ppermute | solution.py:24
  58.2 4.3 %collective-permute-start.14 = (f32[32,128]{1,0:T(8,128)S(1)}, f32[32,128]{1,0:T(8,128)S(1)}, u32[]{:S(2)}, u32[]{:S(2)}) collective-permute-start(f32[32,128]{1,0:T(8,128)S(1)} %row_pass.1.refs_1_), channel_id=1, source_target_pairs={{0,9},{1,8},{2,11},{3,10},{4,13},{5,12},{6,15},{7,14},{8,1},{9,0},... | collective-permute-start | bytes 49160 | tf_op jit(solution)/shard_map/ppermute | solution.py:24
  58.2 4.3 %collective-permute-start.15 = (f32[32,128]{1,0:T(8,128)S(1)}, f32[32,128]{1,0:T(8,128)S(1)}, u32[]{:S(2)}, u32[]{:S(2)}) collective-permute-start(f32[32,128]{1,0:T(8,128)S(1)} %row_pass.1.refs_1_), channel_id=1, source_target_pairs={{0,1},{1,0},{2,3},{3,2},{4,5},{5,4},{6,7},{7,6},{8,9},{9,8},{10,11... | collective-permute-start | bytes 49160 | tf_op jit(solution)/shard_map/ppermute | solution.py:24
  64.5 3.9 %collective-permute-start.16 = (f32[32,128]{1,0:T(8,128)S(1)}, f32[32,128]{1,0:T(8,128)S(1)}, u32[]{:S(2)}, u32[]{:S(2)}) collective-permute-start(f32[32,128]{1,0:T(8,128)S(1)} %get-tuple-element.34.refs_0_), channel_id=1, source_target_pairs={{0,2},{1,3},{2,0},{3,1},{4,6},{5,7},{6,4},{7,5},{8,10},{9,11},{10,... | collective-permute-start | bytes 49160 | tf_op jit(solution)/shard_map/ppermute | solution.py:24
  64.6 3.9 %collective-permute-start.17 = (f32[32,128]{1,0:T(8,128)S(1)}, f32[32,128]{1,0:T(8,128)S(1)}, u32[]{:S(2)}, u32[]{:S(2)}) collective-permute-start(f32[32,128]{1,0:T(8,128)S(1)} %get-tuple-element.34.refs_0_), channel_id=1, source_target_pairs={{0,4},{1,5},{2,6},{3,7},{4,0},{5,1},{6,2},{7,3},{8,12},{9,13},{10,... | collective-permute-start | bytes 49160 | tf_op jit(solution)/shard_map/ppermute | solution.py:24
  66.1 4.6 %collective-permute-start.18 = (f32[32,128]{1,0:T(8,128)S(1)}, f32[32,128]{1,0:T(8,128)S(1)}, u32[]{:S(2)}, u32[]{:S(2)}) collective-permute-start(f32[32,128]{1,0:T(8,128)S(1)} %get-tuple-element.34.refs_0_), channel_id=1, source_target_pairs={{0,6},{1,7},{2,4},{3,5},{4,2},{5,3},{6,0},{7,1},{8,14},{9,15},{10,... | collective-permute-start | bytes 49160 | tf_op jit(solution)/shard_map/ppermute | solution.py:24
  70.8 4.9 %collective-permute-start.19 = (f32[32,128]{1,0:T(8,128)S(1)}, f32[32,128]{1,0:T(8,128)S(1)}, u32[]{:S(2)}, u32[]{:S(2)}) collective-permute-start(f32[32,128]{1,0:T(8,128)S(1)} %finish.1), channel_id=1, source_target_pairs={{0,8},{1,9},{2,10},{3,11},{4,12},{5,13},{6,14},{7,15},{8,0},{9,1},... | collective-permute-start | bytes 49160 | tf_op jit(solution)/shard_map/ppermute | solution.py:24

commit v3 on v2

--- a/solution.py
+++ b/solution.py
@@ -27,13 +27,6 @@
 def half_norms(rows):
     wide = rows.astype(jnp.float32)
     return 0.5 * jnp.sum(wide * wide, axis=-1).reshape(-1, TILE)
-
-
-def share_kernel(side, source, share, sems):
-    begin = lax.axis_index("tgt") * side
-    move = pltpu.make_async_copy(source.at[pl.ds(begin, side)], share, sems.at[0])
-    move.start()
-    move.wait()
 
 
 def list_kernel(half, src_rows, own_cols, slots, own, peer, ids):
@@ -267,22 +260,14 @@
     anywhere = pl.BlockSpec(memory_space=pl.ANY)
     params = pltpu.CompilerParams(vmem_limit_bytes=VMEM_LIMIT)
 
-    peer_list = hop(tile_list, half)
-    peer_count = hop(tile_count, half)
-
     def live_list(tiles, count):
         live = lax.broadcasted_iota(jnp.int32, tiles.shape, 3) < count[0, 0]
         return jnp.where(live, tiles, -1)
 
-    share = pl.pallas_call(
-        lambda *refs: share_kernel(side, *refs),
-        out_shape=jax.ShapeDtypeStruct((side, TILE, width), source_embed.dtype),
-        in_specs=[anywhere],
-        out_specs=vmem,
-        scratch_shapes=[pltpu.SemaphoreType.DMA((1,))],
-        compiler_params=params,
-        name="outgoing",
-    )(source_blocks)
+    share = lax.dynamic_slice_in_dim(source_blocks, lax.axis_index("tgt") * side, side)
+    peer_count = hop(tile_count, half)
+    sent_list, share = lax.optimization_barrier((tile_list, share))
+    peer_list = hop(sent_list, half)
     direct = hop(share, half)
     held = {0: target_blocks}
     for slot in range(1, half):

time: 76.8 us -> 77 us (level)
  waiting for transfers between devices: 26.2 us -> 23.1 us
  other arithmetic: 4.05 us -> 5.56 us
  starting transfers between devices: 27.4 us -> 28.7 us
    ppermute x20, waiting for transfers between devices: 26.2 us -> 23.1 us  [hop(): lax.ppermute(value, ('src', 'tgt'), [(i, i ^ flip) for i in range(total)])]
    dynamic_slice x0 -> x1, local copies, waits for them, and re-layouts: none -> 1.87 us  [shards(): lax.dynamic_slice_in_dim(source_blocks, lax.axis_index('tgt') * side, side)]
    ppermute x20, starting transfers between devices: 27.4 us -> 28.7 us  [hop(): lax.ppermute(value, ('src', 'tgt'), [(i, i ^ flip) for i in range(total)])]
    unnamed x14 -> x8, local copies, waits for them, and re-layouts: 1.25 us -> 0.02 us
    pallas_call x1 -> x0, Pallas kernels: 0.84 us -> none  [shards(): pl.pallas_call(lambda *refs: share_kernel(side, *refs), out_shape=jax.Sha...]
  transfers between devices with their start and end apart: 20 -> 20, of which waited for: 13 -> 14; matrix products, arithmetic and copies ran while one was open for 4% -> 9% of each run, Pallas kernels for 9% -> 8%
where the time goes in v3:
time: 77 us; the launch traced here: 76.3 us
  starting transfers between devices  28.7 us (37%)
  waiting for transfers between devices  23.1 us (30%)
  Pallas kernels  15.6 us (20%)
  other arithmetic  5.56 us (7%)
  local copies, waits for them, and re-layouts  1.89 us (2%)
  between operations  1.55 us (2%)
    ppermute x20, starting transfers between devices, hop(): lax.ppermute(value, ('src', 'tgt'), [(i, i ^ flip) for i in range(total)])  28.7 us
    ppermute x20, waiting for transfers between devices, hop(): lax.ppermute(value, ('src', 'tgt'), [(i, i ^ flip) for i in range(total)])  23.1 us
    pallas_call x3, Pallas kernels, run(): pl.pallas_call(lambda *refs: pass_kernel(half, slots, row_pass, len(parts...  7.43 us
    pallas_call x2, Pallas kernels, first(): pl.pallas_call(lambda *refs: first_kernel(scale, half, slots, late, (src_...  4.43 us
    pallas_call x1, Pallas kernels, shards(): pl.pallas_call(lambda *refs: list_kernel(half, src_rows, own_cols, slots,...  3.68 us
    reduce_sum x5, other arithmetic, half_norms(): return 0.5 * jnp.sum(wide * wide, axis=-1).reshape(-1, TILE)  2.23 us
    dynamic_slice x1, local copies, waits for them, and re-layouts, shards(): lax.dynamic_slice_in_dim(source_blocks, lax.axis_index('tgt') * side, side)  1.87 us
  transfers between devices with their start and end apart: 20, of which 14 were waited for; matrix products, arithmetic and copies ran while one was open for 9% of the time, Pallas kernels for 8%

profile of v3, /device:TPU:0, one launch (start us, length us, event | category | flops | bytes accessed | tf_op | source)
XLA Modules:
  0.0 76.3 jit_solution(7200029375123583942)
XLA Ops:
  0.6 0.0 copy-start.1
  0.6 0.0 copy-start
  0.7 3.1 %collective-permute-start.2 = (bf16[8,128,256]{2,1,0:T(8,128)(2,1)}, bf16[8,128,256]{2,1,0:T(8,128)(2,1)S(1)}, u32[]{:S(2)}, u32[]{:S(2)}) collective-permute-start(bf16[8,128,256]{2,1,0:T(8,128)(2,1)} %bitcast.22), channel_id=1, source_target_pairs={{0,4},{1,5},{2,6},{3,7},{4,0},{5,1},{6,2},{7,3},{8,12},{9,13},{10,... | collective-permute-start | bytes 1572872 | tf_op jit(solution)/shard_map/ppermute | solution.py:24
  3.7 1.5 %collective-permute-start.5 = (bf16[8,128,256]{2,1,0:T(8,128)(2,1)}, bf16[8,128,256]{2,1,0:T(8,128)(2,1)S(1)}, u32[]{:S(2)}, u32[]{:S(2)}) collective-permute-start(bf16[8,128,256]{2,1,0:T(8,128)(2,1)} %bitcast.23), channel_id=1, source_target_pairs={{0,2},{1,3},{2,0},{3,1},{4,6},{5,7},{6,4},{7,5},{8,10},{9,11},{10,... | collective-permute-start | bytes 1572872 | tf_op jit(solution)/shard_map/ppermute | solution.py:24
  5.3 1.9 %constant_dynamic-slice_fusion = bf16[8,128,256]{2,1,0:T(8,128)(2,1)} fusion(bf16[16,128,256]{2,1,0:T(8,128)(2,1)} %bitcast.20, s32[]{:T(128)S(6)} %select_n.35), kind=kLoop, calls=%fused_computation.16 | loop fusion | bytes 1048580 | tf_op jit(solution)/shard_map/dynamic_slice | solution.py:267
  7.1 2.6 %collective-permute-start.1 = (s32[1,1,2,128]{3,2,1,0:T(2,128)}, s32[1,1,2,128]{3,2,1,0:T(2,128)S(1)}, u32[]{:S(2)}, u32[]{:S(2)}) collective-permute-start(s32[1,1,2,128]{3,2,1,0:T(2,128)} %param.12), channel_id=1, source_target_pairs={{0,8},{1,9},{2,10},{3,11},{4,12},{5,13},{6,14},{7,15},{8,0},{9,1},... | collective-permute-start | bytes 3080 | tf_op jit(solution)/shard_map/ppermute | solution.py:24
  9.7 0.3 collective-permute-start
  10.1 2.6 %collective-permute-start.4 = (bf16[8,128,256]{2,1,0:T(8,128)(2,1)}, bf16[8,128,256]{2,1,0:T(8,128)(2,1)S(1)}, u32[]{:S(2)}, u32[]{:S(2)}) collective-permute-start(bf16[8,128,256]{2,1,0:T(8,128)(2,1)} %constant_dynamic-slice_fusion), channel_id=1, source_target_pairs={{0,8},{1,9},{2,10},{3,11},{4,12},{5,13},{6,14},{7,15},{8,0},{9,1},... | collective-permute-start | bytes 1572872 | tf_op jit(solution)/shard_map/ppermute | solution.py:24
  13.3 1.3 %multiply_reduce_fusion.3 = f32[1024]{0:T(1024)S(1)} fusion(bf16[1024,256]{1,0:T(8,128)(2,1)} %param.8), kind=kLoop, calls=%fused_computation.3 | loop fusion | flops 785408 | bytes 528384 | tf_op jit(solution)/shard_map/reduce_sum | solution.py:29
  14.6 0.7 dynamic-slice_multiply_fusion.refs_1_
  15.3 0.7 broadcast_select_fusion.1.refs_0_
  16.0 0.4 collective-permute-done
  16.4 0.7 iota_compare_fusion
  17.1 0.0 collective-permute-done.1
  17.1 3.7 %tile_lists.1.refs_0_ = s32[1024]{0:T(1024)S(1)} custom-call(s32[1,1,2,128]{3,2,1,0:T(2,128)S(1)} %broadcast_select_fusion.1.refs_0_, s32[1,1,2,128]{3,2,1,0:T(2,128)S(1)} %broadcast_select_fusion.refs_1_), custom_call_target="tpu_custom_call" | custom-call | tf_op jit(solution)/shard_map/tile_lists/pallas_call | solution.py:277
  20.8 0.0 copy-start.2
  20.8 0.8 collective-permute-done.2.refs_8_
  21.5 2.7 %collective-permute-start.3 = (bf16[8,128,256]{2,1,0:T(8,128)(2,1)S(1)}, bf16[8,128,256]{2,1,0:T(8,128)(2,1)S(1)}, u32[]{:S(2)}, u32[]{:S(2)}) collective-permute-start(bf16[8,128,256]{2,1,0:T(8,128)(2,1)S(1)} %collective-permute-done.2.refs_8_), channel_id=1, source_target_pairs={{0,2},{1,3},{2,0},{3,1},{4,6},{5,7},{6,4},{7,5},{8,10},{9,11},{10,... | collective-permute-start | bytes 1572872 | tf_op jit(solution)/shard_map/ppermute | solution.py:24
  24.2 0.2 multiply_reduce_fusion.1
  24.5 0.0 collective-permute-done.5.refs_7_
  24.5 0.2 multiply_reduce_fusion.2
  24.7 0.0 copy-done.1
  24.7 0.0 copy-done
  24.7 2.3 %early_row_pass.1 = (f32[257,128,128]{2,1,0:T(8,128)S(1)}, bf16[32,128,256]{2,1,0:T(8,128)(2,1)S(1)}, bf16[32,128,256]{2,1,0:T(8,128)(2,1)S(1)}, f32[32,128]{1,0...) custom-call(s32[1024]{0:T(1024)S(1)} %tile_lists.1.refs_0_, ...), custom_call_target="tpu_custom_call" | custom-call | tf_op jit(solution)/shard_map/early_row_pass/pallas_call | solution.py:334
  27.0 8.0 %collective-permute-done.4.refs_3_ = bf16[8,128,256]{2,1,0:T(8,128)(2,1)S(1)} collective-permute-done((bf16[8,128,256]{2,1,0:T(8,128)(2,1)}, bf16[8,128,256]{2,1,0:T(8,128)(2,1)S(1)}, u32[]{:S(2)}, u32[]{:S(2)}) %collective-permute-start.4) | collective-permute-done | bytes 524320 | tf_op jit(solution)/shard_map/ppermute | solution.py:24
  35.0 0.0 collective-permute-start.6
  35.0 0.3 collective-permute-done.3.refs_5_
  35.3 0.2 multiply_reduce_fusion.4
  35.5 1.4 %collective-permute-done.6.refs_4_ = bf16[8,128,256]{2,1,0:T(8,128)(2,1)S(1)} collective-permute-done((bf16[8,128,256]{2,1,0:T(8,128)(2,1)S(1)}, bf16[8,128,256]{2,1,0:T(8,128)(2,1)S(1)}, u32[]{:S(2)}, u32[]{:S(2)}) %collective-permute-start.6) | collective-permute-done | bytes 524320 | tf_op jit(solution)/shard_map/ppermute | solution.py:24
  36.9 0.0 copy-done.2
  36.9 2.1 %late_row_pass.1 = (f32[48,128]{1,0:T(8,128)S(1)}, f32[257,128,128]{2,1,0:T(8,128)S(1)}, bf16[32,128,256]{2,1,0:T(8,128)(2,1)S(1)}, bf16[32,128,256]{2,1,0:T(8,1...) custom-call(s32[1024]{0:T(1024)S(1)} %tile_lists.1.refs_0_, ...), custom_call_target="tpu_custom_call", output_to_operand_aliasing={{1}: (7, {}), {2}: (8, {}), {3}: (9, {}), {4}: (10, {}), {5... | custom-call | tf_op jit(solution)/shard_map/late_row_pass/pallas_call | solution.py:334
  39.1 0.1 collective-permute-start.7
  39.2 2.4 %collective-permute-start.8 = (f32[48,128]{1,0:T(8,128)S(1)}, f32[48,128]{1,0:T(8,128)S(1)}, u32[]{:S(2)}, u32[]{:S(2)}) collective-permute-start(f32[48,128]{1,0:T(8,128)S(1)} %get-tuple-element.32.refs_1_.refs_5_), channel_id=1, source_target_pairs={{0,9},{1,8},{2,11},{3,10},{4,13},{5,12},{6,15},{7,14},{8,1},{9,0},... | collective-permute-start | bytes 73736 | tf_op jit(solution)/shard_map/ppermute | solution.py:24
  41.5 0.7 collective-permute-start.9
  42.2 2.0 %collective-permute-done.7.refs_2_ = f32[48,128]{1,0:T(8,128)S(1)} collective-permute-done((f32[48,128]{1,0:T(8,128)S(1)}, f32[48,128]{1,0:T(8,128)S(1)}, u32[]{:S(2)}, u32[]{:S(2)}) %collective-permute-start.7) | collective-permute-done | bytes 24608 | tf_op jit(solution)/shard_map/ppermute | solution.py:24
  44.2 0.0 collective-permute-done.8.refs_3_
  44.2 0.0 collective-permute-done.9.refs_4_
  44.2 3.0 %column_pass.2 = (f32[32,128]{1,0:T(8,128)S(1)}, f32[257,128,128]{2,1,0:T(8,128)S(1)}, f32[32,128]{1,0:T(8,128)S(1)}) custom-call(s32[1024]{0:T(1024)S(1)} %tile_lists.1.refs_0_, f32[48,128]{1,0:T(8,128)S(1)} %get-tuple-element.32.refs_1_.refs_5_, f32[48,128]{1,0:T(8,128)S(1)} %collective-permute-done.7.refs_2_, ...), custom_call_target="tpu_custom_call" | custom-call | tf_op jit(solution)/shard_map/column_pass/pallas_call | solution.py:364
  47.2 2.2 %collective-permute-start.10 = (f32[32,128]{1,0:T(8,128)S(1)}, f32[32,128]{1,0:T(8,128)S(1)}, u32[]{:S(2)}, u32[]{:S(2)}) collective-permute-start(f32[32,128]{1,0:T(8,128)S(1)} %get-tuple-element.34.refs_1_), channel_id=1, source_target_pairs={{0,2},{1,3},{2,0},{3,1},{4,6},{5,7},{6,4},{7,5},{8,10},{9,11},{10,... | collective-permute-start | bytes 49160 | tf_op jit(solution)/shard_map/ppermute | solution.py:24
  49.5 0.0 collective-permute-start.11
  49.5 1.5 %collective-permute-start.12 = (f32[32,128]{1,0:T(8,128)S(1)}, f32[32,128]{1,0:T(8,128)S(1)}, u32[]{:S(2)}, u32[]{:S(2)}) collective-permute-start(f32[32,128]{1,0:T(8,128)S(1)} %get-tuple-element.34.refs_1_), channel_id=1, source_target_pairs={{0,6},{1,7},{2,4},{3,5},{4,2},{5,3},{6,0},{7,1},{8,14},{9,15},{10,... | collective-permute-start | bytes 49160 | tf_op jit(solution)/shard_map/ppermute | solution.py:24
  51.0 0.0 copy-done.3
  51.0 0.2 collective-permute-done.10.refs_2_
  51.2 2.0 %collective-permute-done.11.refs_3_ = f32[32,128]{1,0:T(8,128)S(1)} collective-permute-done((f32[32,128]{1,0:T(8,128)S(1)}, f32[32,128]{1,0:T(8,128)S(1)}, u32[]{:S(2)}, u32[]{:S(2)}) %collective-permute-start.11) | collective-permute-done | bytes 16416 | tf_op jit(solution)/shard_map/ppermute | solution.py:24
  53.2 0.9 %collective-permute-done.12.refs_4_ = f32[32,128]{1,0:T(8,128)S(1)} collective-permute-done((f32[32,128]{1,0:T(8,128)S(1)}, f32[32,128]{1,0:T(8,128)S(1)}, u32[]{:S(2)}, u32[]{:S(2)}) %collective-permute-start.12) | collective-permute-done | bytes 16416 | tf_op jit(solution)/shard_map/ppermute | solution.py:24
  54.1 2.2 %row_pass.1.refs_1_ = f32[32,128]{1,0:T(8,128)S(1)} custom-call(s32[1024]{0:T(1024)S(1)} %tile_lists.1.refs_0_, f32[32,128]{1,0:T(8,128)S(1)} %get-tuple-element.34.refs_1_, f32[32,128]{1,0:T(8,128)S(1)} %collective-permute-done.10.refs_2_, f32[32,128]{1,0:T(8,128)S(1)} %collective-permute-done.11.refs_3_, f32[32,128]{1,0:T(8,128)S(1)} %collective-permute-done.12.refs_4_, ...), custom_call_target="tpu_custom_call" | custom-call | tf_op jit(solution)/shard_map/row_pass/pallas_call | solution.py:364
  56.3 1.1 %collective-permute-start.13 = (f32[32,128]{1,0:T(8,128)S(1)}, f32[32,128]{1,0:T(8,128)S(1)}, u32[]{:S(2)}, u32[]{:S(2)}) collective-permute-start(f32[32,128]{1,0:T(8,128)S(1)} %row_pass.1.refs_1_), channel_id=1, source_target_pairs={{0,8},{1,9},{2,10},{3,11},{4,12},{5,13},{6,14},{7,15},{8,0},{9,1},... | collective-permute-start | bytes 49160 | tf_op jit(solution)/shard_map/ppermute | solution.py:24
  57.4 0.0 collective-permute-start.14
  57.4 2.0 %collective-permute-start.15 = (f32[32,128]{1,0:T(8,128)S(1)}, f32[32,128]{1,0:T(8,128)S(1)}, u32[]{:S(2)}, u32[]{:S(2)}) collective-permute-start(f32[32,128]{1,0:T(8,128)S(1)} %row_pass.1.refs_1_), channel_id=1, source_target_pairs={{0,1},{1,0},{2,3},{3,2},{4,5},{5,4},{6,7},{7,6},{8,9},{9,8},{10,11... | collective-permute-start | bytes 49160 | tf_op jit(solution)/shard_map/ppermute | solution.py:24
  59.4 1.6 %collective-permute-done.13.refs_2_ = f32[32,128]{1,0:T(8,128)S(1)} collective-permute-done((f32[32,128]{1,0:T(8,128)S(1)}, f32[32,128]{1,0:T(8,128)S(1)}, u32[]{:S(2)}, u32[]{:S(2)}) %collective-permute-start.13) | collective-permute-done | bytes 16416 | tf_op jit(solution)/shard_map/ppermute | solution.py:24
  61.0 0.4 collective-permute-done.14.refs_3_
  61.5 0.0 collective-permute-done.15.refs_4_
  61.5 2.2 %column_pass.3 = (f32[32,128]{1,0:T(8,128)S(1)}, f32[32,128]{1,0:T(8,128)S(1)}) custom-call(s32[1024]{0:T(1024)S(1)} %tile_lists.1.refs_0_, f32[32,128]{1,0:T(8,128)S(1)} %row_pass.1.refs_1_, f32[32,128]{1,0:T(8,128)S(1)} %collective-permute-done.13.refs_2_, f32[32,128]{1,0:T(8,128)S(1)} %collective-permute-done.14.refs_3_, ...), custom_call_target="tpu_custom_call" | custom-call | tf_op jit(solution)/shard_map/column_pass/pallas_call | solution.py:364
  63.7 2.7 %collective-permute-start.16 = (f32[32,128]{1,0:T(8,128)S(1)}, f32[32,128]{1,0:T(8,128)S(1)}, u32[]{:S(2)}, u32[]{:S(2)}) collective-permute-start(f32[32,128]{1,0:T(8,128)S(1)} %get-tuple-element.38.refs_0_), channel_id=1, source_target_pairs={{0,2},{1,3},{2,0},{3,1},{4,6},{5,7},{6,4},{7,5},{8,10},{9,11},{10,... | collective-permute-start | bytes 49160 | tf_op jit(solution)/shard_map/ppermute | solution.py:24
  66.3 0.0 collective-permute-start.17
  66.3 1.5 %collective-permute-start.18 = (f32[32,128]{1,0:T(8,128)S(1)}, f32[32,128]{1,0:T(8,128)S(1)}, u32[]{:S(2)}, u32[]{:S(2)}) collective-permute-start(f32[32,128]{1,0:T(8,128)S(1)} %get-tuple-element.38.refs_0_), channel_id=1, source_target_pairs={{0,6},{1,7},{2,4},{3,5},{4,2},{5,3},{6,0},{7,1},{8,14},{9,15},{10,... | collective-permute-start | bytes 49160 | tf_op jit(solution)/shard_map/ppermute | solution.py:24
  67.9 0.3 multiply_reduce_fusion
  68.2 0.0 collective-permute-done.16.refs_1_
  68.2 1.8 %collective-permute-done.17.refs_2_ = f32[32,128]{1,0:T(8,128)S(1)} collective-permute-done((f32[32,128]{1,0:T(8,128)S(1)}, f32[32,128]{1,0:T(8,128)S(1)}, u32[]{:S(2)}, u32[]{:S(2)}) %collective-permute-start.17) | collective-permute-done | bytes 16416 | tf_op jit(solution)/shard_map/ppermute | solution.py:24
  70.1 0.9 %collective-permute-done.18.refs_3_ = f32[32,128]{1,0:T(8,128)S(1)} collective-permute-done((f32[32,128]{1,0:T(8,128)S(1)}, f32[32,128]{1,0:T(8,128)S(1)}, u32[]{:S(2)}, u32[]{:S(2)}) %collective-permute-start.18) | collective-permute-done | bytes 16416 | tf_op jit(solution)/shard_map/ppermute | solution.py:24
  71.0 1.6 %collective-permute-start.19 = (f32[32,128]{1,0:T(8,128)S(1)}, f32[32,128]{1,0:T(8,128)S(1)}, u32[]{:S(2)}, u32[]{:S(2)}) collective-permute-start(f32[32,128]{1,0:T(8,128)S(1)} %finish.1), channel_id=1, source_target_pairs={{0,8},{1,9},{2,10},{3,11},{4,12},{5,13},{6,14},{7,15},{8,0},{9,1},... | collective-permute-start | bytes 49160 | tf_op jit(solution)/shard_map/ppermute | solution.py:24
  72.7 0.6 fusion.2
  73.3 2.5 %collective-permute-done.19 = f32[32,128]{1,0:T(8,128)S(1)} collective-permute-done((f32[32,128]{1,0:T(8,128)S(1)}, f32[32,128]{1,0:T(8,128)S(1)}, u32[]{:S(2)}, u32[]{:S(2)}) %collective-permute-start.19) | collective-permute-done | bytes 16416 | tf_op jit(solution)/shard_map/ppermute | solution.py:24
  75.7 0.6 fusion
  (9 shorter events, 0.1 us)
Async XLA Ops:
  0.6 24.1 %copy-start.1 = (bf16[1024,256]{1,0:T(8,128)(2,1)S(1)}, bf16[1024,256]{1,0:T(8,128)(2,1)}, u32[]{:S(2)}) copy-start(bf16[1024,256]{1,0:T(8,128)(2,1)} %param.8) | copy-start | bytes 1572868
  0.6 24.1 %copy-start = (bf16[2048,256]{1,0:T(8,128)(2,1)S(1)}, bf16[2048,256]{1,0:T(8,128)(2,1)}, u32[]{:S(2)}) copy-start(bf16[2048,256]{1,0:T(8,128)(2,1)} %param.7) | copy-start | bytes 3145732
  0.7 20.9 %collective-permute-start.2 = (bf16[8,128,256]{2,1,0:T(8,128)(2,1)}, bf16[8,128,256]{2,1,0:T(8,128)(2,1)S(1)}, u32[]{:S(2)}, u32[]{:S(2)}) collective-permute-start(bf16[8,128,256]{2,1,0:T(8,128)(2,1)} %bitcast.22), channel_id=1, source_target_pairs={{0,4},{1,5},{2,6},{3,7},{4,0},{5,1},{6,2},{7,3},{8,12},{9,13},{10,... | collective-permute-start | bytes 1572872 | tf_op jit(solution)/shard_map/ppermute | solution.py:24
  3.7 20.7 %collective-permute-start.5 = (bf16[8,128,256]{2,1,0:T(8,128)(2,1)}, bf16[8,128,256]{2,1,0:T(8,128)(2,1)S(1)}, u32[]{:S(2)}, u32[]{:S(2)}) collective-permute-start(bf16[8,128,256]{2,1,0:T(8,128)(2,1)} %bitcast.23), channel_id=1, source_target_pairs={{0,2},{1,3},{2,0},{3,1},{4,6},{5,7},{6,4},{7,5},{8,10},{9,11},{10,... | collective-permute-start | bytes 1572872 | tf_op jit(solution)/shard_map/ppermute | solution.py:24
  7.1 9.9 %collective-permute-start.1 = (s32[1,1,2,128]{3,2,1,0:T(2,128)}, s32[1,1,2,128]{3,2,1,0:T(2,128)S(1)}, u32[]{:S(2)}, u32[]{:S(2)}) collective-permute-start(s32[1,1,2,128]{3,2,1,0:T(2,128)} %param.12), channel_id=1, source_target_pairs={{0,8},{1,9},{2,10},{3,11},{4,12},{5,13},{6,14},{7,15},{8,0},{9,1},... | collective-permute-start | bytes 3080 | tf_op jit(solution)/shard_map/ppermute | solution.py:24
  9.7 6.7 %collective-permute-start = (s32[1,1]{1,0:T(1,128)}, s32[1,1]{1,0:T(1,128)}, u32[]{:S(2)}, u32[]{:S(2)}) collective-permute-start(s32[1,1]{1,0:T(1,128)} %param.13), channel_id=1, source_target_pairs={{0,8},{1,9},{2,10},{3,11},{4,12},{5,13},{6,14},{7,15},{8,0},{9,1},... | collective-permute-start | bytes 20 | tf_op jit(solution)/shard_map/ppermute | solution.py:24
  10.1 25.0 %collective-permute-start.4 = (bf16[8,128,256]{2,1,0:T(8,128)(2,1)}, bf16[8,128,256]{2,1,0:T(8,128)(2,1)S(1)}, u32[]{:S(2)}, u32[]{:S(2)}) collective-permute-start(bf16[8,128,256]{2,1,0:T(8,128)(2,1)} %constant_dynamic-slice_fusion), channel_id=1, source_target_pairs={{0,8},{1,9},{2,10},{3,11},{4,12},{5,13},{6,14},{7,15},{8,0},{9,1},... | collective-permute-start | bytes 1572872 | tf_op jit(solution)/shard_map/ppermute | solution.py:24
  20.8 16.2 %copy-start.2 = (f32[2048]{0:T(1024)S(1)}, f32[2048]{0:T(1024)}, u32[]{:S(2)}) copy-start(f32[2048]{0:T(1024)} %param.9) | copy-start | bytes 24580
  21.5 13.8 %collective-permute-start.3 = (bf16[8,128,256]{2,1,0:T(8,128)(2,1)S(1)}, bf16[8,128,256]{2,1,0:T(8,128)(2,1)S(1)}, u32[]{:S(2)}, u32[]{:S(2)}) collective-permute-start(bf16[8,128,256]{2,1,0:T(8,128)(2,1)S(1)} %collective-permute-done.2.refs_8_), channel_id=1, source_target_pairs={{0,2},{1,3},{2,0},{3,1},{4,6},{5,7},{6,4},{7,5},{8,10},{9,11},{10,... | collective-permute-start | bytes 1572872 | tf_op jit(solution)/shard_map/ppermute | solution.py:24
  35.0 1.9 %collective-permute-start.6 = (bf16[8,128,256]{2,1,0:T(8,128)(2,1)S(1)}, bf16[8,128,256]{2,1,0:T(8,128)(2,1)S(1)}, u32[]{:S(2)}, u32[]{:S(2)}) collective-permute-start(bf16[8,128,256]{2,1,0:T(8,128)(2,1)S(1)} %collective-permute-done.4.refs_3_), channel_id=1, source_target_pairs={{0,1},{1,0},{2,3},{3,2},{4,5},{5,4},{6,7},{7,6},{8,9},{9,8},{10,11... | collective-permute-start | bytes 1572872 | tf_op jit(solution)/shard_map/ppermute | solution.py:24
  39.1 5.1 %collective-permute-start.7 = (f32[48,128]{1,0:T(8,128)S(1)}, f32[48,128]{1,0:T(8,128)S(1)}, u32[]{:S(2)}, u32[]{:S(2)}) collective-permute-start(f32[48,128]{1,0:T(8,128)S(1)} %get-tuple-element.32.refs_1_.refs_5_), channel_id=1, source_target_pairs={{0,8},{1,9},{2,10},{3,11},{4,12},{5,13},{6,14},{7,15},{8,0},{9,1},... | collective-permute-start | bytes 73736 | tf_op jit(solution)/shard_map/ppermute | solution.py:24
  39.2 5.0 %collective-permute-start.8 = (f32[48,128]{1,0:T(8,128)S(1)}, f32[48,128]{1,0:T(8,128)S(1)}, u32[]{:S(2)}, u32[]{:S(2)}) collective-permute-start(f32[48,128]{1,0:T(8,128)S(1)} %get-tuple-element.32.refs_1_.refs_5_), channel_id=1, source_target_pairs={{0,9},{1,8},{2,11},{3,10},{4,13},{5,12},{6,15},{7,14},{8,1},{9,0},... | collective-permute-start | bytes 73736 | tf_op jit(solution)/shard_map/ppermute | solution.py:24
  41.5 2.6 %collective-permute-start.9 = (f32[48,128]{1,0:T(8,128)S(1)}, f32[48,128]{1,0:T(8,128)S(1)}, u32[]{:S(2)}, u32[]{:S(2)}) collective-permute-start(f32[48,128]{1,0:T(8,128)S(1)} %get-tuple-element.32.refs_1_.refs_5_), channel_id=1, source_target_pairs={{0,1},{1,0},{2,3},{3,2},{4,5},{5,4},{6,7},{7,6},{8,9},{9,8},{10,11... | collective-permute-start | bytes 73736 | tf_op jit(solution)/shard_map/ppermute | solution.py:24
  44.2 6.8 %copy-start.3 = (f32[8192]{0:T(1024)S(1)}, f32[8192]{0:T(1024)}, u32[]{:S(2)}) copy-start(f32[8192]{0:T(1024)} %param.10) | copy-start | bytes 98308
  47.2 4.0 %collective-permute-start.10 = (f32[32,128]{1,0:T(8,128)S(1)}, f32[32,128]{1,0:T(8,128)S(1)}, u32[]{:S(2)}, u32[]{:S(2)}) collective-permute-start(f32[32,128]{1,0:T(8,128)S(1)} %get-tuple-element.34.refs_1_), channel_id=1, source_target_pairs={{0,2},{1,3},{2,0},{3,1},{4,6},{5,7},{6,4},{7,5},{8,10},{9,11},{10,... | collective-permute-start | bytes 49160 | tf_op jit(solution)/shard_map/ppermute | solution.py:24
  49.5 3.7 %collective-permute-start.11 = (f32[32,128]{1,0:T(8,128)S(1)}, f32[32,128]{1,0:T(8,128)S(1)}, u32[]{:S(2)}, u32[]{:S(2)}) collective-permute-start(f32[32,128]{1,0:T(8,128)S(1)} %get-tuple-element.34.refs_1_), channel_id=1, source_target_pairs={{0,4},{1,5},{2,6},{3,7},{4,0},{5,1},{6,2},{7,3},{8,12},{9,13},{10,... | collective-permute-start | bytes 49160 | tf_op jit(solution)/shard_map/ppermute | solution.py:24
  49.5 4.6 %collective-permute-start.12 = (f32[32,128]{1,0:T(8,128)S(1)}, f32[32,128]{1,0:T(8,128)S(1)}, u32[]{:S(2)}, u32[]{:S(2)}) collective-permute-start(f32[32,128]{1,0:T(8,128)S(1)} %get-tuple-element.34.refs_1_), channel_id=1, source_target_pairs={{0,6},{1,7},{2,4},{3,5},{4,2},{5,3},{6,0},{7,1},{8,14},{9,15},{10,... | collective-permute-start | bytes 49160 | tf_op jit(solution)/shard_map/ppermute | solution.py:24
  56.3 4.7 %collective-permute-start.13 = (f32[32,128]{1,0:T(8,128)S(1)}, f32[32,128]{1,0:T(8,128)S(1)}, u32[]{:S(2)}, u32[]{:S(2)}) collective-permute-start(f32[32,128]{1,0:T(8,128)S(1)} %row_pass.1.refs_1_), channel_id=1, source_target_pairs={{0,8},{1,9},{2,10},{3,11},{4,12},{5,13},{6,14},{7,15},{8,0},{9,1},... | collective-permute-start | bytes 49160 | tf_op jit(solution)/shard_map/ppermute | solution.py:24
  57.4 4.1 %collective-permute-start.14 = (f32[32,128]{1,0:T(8,128)S(1)}, f32[32,128]{1,0:T(8,128)S(1)}, u32[]{:S(2)}, u32[]{:S(2)}) collective-permute-start(f32[32,128]{1,0:T(8,128)S(1)} %row_pass.1.refs_1_), channel_id=1, source_target_pairs={{0,9},{1,8},{2,11},{3,10},{4,13},{5,12},{6,15},{7,14},{8,1},{9,0},... | collective-permute-start | bytes 49160 | tf_op jit(solution)/shard_map/ppermute | solution.py:24
  57.4 4.1 %collective-permute-start.15 = (f32[32,128]{1,0:T(8,128)S(1)}, f32[32,128]{1,0:T(8,128)S(1)}, u32[]{:S(2)}, u32[]{:S(2)}) collective-permute-start(f32[32,128]{1,0:T(8,128)S(1)} %row_pass.1.refs_1_), channel_id=1, source_target_pairs={{0,1},{1,0},{2,3},{3,2},{4,5},{5,4},{6,7},{7,6},{8,9},{9,8},{10,11... | collective-permute-start | bytes 49160 | tf_op jit(solution)/shard_map/ppermute | solution.py:24
  63.7 4.6 %collective-permute-start.16 = (f32[32,128]{1,0:T(8,128)S(1)}, f32[32,128]{1,0:T(8,128)S(1)}, u32[]{:S(2)}, u32[]{:S(2)}) collective-permute-start(f32[32,128]{1,0:T(8,128)S(1)} %get-tuple-element.38.refs_0_), channel_id=1, source_target_pairs={{0,2},{1,3},{2,0},{3,1},{4,6},{5,7},{6,4},{7,5},{8,10},{9,11},{10,... | collective-permute-start | bytes 49160 | tf_op jit(solution)/shard_map/ppermute | solution.py:24
  66.3 3.7 %collective-permute-start.17 = (f32[32,128]{1,0:T(8,128)S(1)}, f32[32,128]{1,0:T(8,128)S(1)}, u32[]{:S(2)}, u32[]{:S(2)}) collective-permute-start(f32[32,128]{1,0:T(8,128)S(1)} %get-tuple-element.38.refs_0_), channel_id=1, source_target_pairs={{0,4},{1,5},{2,6},{3,7},{4,0},{5,1},{6,2},{7,3},{8,12},{9,13},{10,... | collective-permute-start | bytes 49160 | tf_op jit(solution)/shard_map/ppermute | solution.py:24
  66.3 4.6 %collective-permute-start.18 = (f32[32,128]{1,0:T(8,128)S(1)}, f32[32,128]{1,0:T(8,128)S(1)}, u32[]{:S(2)}, u32[]{:S(2)}) collective-permute-start(f32[32,128]{1,0:T(8,128)S(1)} %get-tuple-element.38.refs_0_), channel_id=1, source_target_pairs={{0,6},{1,7},{2,4},{3,5},{4,2},{5,3},{6,0},{7,1},{8,14},{9,15},{10,... | collective-permute-start | bytes 49160 | tf_op jit(solution)/shard_map/ppermute | solution.py:24
  71.0 4.7 %collective-permute-start.19 = (f32[32,128]{1,0:T(8,128)S(1)}, f32[32,128]{1,0:T(8,128)S(1)}, u32[]{:S(2)}, u32[]{:S(2)}) collective-permute-start(f32[32,128]{1,0:T(8,128)S(1)} %finish.1), channel_id=1, source_target_pairs={{0,8},{1,9},{2,10},{3,11},{4,12},{5,13},{6,14},{7,15},{8,0},{9,1},... | collective-permute-start | bytes 49160 | tf_op jit(solution)/shard_map/ppermute | solution.py:24

commit v4 on v3

--- a/solution.py
+++ b/solution.py
@@ -375,7 +375,7 @@
         return [part, hop(part, half), hop(part, half, 1), hop(part, 0, 1)]
 
     def share_columns(part):
-        return [part] + [hop(part, mask) for mask in range(1, half)]
+        return [part] + [hop(part, mask) for mask in reversed(range(1, half))]
 
     columns, by_row, log_pair = run(False, share_rows(rows), rows, by_col, True, False)
     rows = run(True, share_columns(columns), log_half, by_col, False, False)[0]

time: 77 us -> 76.5 us (level); the launches traced: 76.3 us -> 76.7 us
  Pallas kernels: 15.6 us -> 13.4 us
  waiting for transfers between devices: 23.1 us -> 24.4 us
  starting transfers between devices: 28.7 us -> 29.9 us
    pallas_call x3, Pallas kernels: 7.43 us -> 5.82 us  [run(): pl.pallas_call(lambda *refs: pass_kernel(half, slots, row_pass, len(parts...]
    ppermute x20, waiting for transfers between devices: 23.1 us -> 24.4 us  [hop(): lax.ppermute(value, ('src', 'tgt'), [(i, i ^ flip) for i in range(total)])]
    ppermute x20, starting transfers between devices: 28.7 us -> 29.9 us  [hop(): lax.ppermute(value, ('src', 'tgt'), [(i, i ^ flip) for i in range(total)])]
  transfers between devices with their start and end apart: 20 -> 20, of which waited for: 14 -> 13; matrix products, arithmetic and copies ran while one was open for 9% -> 9% of each run, Pallas kernels for 8% -> 7%
where the time goes in v4:
time: 76.5 us; the launch traced here: 76.7 us
  starting transfers between devices  29.9 us (39%)
  waiting for transfers between devices  24.4 us (32%)
  Pallas kernels  13.4 us (18%)
  other arithmetic  5.56 us (7%)
  local copies, waits for them, and re-layouts  1.89 us (2%)
  between operations  1.55 us (2%)
    ppermute x20, starting transfers between devices, hop(): lax.ppermute(value, ('src', 'tgt'), [(i, i ^ flip) for i in range(total)])  29.9 us
    ppermute x20, waiting for transfers between devices, hop(): lax.ppermute(value, ('src', 'tgt'), [(i, i ^ flip) for i in range(total)])  24.4 us
    pallas_call x3, Pallas kernels, run(): pl.pallas_call(lambda *refs: pass_kernel(half, slots, row_pass, len(parts...  5.82 us
    pallas_call x2, Pallas kernels, first(): pl.pallas_call(lambda *refs: first_kernel(scale, half, slots, late, (src_...  3.84 us
    pallas_call x1, Pallas kernels, shards(): pl.pallas_call(lambda *refs: list_kernel(half, src_rows, own_cols, slots,...  3.68 us
    reduce_sum x5, other arithmetic, half_norms(): return 0.5 * jnp.sum(wide * wide, axis=-1).reshape(-1, TILE)  2.23 us
    dynamic_slice x1, local copies, waits for them, and re-layouts, shards(): lax.dynamic_slice_in_dim(source_blocks, lax.axis_index('tgt') * side, side)  1.87 us
  transfers between devices with their start and end apart: 20, of which 13 were waited for; matrix products, arithmetic and copies ran while one was open for 9% of the time, Pallas kernels for 7%

profile of v4, /device:TPU:0, one launch (start us, length us, event | category | flops | bytes accessed | tf_op | source)
XLA Modules:
  0.0 76.7 jit_solution(17857630712749332492)
XLA Ops:
  0.6 0.0 copy-start.1
  0.6 0.0 copy-start
  0.7 3.1 %collective-permute-start.2 = (bf16[8,128,256]{2,1,0:T(8,128)(2,1)}, bf16[8,128,256]{2,1,0:T(8,128)(2,1)S(1)}, u32[]{:S(2)}, u32[]{:S(2)}) collective-permute-start(bf16[8,128,256]{2,1,0:T(8,128)(2,1)} %bitcast.22), channel_id=1, source_target_pairs={{0,4},{1,5},{2,6},{3,7},{4,0},{5,1},{6,2},{7,3},{8,12},{9,13},{10,... | collective-permute-start | bytes 1572872 | tf_op jit(solution)/shard_map/ppermute | solution.py:24
  3.7 1.5 %collective-permute-start.5 = (bf16[8,128,256]{2,1,0:T(8,128)(2,1)}, bf16[8,128,256]{2,1,0:T(8,128)(2,1)S(1)}, u32[]{:S(2)}, u32[]{:S(2)}) collective-permute-start(bf16[8,128,256]{2,1,0:T(8,128)(2,1)} %bitcast.23), channel_id=1, source_target_pairs={{0,2},{1,3},{2,0},{3,1},{4,6},{5,7},{6,4},{7,5},{8,10},{9,11},{10,... | collective-permute-start | bytes 1572872 | tf_op jit(solution)/shard_map/ppermute | solution.py:24
  5.3 1.9 %constant_dynamic-slice_fusion = bf16[8,128,256]{2,1,0:T(8,128)(2,1)} fusion(bf16[16,128,256]{2,1,0:T(8,128)(2,1)} %bitcast.20, s32[]{:T(128)S(6)} %select_n.35), kind=kLoop, calls=%fused_computation.16 | loop fusion | bytes 1048580 | tf_op jit(solution)/shard_map/dynamic_slice | solution.py:267
  7.1 2.6 %collective-permute-start.1 = (s32[1,1,2,128]{3,2,1,0:T(2,128)}, s32[1,1,2,128]{3,2,1,0:T(2,128)S(1)}, u32[]{:S(2)}, u32[]{:S(2)}) collective-permute-start(s32[1,1,2,128]{3,2,1,0:T(2,128)} %param.12), channel_id=1, source_target_pairs={{0,8},{1,9},{2,10},{3,11},{4,12},{5,13},{6,14},{7,15},{8,0},{9,1},... | collective-permute-start | bytes 3080 | tf_op jit(solution)/shard_map/ppermute | solution.py:24
  9.7 0.3 collective-permute-start
  10.1 2.6 %collective-permute-start.4 = (bf16[8,128,256]{2,1,0:T(8,128)(2,1)}, bf16[8,128,256]{2,1,0:T(8,128)(2,1)S(1)}, u32[]{:S(2)}, u32[]{:S(2)}) collective-permute-start(bf16[8,128,256]{2,1,0:T(8,128)(2,1)} %constant_dynamic-slice_fusion), channel_id=1, source_target_pairs={{0,8},{1,9},{2,10},{3,11},{4,12},{5,13},{6,14},{7,15},{8,0},{9,1},... | collective-permute-start | bytes 1572872 | tf_op jit(solution)/shard_map/ppermute | solution.py:24
  13.3 1.3 %multiply_reduce_fusion.3 = f32[1024]{0:T(1024)S(1)} fusion(bf16[1024,256]{1,0:T(8,128)(2,1)} %param.8), kind=kLoop, calls=%fused_computation.3 | loop fusion | flops 785408 | bytes 528384 | tf_op jit(solution)/shard_map/reduce_sum | solution.py:29
  14.6 0.7 dynamic-slice_multiply_fusion.refs_1_
  15.3 0.7 broadcast_select_fusion.1.refs_0_
  16.0 0.4 collective-permute-done
  16.4 0.7 iota_compare_fusion
  17.1 0.0 collective-permute-done.1
  17.1 3.7 %tile_lists.1.refs_0_ = s32[1024]{0:T(1024)S(1)} custom-call(s32[1,1,2,128]{3,2,1,0:T(2,128)S(1)} %broadcast_select_fusion.1.refs_0_, s32[1,1,2,128]{3,2,1,0:T(2,128)S(1)} %broadcast_select_fusion.refs_1_), custom_call_target="tpu_custom_call" | custom-call | tf_op jit(solution)/shard_map/tile_lists/pallas_call | solution.py:277
  20.8 0.0 copy-start.2
  20.8 0.8 collective-permute-done.2.refs_8_
  21.5 2.7 %collective-permute-start.3 = (bf16[8,128,256]{2,1,0:T(8,128)(2,1)S(1)}, bf16[8,128,256]{2,1,0:T(8,128)(2,1)S(1)}, u32[]{:S(2)}, u32[]{:S(2)}) collective-permute-start(bf16[8,128,256]{2,1,0:T(8,128)(2,1)S(1)} %collective-permute-done.2.refs_8_), channel_id=1, source_target_pairs={{0,2},{1,3},{2,0},{3,1},{4,6},{5,7},{6,4},{7,5},{8,10},{9,11},{10,... | collective-permute-start | bytes 1572872 | tf_op jit(solution)/shard_map/ppermute | solution.py:24
  24.2 0.2 multiply_reduce_fusion.1
  24.5 0.0 collective-permute-done.5.refs_7_
  24.5 0.2 multiply_reduce_fusion.2
  24.7 0.0 copy-done.1
  24.7 0.0 copy-done
  24.7 1.7 %early_row_pass.1 = (f32[257,128,128]{2,1,0:T(8,128)S(1)}, bf16[32,128,256]{2,1,0:T(8,128)(2,1)S(1)}, bf16[32,128,256]{2,1,0:T(8,128)(2,1)S(1)}, f32[32,128]{1,0...) custom-call(s32[1024]{0:T(1024)S(1)} %tile_lists.1.refs_0_, ...), custom_call_target="tpu_custom_call" | custom-call | tf_op jit(solution)/shard_map/early_row_pass/pallas_call | solution.py:334
  26.4 8.6 %collective-permute-done.4.refs_3_ = bf16[8,128,256]{2,1,0:T(8,128)(2,1)S(1)} collective-permute-done((bf16[8,128,256]{2,1,0:T(8,128)(2,1)}, bf16[8,128,256]{2,1,0:T(8,128)(2,1)S(1)}, u32[]{:S(2)}, u32[]{:S(2)}) %collective-permute-start.4) | collective-permute-done | bytes 524320 | tf_op jit(solution)/shard_map/ppermute | solution.py:24
  35.0 0.0 collective-permute-start.6
  35.0 0.3 collective-permute-done.3.refs_5_
  35.3 0.2 multiply_reduce_fusion.4
  35.5 1.4 %collective-permute-done.6.refs_4_ = bf16[8,128,256]{2,1,0:T(8,128)(2,1)S(1)} collective-permute-done((bf16[8,128,256]{2,1,0:T(8,128)(2,1)S(1)}, bf16[8,128,256]{2,1,0:T(8,128)(2,1)S(1)}, u32[]{:S(2)}, u32[]{:S(2)}) %collective-permute-start.6) | collective-permute-done | bytes 524320 | tf_op jit(solution)/shard_map/ppermute | solution.py:24
  36.9 0.0 copy-done.2
  36.9 2.2 %late_row_pass.1 = (f32[48,128]{1,0:T(8,128)S(1)}, f32[257,128,128]{2,1,0:T(8,128)S(1)}, bf16[32,128,256]{2,1,0:T(8,128)(2,1)S(1)}, bf16[32,128,256]{2,1,0:T(8,1...) custom-call(s32[1024]{0:T(1024)S(1)} %tile_lists.1.refs_0_, ...), custom_call_target="tpu_custom_call", output_to_operand_aliasing={{1}: (7, {}), {2}: (8, {}), {3}: (9, {}), {4}: (10, {}), {5... | custom-call | tf_op jit(solution)/shard_map/late_row_pass/pallas_call | solution.py:334
  39.1 0.1 collective-permute-start.7
  39.2 2.3 %collective-permute-start.8 = (f32[48,128]{1,0:T(8,128)S(1)}, f32[48,128]{1,0:T(8,128)S(1)}, u32[]{:S(2)}, u32[]{:S(2)}) collective-permute-start(f32[48,128]{1,0:T(8,128)S(1)} %get-tuple-element.32.refs_1_.refs_5_), channel_id=1, source_target_pairs={{0,9},{1,8},{2,11},{3,10},{4,13},{5,12},{6,15},{7,14},{8,1},{9,0},... | collective-permute-start | bytes 73736 | tf_op jit(solution)/shard_map/ppermute | solution.py:24
  41.5 0.7 collective-permute-start.9
  42.2 2.0 %collective-permute-done.7.refs_2_ = f32[48,128]{1,0:T(8,128)S(1)} collective-permute-done((f32[48,128]{1,0:T(8,128)S(1)}, f32[48,128]{1,0:T(8,128)S(1)}, u32[]{:S(2)}, u32[]{:S(2)}) %collective-permute-start.7) | collective-permute-done | bytes 24608 | tf_op jit(solution)/shard_map/ppermute | solution.py:24
  44.2 0.0 collective-permute-done.8.refs_3_
  44.2 0.0 collective-permute-done.9.refs_4_
  44.2 2.2 %column_pass.2 = (f32[32,128]{1,0:T(8,128)S(1)}, f32[257,128,128]{2,1,0:T(8,128)S(1)}, f32[32,128]{1,0:T(8,128)S(1)}) custom-call(s32[1024]{0:T(1024)S(1)} %tile_lists.1.refs_0_, f32[48,128]{1,0:T(8,128)S(1)} %get-tuple-element.32.refs_1_.refs_5_, f32[48,128]{1,0:T(8,128)S(1)} %collective-permute-done.7.refs_2_, ...), custom_call_target="tpu_custom_call" | custom-call | tf_op jit(solution)/shard_map/column_pass/pallas_call | solution.py:364
  46.5 2.1 %collective-permute-start.10 = (f32[32,128]{1,0:T(8,128)S(1)}, f32[32,128]{1,0:T(8,128)S(1)}, u32[]{:S(2)}, u32[]{:S(2)}) collective-permute-start(f32[32,128]{1,0:T(8,128)S(1)} %get-tuple-element.34.refs_1_), channel_id=1, source_target_pairs={{0,6},{1,7},{2,4},{3,5},{4,2},{5,3},{6,0},{7,1},{8,14},{9,15},{10,... | collective-permute-start | bytes 49160 | tf_op jit(solution)/shard_map/ppermute | solution.py:24
  48.5 3.1 %collective-permute-start.11 = (f32[32,128]{1,0:T(8,128)S(1)}, f32[32,128]{1,0:T(8,128)S(1)}, u32[]{:S(2)}, u32[]{:S(2)}) collective-permute-start(f32[32,128]{1,0:T(8,128)S(1)} %get-tuple-element.34.refs_1_), channel_id=1, source_target_pairs={{0,4},{1,5},{2,6},{3,7},{4,0},{5,1},{6,2},{7,3},{8,12},{9,13},{10,... | collective-permute-start | bytes 49160 | tf_op jit(solution)/shard_map/ppermute | solution.py:24
  51.6 0.0 collective-permute-start.12
  51.6 0.0 copy-done.3
  51.6 0.0 collective-permute-done.10.refs_2_
  51.6 1.9 %collective-permute-done.11.refs_3_ = f32[32,128]{1,0:T(8,128)S(1)} collective-permute-done((f32[32,128]{1,0:T(8,128)S(1)}, f32[32,128]{1,0:T(8,128)S(1)}, u32[]{:S(2)}, u32[]{:S(2)}) %collective-permute-start.11) | collective-permute-done | bytes 16416 | tf_op jit(solution)/shard_map/ppermute | solution.py:24
  53.5 1.9 %collective-permute-done.12.refs_4_ = f32[32,128]{1,0:T(8,128)S(1)} collective-permute-done((f32[32,128]{1,0:T(8,128)S(1)}, f32[32,128]{1,0:T(8,128)S(1)}, u32[]{:S(2)}, u32[]{:S(2)}) %collective-permute-start.12) | collective-permute-done | bytes 16416 | tf_op jit(solution)/shard_map/ppermute | solution.py:24
  55.3 1.8 %row_pass.1.refs_1_ = f32[32,128]{1,0:T(8,128)S(1)} custom-call(s32[1024]{0:T(1024)S(1)} %tile_lists.1.refs_0_, f32[32,128]{1,0:T(8,128)S(1)} %get-tuple-element.34.refs_1_, f32[32,128]{1,0:T(8,128)S(1)} %collective-permute-done.10.refs_2_, f32[32,128]{1,0:T(8,128)S(1)} %collective-permute-done.11.refs_3_, f32[32,128]{1,0:T(8,128)S(1)} %collective-permute-done.12.refs_4_, ...), custom_call_target="tpu_custom_call" | custom-call | tf_op jit(solution)/shard_map/row_pass/pallas_call | solution.py:364
  57.1 0.4 collective-permute-start.13
  57.6 0.0 collective-permute-start.14
  57.6 2.7 %collective-permute-start.15 = (f32[32,128]{1,0:T(8,128)S(1)}, f32[32,128]{1,0:T(8,128)S(1)}, u32[]{:S(2)}, u32[]{:S(2)}) collective-permute-start(f32[32,128]{1,0:T(8,128)S(1)} %row_pass.1.refs_1_), channel_id=1, source_target_pairs={{0,1},{1,0},{2,3},{3,2},{4,5},{5,4},{6,7},{7,6},{8,9},{9,8},{10,11... | collective-permute-start | bytes 49160 | tf_op jit(solution)/shard_map/ppermute | solution.py:24
  60.3 1.6 %collective-permute-done.13.refs_2_ = f32[32,128]{1,0:T(8,128)S(1)} collective-permute-done((f32[32,128]{1,0:T(8,128)S(1)}, f32[32,128]{1,0:T(8,128)S(1)}, u32[]{:S(2)}, u32[]{:S(2)}) %collective-permute-start.13) | collective-permute-done | bytes 16416 | tf_op jit(solution)/shard_map/ppermute | solution.py:24
  61.9 0.0 collective-permute-done.14.refs_3_
  61.9 0.0 collective-permute-done.15.refs_4_
  61.9 1.8 %column_pass.3 = (f32[32,128]{1,0:T(8,128)S(1)}, f32[32,128]{1,0:T(8,128)S(1)}) custom-call(s32[1024]{0:T(1024)S(1)} %tile_lists.1.refs_0_, f32[32,128]{1,0:T(8,128)S(1)} %row_pass.1.refs_1_, f32[32,128]{1,0:T(8,128)S(1)} %collective-permute-done.13.refs_2_, f32[32,128]{1,0:T(8,128)S(1)} %collective-permute-done.14.refs_3_, ...), custom_call_target="tpu_custom_call" | custom-call | tf_op jit(solution)/shard_map/column_pass/pallas_call | solution.py:364
  63.7 1.2 %collective-permute-start.16 = (f32[32,128]{1,0:T(8,128)S(1)}, f32[32,128]{1,0:T(8,128)S(1)}, u32[]{:S(2)}, u32[]{:S(2)}) collective-permute-start(f32[32,128]{1,0:T(8,128)S(1)} %get-tuple-element.38.refs_0_), channel_id=1, source_target_pairs={{0,6},{1,7},{2,4},{3,5},{4,2},{5,3},{6,0},{7,1},{8,14},{9,15},{10,... | collective-permute-start | bytes 49160 | tf_op jit(solution)/shard_map/ppermute | solution.py:24
  64.9 2.7 %collective-permute-start.17 = (f32[32,128]{1,0:T(8,128)S(1)}, f32[32,128]{1,0:T(8,128)S(1)}, u32[]{:S(2)}, u32[]{:S(2)}) collective-permute-start(f32[32,128]{1,0:T(8,128)S(1)} %get-tuple-element.38.refs_0_), channel_id=1, source_target_pairs={{0,4},{1,5},{2,6},{3,7},{4,0},{5,1},{6,2},{7,3},{8,12},{9,13},{10,... | collective-permute-start | bytes 49160 | tf_op jit(solution)/shard_map/ppermute | solution.py:24
  67.6 0.0 collective-permute-start.18
  67.6 0.3 multiply_reduce_fusion
  68.0 0.4 collective-permute-done.16.refs_1_
  68.4 1.2 %collective-permute-done.17.refs_2_ = f32[32,128]{1,0:T(8,128)S(1)} collective-permute-done((f32[32,128]{1,0:T(8,128)S(1)}, f32[32,128]{1,0:T(8,128)S(1)}, u32[]{:S(2)}, u32[]{:S(2)}) %collective-permute-start.17) | collective-permute-done | bytes 16416 | tf_op jit(solution)/shard_map/ppermute | solution.py:24
  69.5 1.9 %collective-permute-done.18.refs_3_ = f32[32,128]{1,0:T(8,128)S(1)} collective-permute-done((f32[32,128]{1,0:T(8,128)S(1)}, f32[32,128]{1,0:T(8,128)S(1)}, u32[]{:S(2)}, u32[]{:S(2)}) %collective-permute-start.18) | collective-permute-done | bytes 16416 | tf_op jit(solution)/shard_map/ppermute | solution.py:24
  71.4 1.7 %collective-permute-start.19 = (f32[32,128]{1,0:T(8,128)S(1)}, f32[32,128]{1,0:T(8,128)S(1)}, u32[]{:S(2)}, u32[]{:S(2)}) collective-permute-start(f32[32,128]{1,0:T(8,128)S(1)} %finish.1), channel_id=1, source_target_pairs={{0,8},{1,9},{2,10},{3,11},{4,12},{5,13},{6,14},{7,15},{8,0},{9,1},... | collective-permute-start | bytes 49160 | tf_op jit(solution)/shard_map/ppermute | solution.py:24
  73.1 0.6 fusion.2
  73.7 2.4 %collective-permute-done.19 = f32[32,128]{1,0:T(8,128)S(1)} collective-permute-done((f32[32,128]{1,0:T(8,128)S(1)}, f32[32,128]{1,0:T(8,128)S(1)}, u32[]{:S(2)}, u32[]{:S(2)}) %collective-permute-start.19) | collective-permute-done | bytes 16416 | tf_op jit(solution)/shard_map/ppermute | solution.py:24
  76.1 0.6 fusion
  (9 shorter events, 0.1 us)
Async XLA Ops:
  0.6 24.1 %copy-start.1 = (bf16[1024,256]{1,0:T(8,128)(2,1)S(1)}, bf16[1024,256]{1,0:T(8,128)(2,1)}, u32[]{:S(2)}) copy-start(bf16[1024,256]{1,0:T(8,128)(2,1)} %param.8) | copy-start | bytes 1572868
  0.6 24.1 %copy-start = (bf16[2048,256]{1,0:T(8,128)(2,1)S(1)}, bf16[2048,256]{1,0:T(8,128)(2,1)}, u32[]{:S(2)}) copy-start(bf16[2048,256]{1,0:T(8,128)(2,1)} %param.7) | copy-start | bytes 3145732
  0.7 20.9 %collective-permute-start.2 = (bf16[8,128,256]{2,1,0:T(8,128)(2,1)}, bf16[8,128,256]{2,1,0:T(8,128)(2,1)S(1)}, u32[]{:S(2)}, u32[]{:S(2)}) collective-permute-start(bf16[8,128,256]{2,1,0:T(8,128)(2,1)} %bitcast.22), channel_id=1, source_target_pairs={{0,4},{1,5},{2,6},{3,7},{4,0},{5,1},{6,2},{7,3},{8,12},{9,13},{10,... | collective-permute-start | bytes 1572872 | tf_op jit(solution)/shard_map/ppermute | solution.py:24
  3.7 20.7 %collective-permute-start.5 = (bf16[8,128,256]{2,1,0:T(8,128)(2,1)}, bf16[8,128,256]{2,1,0:T(8,128)(2,1)S(1)}, u32[]{:S(2)}, u32[]{:S(2)}) collective-permute-start(bf16[8,128,256]{2,1,0:T(8,128)(2,1)} %bitcast.23), channel_id=1, source_target_pairs={{0,2},{1,3},{2,0},{3,1},{4,6},{5,7},{6,4},{7,5},{8,10},{9,11},{10,... | collective-permute-start | bytes 1572872 | tf_op jit(solution)/shard_map/ppermute | solution.py:24
  7.1 9.9 %collective-permute-start.1 = (s32[1,1,2,128]{3,2,1,0:T(2,128)}, s32[1,1,2,128]{3,2,1,0:T(2,128)S(1)}, u32[]{:S(2)}, u32[]{:S(2)}) collective-permute-start(s32[1,1,2,128]{3,2,1,0:T(2,128)} %param.12), channel_id=1, source_target_pairs={{0,8},{1,9},{2,10},{3,11},{4,12},{5,13},{6,14},{7,15},{8,0},{9,1},... | collective-permute-start | bytes 3080 | tf_op jit(solution)/shard_map/ppermute | solution.py:24
  9.7 6.7 %collective-permute-start = (s32[1,1]{1,0:T(1,128)}, s32[1,1]{1,0:T(1,128)}, u32[]{:S(2)}, u32[]{:S(2)}) collective-permute-start(s32[1,1]{1,0:T(1,128)} %param.13), channel_id=1, source_target_pairs={{0,8},{1,9},{2,10},{3,11},{4,12},{5,13},{6,14},{7,15},{8,0},{9,1},... | collective-permute-start | bytes 20 | tf_op jit(solution)/shard_map/ppermute | solution.py:24
  10.1 25.0 %collective-permute-start.4 = (bf16[8,128,256]{2,1,0:T(8,128)(2,1)}, bf16[8,128,256]{2,1,0:T(8,128)(2,1)S(1)}, u32[]{:S(2)}, u32[]{:S(2)}) collective-permute-start(bf16[8,128,256]{2,1,0:T(8,128)(2,1)} %constant_dynamic-slice_fusion), channel_id=1, source_target_pairs={{0,8},{1,9},{2,10},{3,11},{4,12},{5,13},{6,14},{7,15},{8,0},{9,1},... | collective-permute-start | bytes 1572872 | tf_op jit(solution)/shard_map/ppermute | solution.py:24
  20.8 16.2 %copy-start.2 = (f32[2048]{0:T(1024)S(1)}, f32[2048]{0:T(1024)}, u32[]{:S(2)}) copy-start(f32[2048]{0:T(1024)} %param.9) | copy-start | bytes 24580
  21.5 13.8 %collective-permute-start.3 = (bf16[8,128,256]{2,1,0:T(8,128)(2,1)S(1)}, bf16[8,128,256]{2,1,0:T(8,128)(2,1)S(1)}, u32[]{:S(2)}, u32[]{:S(2)}) collective-permute-start(bf16[8,128,256]{2,1,0:T(8,128)(2,1)S(1)} %collective-permute-done.2.refs_8_), channel_id=1, source_target_pairs={{0,2},{1,3},{2,0},{3,1},{4,6},{5,7},{6,4},{7,5},{8,10},{9,11},{10,... | collective-permute-start | bytes 1572872 | tf_op jit(solution)/shard_map/ppermute | solution.py:24
  35.0 1.9 %collective-permute-start.6 = (bf16[8,128,256]{2,1,0:T(8,128)(2,1)S(1)}, bf16[8,128,256]{2,1,0:T(8,128)(2,1)S(1)}, u32[]{:S(2)}, u32[]{:S(2)}) collective-permute-start(bf16[8,128,256]{2,1,0:T(8,128)(2,1)S(1)} %collective-permute-done.4.refs_3_), channel_id=1, source_target_pairs={{0,1},{1,0},{2,3},{3,2},{4,5},{5,4},{6,7},{7,6},{8,9},{9,8},{10,11... | collective-permute-start | bytes 1572872 | tf_op jit(solution)/shard_map/ppermute | solution.py:24
  39.1 5.1 %collective-permute-start.7 = (f32[48,128]{1,0:T(8,128)S(1)}, f32[48,128]{1,0:T(8,128)S(1)}, u32[]{:S(2)}, u32[]{:S(2)}) collective-permute-start(f32[48,128]{1,0:T(8,128)S(1)} %get-tuple-element.32.refs_1_.refs_5_), channel_id=1, source_target_pairs={{0,8},{1,9},{2,10},{3,11},{4,12},{5,13},{6,14},{7,15},{8,0},{9,1},... | collective-permute-start | bytes 73736 | tf_op jit(solution)/shard_map/ppermute | solution.py:24
  39.2 5.0 %collective-permute-start.8 = (f32[48,128]{1,0:T(8,128)S(1)}, f32[48,128]{1,0:T(8,128)S(1)}, u32[]{:S(2)}, u32[]{:S(2)}) collective-permute-start(f32[48,128]{1,0:T(8,128)S(1)} %get-tuple-element.32.refs_1_.refs_5_), channel_id=1, source_target_pairs={{0,9},{1,8},{2,11},{3,10},{4,13},{5,12},{6,15},{7,14},{8,1},{9,0},... | collective-permute-start | bytes 73736 | tf_op jit(solution)/shard_map/ppermute | solution.py:24
  41.5 2.7 %collective-permute-start.9 = (f32[48,128]{1,0:T(8,128)S(1)}, f32[48,128]{1,0:T(8,128)S(1)}, u32[]{:S(2)}, u32[]{:S(2)}) collective-permute-start(f32[48,128]{1,0:T(8,128)S(1)} %get-tuple-element.32.refs_1_.refs_5_), channel_id=1, source_target_pairs={{0,1},{1,0},{2,3},{3,2},{4,5},{5,4},{6,7},{7,6},{8,9},{9,8},{10,11... | collective-permute-start | bytes 73736 | tf_op jit(solution)/shard_map/ppermute | solution.py:24
  44.2 7.4 %copy-start.3 = (f32[8192]{0:T(1024)S(1)}, f32[8192]{0:T(1024)}, u32[]{:S(2)}) copy-start(f32[8192]{0:T(1024)} %param.10) | copy-start | bytes 98308
  46.5 5.2 %collective-permute-start.10 = (f32[32,128]{1,0:T(8,128)S(1)}, f32[32,128]{1,0:T(8,128)S(1)}, u32[]{:S(2)}, u32[]{:S(2)}) collective-permute-start(f32[32,128]{1,0:T(8,128)S(1)} %get-tuple-element.34.refs_1_), channel_id=1, source_target_pairs={{0,6},{1,7},{2,4},{3,5},{4,2},{5,3},{6,0},{7,1},{8,14},{9,15},{10,... | collective-permute-start | bytes 49160 | tf_op jit(solution)/shard_map/ppermute | solution.py:24
  48.5 5.0 %collective-permute-start.11 = (f32[32,128]{1,0:T(8,128)S(1)}, f32[32,128]{1,0:T(8,128)S(1)}, u32[]{:S(2)}, u32[]{:S(2)}) collective-permute-start(f32[32,128]{1,0:T(8,128)S(1)} %get-tuple-element.34.refs_1_), channel_id=1, source_target_pairs={{0,4},{1,5},{2,6},{3,7},{4,0},{5,1},{6,2},{7,3},{8,12},{9,13},{10,... | collective-permute-start | bytes 49160 | tf_op jit(solution)/shard_map/ppermute | solution.py:24
  51.6 3.7 %collective-permute-start.12 = (f32[32,128]{1,0:T(8,128)S(1)}, f32[32,128]{1,0:T(8,128)S(1)}, u32[]{:S(2)}, u32[]{:S(2)}) collective-permute-start(f32[32,128]{1,0:T(8,128)S(1)} %get-tuple-element.34.refs_1_), channel_id=1, source_target_pairs={{0,2},{1,3},{2,0},{3,1},{4,6},{5,7},{6,4},{7,5},{8,10},{9,11},{10,... | collective-permute-start | bytes 49160 | tf_op jit(solution)/shard_map/ppermute | solution.py:24
  57.1 4.7 %collective-permute-start.13 = (f32[32,128]{1,0:T(8,128)S(1)}, f32[32,128]{1,0:T(8,128)S(1)}, u32[]{:S(2)}, u32[]{:S(2)}) collective-permute-start(f32[32,128]{1,0:T(8,128)S(1)} %row_pass.1.refs_1_), channel_id=1, source_target_pairs={{0,8},{1,9},{2,10},{3,11},{4,12},{5,13},{6,14},{7,15},{8,0},{9,1},... | collective-permute-start | bytes 49160 | tf_op jit(solution)/shard_map/ppermute | solution.py:24
  57.6 4.3 %collective-permute-start.14 = (f32[32,128]{1,0:T(8,128)S(1)}, f32[32,128]{1,0:T(8,128)S(1)}, u32[]{:S(2)}, u32[]{:S(2)}) collective-permute-start(f32[32,128]{1,0:T(8,128)S(1)} %row_pass.1.refs_1_), channel_id=1, source_target_pairs={{0,9},{1,8},{2,11},{3,10},{4,13},{5,12},{6,15},{7,14},{8,1},{9,0},... | collective-permute-start | bytes 49160 | tf_op jit(solution)/shard_map/ppermute | solution.py:24
  57.6 4.3 %collective-permute-start.15 = (f32[32,128]{1,0:T(8,128)S(1)}, f32[32,128]{1,0:T(8,128)S(1)}, u32[]{:S(2)}, u32[]{:S(2)}) collective-permute-start(f32[32,128]{1,0:T(8,128)S(1)} %row_pass.1.refs_1_), channel_id=1, source_target_pairs={{0,1},{1,0},{2,3},{3,2},{4,5},{5,4},{6,7},{7,6},{8,9},{9,8},{10,11... | collective-permute-start | bytes 49160 | tf_op jit(solution)/shard_map/ppermute | solution.py:24
  63.7 4.7 %collective-permute-start.16 = (f32[32,128]{1,0:T(8,128)S(1)}, f32[32,128]{1,0:T(8,128)S(1)}, u32[]{:S(2)}, u32[]{:S(2)}) collective-permute-start(f32[32,128]{1,0:T(8,128)S(1)} %get-tuple-element.38.refs_0_), channel_id=1, source_target_pairs={{0,6},{1,7},{2,4},{3,5},{4,2},{5,3},{6,0},{7,1},{8,14},{9,15},{10,... | collective-permute-start | bytes 49160 | tf_op jit(solution)/shard_map/ppermute | solution.py:24
  64.9 4.6 %collective-permute-start.17 = (f32[32,128]{1,0:T(8,128)S(1)}, f32[32,128]{1,0:T(8,128)S(1)}, u32[]{:S(2)}, u32[]{:S(2)}) collective-permute-start(f32[32,128]{1,0:T(8,128)S(1)} %get-tuple-element.38.refs_0_), channel_id=1, source_target_pairs={{0,4},{1,5},{2,6},{3,7},{4,0},{5,1},{6,2},{7,3},{8,12},{9,13},{10,... | collective-permute-start | bytes 49160 | tf_op jit(solution)/shard_map/ppermute | solution.py:24
  67.6 3.7 %collective-permute-start.18 = (f32[32,128]{1,0:T(8,128)S(1)}, f32[32,128]{1,0:T(8,128)S(1)}, u32[]{:S(2)}, u32[]{:S(2)}) collective-permute-start(f32[32,128]{1,0:T(8,128)S(1)} %get-tuple-element.38.refs_0_), channel_id=1, source_target_pairs={{0,2},{1,3},{2,0},{3,1},{4,6},{5,7},{6,4},{7,5},{8,10},{9,11},{10,... | collective-permute-start | bytes 49160 | tf_op jit(solution)/shard_map/ppermute | solution.py:24
  71.4 4.7 %collective-permute-start.19 = (f32[32,128]{1,0:T(8,128)S(1)}, f32[32,128]{1,0:T(8,128)S(1)}, u32[]{:S(2)}, u32[]{:S(2)}) collective-permute-start(f32[32,128]{1,0:T(8,128)S(1)} %finish.1), channel_id=1, source_target_pairs={{0,8},{1,9},{2,10},{3,11},{4,12},{5,13},{6,14},{7,15},{8,0},{9,1},... | collective-permute-start | bytes 49160 | tf_op jit(solution)/shard_map/ppermute | solution.py:24

commit v5 on v4

--- a/solution.py
+++ b/solution.py
@@ -12,8 +12,8 @@
 FLOOR = -1e30
 MAKE_UNROLL = 20
 READ_UNROLL = 8
-TURN_UNROLL = 16
-PADDING = max(MAKE_UNROLL, READ_UNROLL)
+TURN_UNROLL = 20
+PADDING = max(MAKE_UNROLL, READ_UNROLL, TURN_UNROLL)
 VMEM_LIMIT = 3 * 1024 * 1024
 
 

time: 76.5 us -> 76 us (level)
  Pallas kernels: 13.4 us -> 15.3 us
  starting transfers between devices: 29.9 us -> 28.3 us
  waiting for transfers between devices: 24.4 us -> 23.2 us
    ppermute x20, starting transfers between devices: 29.9 us -> 28.3 us  [hop(): lax.ppermute(value, ('src', 'tgt'), [(i, i ^ flip) for i in range(total)])]
    pallas_call x3, Pallas kernels: 5.82 us -> 7.12 us  [run(): pl.pallas_call(lambda *refs: pass_kernel(half, slots, row_pass, len(parts...]
    ppermute x20, waiting for transfers between devices: 24.4 us -> 23.2 us  [hop(): lax.ppermute(value, ('src', 'tgt'), [(i, i ^ flip) for i in range(total)])]
  transfers between devices with their start and end apart: 20 -> 20, of which waited for: 13 -> 13; matrix products, arithmetic and copies ran while one was open for 9% -> 9% of each run, Pallas kernels for 7% -> 8%
where the time goes in v5:
time: 76 us; the launch traced here: 75.7 us
  starting transfers between devices  28.3 us (37%)
  waiting for transfers between devices  23.2 us (31%)
  Pallas kernels  15.3 us (20%)
  other arithmetic  5.56 us (7%)
  local copies, waits for them, and re-layouts  1.89 us (2%)
  between operations  1.54 us (2%)
    ppermute x20, starting transfers between devices, hop(): lax.ppermute(value, ('src', 'tgt'), [(i, i ^ flip) for i in range(total)])  28.3 us
    ppermute x20, waiting for transfers between devices, hop(): lax.ppermute(value, ('src', 'tgt'), [(i, i ^ flip) for i in range(total)])  23.2 us
    pallas_call x3, Pallas kernels, run(): pl.pallas_call(lambda *refs: pass_kernel(half, slots, row_pass, len(parts...  7.12 us
    pallas_call x2, Pallas kernels, first(): pl.pallas_call(lambda *refs: first_kernel(scale, half, slots, late, (src_...  4.45 us
    pallas_call x1, Pallas kernels, shards(): pl.pallas_call(lambda *refs: list_kernel(half, src_rows, own_cols, slots,...  3.68 us
    reduce_sum x5, other arithmetic, half_norms(): return 0.5 * jnp.sum(wide * wide, axis=-1).reshape(-1, TILE)  2.23 us
    dynamic_slice x1, local copies, waits for them, and re-layouts, shards(): lax.dynamic_slice_in_dim(source_blocks, lax.axis_index('tgt') * side, side)  1.87 us
  transfers between devices with their start and end apart: 20, of which 13 were waited for; matrix products, arithmetic and copies ran while one was open for 9% of the time, Pallas kernels for 8%

profile of v5, /device:TPU:0, one launch (start us, length us, event | category | flops | bytes accessed | tf_op | source)
XLA Modules:
  0.0 75.7 jit_solution(4815838523984677861)
XLA Ops:
  0.6 0.0 copy-start.1
  0.6 0.0 copy-start
  0.7 3.1 %collective-permute-start.2 = (bf16[8,128,256]{2,1,0:T(8,128)(2,1)}, bf16[8,128,256]{2,1,0:T(8,128)(2,1)S(1)}, u32[]{:S(2)}, u32[]{:S(2)}) collective-permute-start(bf16[8,128,256]{2,1,0:T(8,128)(2,1)} %bitcast.22), channel_id=1, source_target_pairs={{0,4},{1,5},{2,6},{3,7},{4,0},{5,1},{6,2},{7,3},{8,12},{9,13},{10,... | collective-permute-start | bytes 1572872 | tf_op jit(solution)/shard_map/ppermute | solution.py:24
  3.7 1.5 %collective-permute-start.5 = (bf16[8,128,256]{2,1,0:T(8,128)(2,1)}, bf16[8,128,256]{2,1,0:T(8,128)(2,1)S(1)}, u32[]{:S(2)}, u32[]{:S(2)}) collective-permute-start(bf16[8,128,256]{2,1,0:T(8,128)(2,1)} %bitcast.23), channel_id=1, source_target_pairs={{0,2},{1,3},{2,0},{3,1},{4,6},{5,7},{6,4},{7,5},{8,10},{9,11},{10,... | collective-permute-start | bytes 1572872 | tf_op jit(solution)/shard_map/ppermute | solution.py:24
  5.3 1.9 %constant_dynamic-slice_fusion = bf16[8,128,256]{2,1,0:T(8,128)(2,1)} fusion(bf16[16,128,256]{2,1,0:T(8,128)(2,1)} %bitcast.20, s32[]{:T(128)S(6)} %select_n.35), kind=kLoop, calls=%fused_computation.16 | loop fusion | bytes 1048580 | tf_op jit(solution)/shard_map/dynamic_slice | solution.py:267
  7.1 2.6 %collective-permute-start.1 = (s32[1,1,2,128]{3,2,1,0:T(2,128)}, s32[1,1,2,128]{3,2,1,0:T(2,128)S(1)}, u32[]{:S(2)}, u32[]{:S(2)}) collective-permute-start(s32[1,1,2,128]{3,2,1,0:T(2,128)} %param.12), channel_id=1, source_target_pairs={{0,8},{1,9},{2,10},{3,11},{4,12},{5,13},{6,14},{7,15},{8,0},{9,1},... | collective-permute-start | bytes 3080 | tf_op jit(solution)/shard_map/ppermute | solution.py:24
  9.7 0.3 collective-permute-start
  10.1 2.6 %collective-permute-start.4 = (bf16[8,128,256]{2,1,0:T(8,128)(2,1)}, bf16[8,128,256]{2,1,0:T(8,128)(2,1)S(1)}, u32[]{:S(2)}, u32[]{:S(2)}) collective-permute-start(bf16[8,128,256]{2,1,0:T(8,128)(2,1)} %constant_dynamic-slice_fusion), channel_id=1, source_target_pairs={{0,8},{1,9},{2,10},{3,11},{4,12},{5,13},{6,14},{7,15},{8,0},{9,1},... | collective-permute-start | bytes 1572872 | tf_op jit(solution)/shard_map/ppermute | solution.py:24
  13.3 1.3 %multiply_reduce_fusion.3 = f32[1024]{0:T(1024)S(1)} fusion(bf16[1024,256]{1,0:T(8,128)(2,1)} %param.8), kind=kLoop, calls=%fused_computation.3 | loop fusion | flops 785408 | bytes 528384 | tf_op jit(solution)/shard_map/reduce_sum | solution.py:29
  14.6 0.7 dynamic-slice_multiply_fusion.refs_1_
  15.3 0.7 broadcast_select_fusion.1.refs_0_
  16.0 0.4 collective-permute-done
  16.4 0.7 iota_compare_fusion
  17.1 0.0 collective-permute-done.1
  17.1 3.7 %tile_lists.1.refs_0_ = s32[1024]{0:T(1024)S(1)} custom-call(s32[1,1,2,128]{3,2,1,0:T(2,128)S(1)} %broadcast_select_fusion.1.refs_0_, s32[1,1,2,128]{3,2,1,0:T(2,128)S(1)} %broadcast_select_fusion.refs_1_), custom_call_target="tpu_custom_call" | custom-call | tf_op jit(solution)/shard_map/tile_lists/pallas_call | solution.py:277
  20.8 0.0 copy-start.2
  20.8 0.8 collective-permute-done.2.refs_8_
  21.5 2.7 %collective-permute-start.3 = (bf16[8,128,256]{2,1,0:T(8,128)(2,1)S(1)}, bf16[8,128,256]{2,1,0:T(8,128)(2,1)S(1)}, u32[]{:S(2)}, u32[]{:S(2)}) collective-permute-start(bf16[8,128,256]{2,1,0:T(8,128)(2,1)S(1)} %collective-permute-done.2.refs_8_), channel_id=1, source_target_pairs={{0,2},{1,3},{2,0},{3,1},{4,6},{5,7},{6,4},{7,5},{8,10},{9,11},{10,... | collective-permute-start | bytes 1572872 | tf_op jit(solution)/shard_map/ppermute | solution.py:24
  24.2 0.2 multiply_reduce_fusion.1
  24.5 0.0 collective-permute-done.5.refs_7_
  24.5 0.2 multiply_reduce_fusion.2
  24.7 0.0 copy-done.1
  24.7 0.0 copy-done
  24.7 2.3 %early_row_pass.1 = (f32[257,128,128]{2,1,0:T(8,128)S(1)}, bf16[32,128,256]{2,1,0:T(8,128)(2,1)S(1)}, bf16[32,128,256]{2,1,0:T(8,128)(2,1)S(1)}, f32[32,128]{1,0...) custom-call(s32[1024]{0:T(1024)S(1)} %tile_lists.1.refs_0_, ...), custom_call_target="tpu_custom_call" | custom-call | tf_op jit(solution)/shard_map/early_row_pass/pallas_call | solution.py:334
  27.0 8.0 %collective-permute-done.4.refs_3_ = bf16[8,128,256]{2,1,0:T(8,128)(2,1)S(1)} collective-permute-done((bf16[8,128,256]{2,1,0:T(8,128)(2,1)}, bf16[8,128,256]{2,1,0:T(8,128)(2,1)S(1)}, u32[]{:S(2)}, u32[]{:S(2)}) %collective-permute-start.4) | collective-permute-done | bytes 524320 | tf_op jit(solution)/shard_map/ppermute | solution.py:24
  35.0 0.0 collective-permute-start.6
  35.0 0.3 collective-permute-done.3.refs_5_
  35.3 0.2 multiply_reduce_fusion.4
  35.5 1.4 %collective-permute-done.6.refs_4_ = bf16[8,128,256]{2,1,0:T(8,128)(2,1)S(1)} collective-permute-done((bf16[8,128,256]{2,1,0:T(8,128)(2,1)S(1)}, bf16[8,128,256]{2,1,0:T(8,128)(2,1)S(1)}, u32[]{:S(2)}, u32[]{:S(2)}) %collective-permute-start.6) | collective-permute-done | bytes 524320 | tf_op jit(solution)/shard_map/ppermute | solution.py:24
  36.9 0.0 copy-done.2
  36.9 2.1 %late_row_pass.1 = (f32[48,128]{1,0:T(8,128)S(1)}, f32[257,128,128]{2,1,0:T(8,128)S(1)}, bf16[32,128,256]{2,1,0:T(8,128)(2,1)S(1)}, bf16[32,128,256]{2,1,0:T(8,1...) custom-call(s32[1024]{0:T(1024)S(1)} %tile_lists.1.refs_0_, ...), custom_call_target="tpu_custom_call", output_to_operand_aliasing={{1}: (7, {}), {2}: (8, {}), {3}: (9, {}), {4}: (10, {}), {5... | custom-call | tf_op jit(solution)/shard_map/late_row_pass/pallas_call | solution.py:334
  39.1 0.1 collective-permute-start.7
  39.2 2.4 %collective-permute-start.8 = (f32[48,128]{1,0:T(8,128)S(1)}, f32[48,128]{1,0:T(8,128)S(1)}, u32[]{:S(2)}, u32[]{:S(2)}) collective-permute-start(f32[48,128]{1,0:T(8,128)S(1)} %get-tuple-element.32.refs_1_.refs_5_), channel_id=1, source_target_pairs={{0,9},{1,8},{2,11},{3,10},{4,13},{5,12},{6,15},{7,14},{8,1},{9,0},... | collective-permute-start | bytes 73736 | tf_op jit(solution)/shard_map/ppermute | solution.py:24
  41.5 0.7 collective-permute-start.9
  42.2 1.7 %collective-permute-done.7.refs_2_ = f32[48,128]{1,0:T(8,128)S(1)} collective-permute-done((f32[48,128]{1,0:T(8,128)S(1)}, f32[48,128]{1,0:T(8,128)S(1)}, u32[]{:S(2)}, u32[]{:S(2)}) %collective-permute-start.7) | collective-permute-done | bytes 24608 | tf_op jit(solution)/shard_map/ppermute | solution.py:24
  43.9 0.0 collective-permute-done.8.refs_3_
  43.9 0.0 collective-permute-done.9.refs_4_
  43.9 3.0 %column_pass.2 = (f32[32,128]{1,0:T(8,128)S(1)}, f32[257,128,128]{2,1,0:T(8,128)S(1)}, f32[32,128]{1,0:T(8,128)S(1)}) custom-call(s32[1024]{0:T(1024)S(1)} %tile_lists.1.refs_0_, f32[48,128]{1,0:T(8,128)S(1)} %get-tuple-element.32.refs_1_.refs_5_, f32[48,128]{1,0:T(8,128)S(1)} %collective-permute-done.7.refs_2_, ...), custom_call_target="tpu_custom_call" | custom-call | tf_op jit(solution)/shard_map/column_pass/pallas_call | solution.py:364
  46.9 3.5 %collective-permute-start.10 = (f32[32,128]{1,0:T(8,128)S(1)}, f32[32,128]{1,0:T(8,128)S(1)}, u32[]{:S(2)}, u32[]{:S(2)}) collective-permute-start(f32[32,128]{1,0:T(8,128)S(1)} %get-tuple-element.34.refs_1_), channel_id=1, source_target_pairs={{0,6},{1,7},{2,4},{3,5},{4,2},{5,3},{6,0},{7,1},{8,14},{9,15},{10,... | collective-permute-start | bytes 49160 | tf_op jit(solution)/shard_map/ppermute | solution.py:24
  50.4 0.0 collective-permute-start.11
  50.4 0.6 collective-permute-start.12
  51.1 0.0 copy-done.3
  51.1 1.2 %collective-permute-done.10.refs_2_ = f32[32,128]{1,0:T(8,128)S(1)} collective-permute-done((f32[32,128]{1,0:T(8,128)S(1)}, f32[32,128]{1,0:T(8,128)S(1)}, u32[]{:S(2)}, u32[]{:S(2)}) %collective-permute-start.10) | collective-permute-done | bytes 16416 | tf_op jit(solution)/shard_map/ppermute | solution.py:24
  52.3 1.9 %collective-permute-done.11.refs_3_ = f32[32,128]{1,0:T(8,128)S(1)} collective-permute-done((f32[32,128]{1,0:T(8,128)S(1)}, f32[32,128]{1,0:T(8,128)S(1)}, u32[]{:S(2)}, u32[]{:S(2)}) %collective-permute-start.11) | collective-permute-done | bytes 16416 | tf_op jit(solution)/shard_map/ppermute | solution.py:24
  54.2 0.0 collective-permute-done.12.refs_4_
  54.2 2.1 %row_pass.1.refs_1_ = f32[32,128]{1,0:T(8,128)S(1)} custom-call(s32[1024]{0:T(1024)S(1)} %tile_lists.1.refs_0_, f32[32,128]{1,0:T(8,128)S(1)} %get-tuple-element.34.refs_1_, f32[32,128]{1,0:T(8,128)S(1)} %collective-permute-done.10.refs_2_, f32[32,128]{1,0:T(8,128)S(1)} %collective-permute-done.11.refs_3_, f32[32,128]{1,0:T(8,128)S(1)} %collective-permute-done.12.refs_4_, ...), custom_call_target="tpu_custom_call" | custom-call | tf_op jit(solution)/shard_map/row_pass/pallas_call | solution.py:364
  56.3 1.2 %collective-permute-start.13 = (f32[32,128]{1,0:T(8,128)S(1)}, f32[32,128]{1,0:T(8,128)S(1)}, u32[]{:S(2)}, u32[]{:S(2)}) collective-permute-start(f32[32,128]{1,0:T(8,128)S(1)} %row_pass.1.refs_1_), channel_id=1, source_target_pairs={{0,8},{1,9},{2,10},{3,11},{4,12},{5,13},{6,14},{7,15},{8,0},{9,1},... | collective-permute-start | bytes 49160 | tf_op jit(solution)/shard_map/ppermute | solution.py:24
  57.5 0.0 collective-permute-start.14
  57.5 1.9 %collective-permute-start.15 = (f32[32,128]{1,0:T(8,128)S(1)}, f32[32,128]{1,0:T(8,128)S(1)}, u32[]{:S(2)}, u32[]{:S(2)}) collective-permute-start(f32[32,128]{1,0:T(8,128)S(1)} %row_pass.1.refs_1_), channel_id=1, source_target_pairs={{0,1},{1,0},{2,3},{3,2},{4,5},{5,4},{6,7},{7,6},{8,9},{9,8},{10,11... | collective-permute-start | bytes 49160 | tf_op jit(solution)/shard_map/ppermute | solution.py:24
  59.4 1.6 %collective-permute-done.13.refs_2_ = f32[32,128]{1,0:T(8,128)S(1)} collective-permute-done((f32[32,128]{1,0:T(8,128)S(1)}, f32[32,128]{1,0:T(8,128)S(1)}, u32[]{:S(2)}, u32[]{:S(2)}) %collective-permute-start.13) | collective-permute-done | bytes 16416 | tf_op jit(solution)/shard_map/ppermute | solution.py:24
  61.0 0.6 collective-permute-done.14.refs_3_
  61.6 0.0 collective-permute-done.15.refs_4_
  61.6 2.1 %column_pass.3 = (f32[32,128]{1,0:T(8,128)S(1)}, f32[32,128]{1,0:T(8,128)S(1)}) custom-call(s32[1024]{0:T(1024)S(1)} %tile_lists.1.refs_0_, f32[32,128]{1,0:T(8,128)S(1)} %row_pass.1.refs_1_, f32[32,128]{1,0:T(8,128)S(1)} %collective-permute-done.13.refs_2_, f32[32,128]{1,0:T(8,128)S(1)} %collective-permute-done.14.refs_3_, ...), custom_call_target="tpu_custom_call" | custom-call | tf_op jit(solution)/shard_map/column_pass/pallas_call | solution.py:364
  63.6 3.0 %collective-permute-start.16 = (f32[32,128]{1,0:T(8,128)S(1)}, f32[32,128]{1,0:T(8,128)S(1)}, u32[]{:S(2)}, u32[]{:S(2)}) collective-permute-start(f32[32,128]{1,0:T(8,128)S(1)} %get-tuple-element.38.refs_0_), channel_id=1, source_target_pairs={{0,6},{1,7},{2,4},{3,5},{4,2},{5,3},{6,0},{7,1},{8,14},{9,15},{10,... | collective-permute-start | bytes 49160 | tf_op jit(solution)/shard_map/ppermute | solution.py:24
  66.6 0.0 collective-permute-start.17
  66.6 0.6 collective-permute-start.18
  67.3 0.3 multiply_reduce_fusion
  67.6 0.7 collective-permute-done.16.refs_1_
  68.3 2.0 %collective-permute-done.17.refs_2_ = f32[32,128]{1,0:T(8,128)S(1)} collective-permute-done((f32[32,128]{1,0:T(8,128)S(1)}, f32[32,128]{1,0:T(8,128)S(1)}, u32[]{:S(2)}, u32[]{:S(2)}) %collective-permute-start.17) | collective-permute-done | bytes 16416 | tf_op jit(solution)/shard_map/ppermute | solution.py:24
  70.4 0.0 collective-permute-done.18.refs_3_
  70.4 1.4 %collective-permute-start.19 = (f32[32,128]{1,0:T(8,128)S(1)}, f32[32,128]{1,0:T(8,128)S(1)}, u32[]{:S(2)}, u32[]{:S(2)}) collective-permute-start(f32[32,128]{1,0:T(8,128)S(1)} %finish.1), channel_id=1, source_target_pairs={{0,8},{1,9},{2,10},{3,11},{4,12},{5,13},{6,14},{7,15},{8,0},{9,1},... | collective-permute-start | bytes 49160 | tf_op jit(solution)/shard_map/ppermute | solution.py:24
  71.8 0.6 fusion.2
  72.5 2.7 %collective-permute-done.19 = f32[32,128]{1,0:T(8,128)S(1)} collective-permute-done((f32[32,128]{1,0:T(8,128)S(1)}, f32[32,128]{1,0:T(8,128)S(1)}, u32[]{:S(2)}, u32[]{:S(2)}) %collective-permute-start.19) | collective-permute-done | bytes 16416 | tf_op jit(solution)/shard_map/ppermute | solution.py:24
  75.1 0.6 fusion
  (9 shorter events, 0.1 us)
Async XLA Ops:
  0.6 24.1 %copy-start.1 = (bf16[1024,256]{1,0:T(8,128)(2,1)S(1)}, bf16[1024,256]{1,0:T(8,128)(2,1)}, u32[]{:S(2)}) copy-start(bf16[1024,256]{1,0:T(8,128)(2,1)} %param.8) | copy-start | bytes 1572868
  0.6 24.1 %copy-start = (bf16[2048,256]{1,0:T(8,128)(2,1)S(1)}, bf16[2048,256]{1,0:T(8,128)(2,1)}, u32[]{:S(2)}) copy-start(bf16[2048,256]{1,0:T(8,128)(2,1)} %param.7) | copy-start | bytes 3145732
  0.7 20.9 %collective-permute-start.2 = (bf16[8,128,256]{2,1,0:T(8,128)(2,1)}, bf16[8,128,256]{2,1,0:T(8,128)(2,1)S(1)}, u32[]{:S(2)}, u32[]{:S(2)}) collective-permute-start(bf16[8,128,256]{2,1,0:T(8,128)(2,1)} %bitcast.22), channel_id=1, source_target_pairs={{0,4},{1,5},{2,6},{3,7},{4,0},{5,1},{6,2},{7,3},{8,12},{9,13},{10,... | collective-permute-start | bytes 1572872 | tf_op jit(solution)/shard_map/ppermute | solution.py:24
  3.7 20.7 %collective-permute-start.5 = (bf16[8,128,256]{2,1,0:T(8,128)(2,1)}, bf16[8,128,256]{2,1,0:T(8,128)(2,1)S(1)}, u32[]{:S(2)}, u32[]{:S(2)}) collective-permute-start(bf16[8,128,256]{2,1,0:T(8,128)(2,1)} %bitcast.23), channel_id=1, source_target_pairs={{0,2},{1,3},{2,0},{3,1},{4,6},{5,7},{6,4},{7,5},{8,10},{9,11},{10,... | collective-permute-start | bytes 1572872 | tf_op jit(solution)/shard_map/ppermute | solution.py:24
  7.1 9.9 %collective-permute-start.1 = (s32[1,1,2,128]{3,2,1,0:T(2,128)}, s32[1,1,2,128]{3,2,1,0:T(2,128)S(1)}, u32[]{:S(2)}, u32[]{:S(2)}) collective-permute-start(s32[1,1,2,128]{3,2,1,0:T(2,128)} %param.12), channel_id=1, source_target_pairs={{0,8},{1,9},{2,10},{3,11},{4,12},{5,13},{6,14},{7,15},{8,0},{9,1},... | collective-permute-start | bytes 3080 | tf_op jit(solution)/shard_map/ppermute | solution.py:24
  9.7 6.7 %collective-permute-start = (s32[1,1]{1,0:T(1,128)}, s32[1,1]{1,0:T(1,128)}, u32[]{:S(2)}, u32[]{:S(2)}) collective-permute-start(s32[1,1]{1,0:T(1,128)} %param.13), channel_id=1, source_target_pairs={{0,8},{1,9},{2,10},{3,11},{4,12},{5,13},{6,14},{7,15},{8,0},{9,1},... | collective-permute-start | bytes 20 | tf_op jit(solution)/shard_map/ppermute | solution.py:24
  10.1 25.0 %collective-permute-start.4 = (bf16[8,128,256]{2,1,0:T(8,128)(2,1)}, bf16[8,128,256]{2,1,0:T(8,128)(2,1)S(1)}, u32[]{:S(2)}, u32[]{:S(2)}) collective-permute-start(bf16[8,128,256]{2,1,0:T(8,128)(2,1)} %constant_dynamic-slice_fusion), channel_id=1, source_target_pairs={{0,8},{1,9},{2,10},{3,11},{4,12},{5,13},{6,14},{7,15},{8,0},{9,1},... | collective-permute-start | bytes 1572872 | tf_op jit(solution)/shard_map/ppermute | solution.py:24
  20.8 16.2 %copy-start.2 = (f32[2048]{0:T(1024)S(1)}, f32[2048]{0:T(1024)}, u32[]{:S(2)}) copy-start(f32[2048]{0:T(1024)} %param.9) | copy-start | bytes 24580
  21.5 13.8 %collective-permute-start.3 = (bf16[8,128,256]{2,1,0:T(8,128)(2,1)S(1)}, bf16[8,128,256]{2,1,0:T(8,128)(2,1)S(1)}, u32[]{:S(2)}, u32[]{:S(2)}) collective-permute-start(bf16[8,128,256]{2,1,0:T(8,128)(2,1)S(1)} %collective-permute-done.2.refs_8_), channel_id=1, source_target_pairs={{0,2},{1,3},{2,0},{3,1},{4,6},{5,7},{6,4},{7,5},{8,10},{9,11},{10,... | collective-permute-start | bytes 1572872 | tf_op jit(solution)/shard_map/ppermute | solution.py:24
  35.0 1.9 %collective-permute-start.6 = (bf16[8,128,256]{2,1,0:T(8,128)(2,1)S(1)}, bf16[8,128,256]{2,1,0:T(8,128)(2,1)S(1)}, u32[]{:S(2)}, u32[]{:S(2)}) collective-permute-start(bf16[8,128,256]{2,1,0:T(8,128)(2,1)S(1)} %collective-permute-done.4.refs_3_), channel_id=1, source_target_pairs={{0,1},{1,0},{2,3},{3,2},{4,5},{5,4},{6,7},{7,6},{8,9},{9,8},{10,11... | collective-permute-start | bytes 1572872 | tf_op jit(solution)/shard_map/ppermute | solution.py:24
  39.1 4.8 %collective-permute-start.7 = (f32[48,128]{1,0:T(8,128)S(1)}, f32[48,128]{1,0:T(8,128)S(1)}, u32[]{:S(2)}, u32[]{:S(2)}) collective-permute-start(f32[48,128]{1,0:T(8,128)S(1)} %get-tuple-element.32.refs_1_.refs_5_), channel_id=1, source_target_pairs={{0,8},{1,9},{2,10},{3,11},{4,12},{5,13},{6,14},{7,15},{8,0},{9,1},... | collective-permute-start | bytes 73736 | tf_op jit(solution)/shard_map/ppermute | solution.py:24
  39.2 4.7 %collective-permute-start.8 = (f32[48,128]{1,0:T(8,128)S(1)}, f32[48,128]{1,0:T(8,128)S(1)}, u32[]{:S(2)}, u32[]{:S(2)}) collective-permute-start(f32[48,128]{1,0:T(8,128)S(1)} %get-tuple-element.32.refs_1_.refs_5_), channel_id=1, source_target_pairs={{0,9},{1,8},{2,11},{3,10},{4,13},{5,12},{6,15},{7,14},{8,1},{9,0},... | collective-permute-start | bytes 73736 | tf_op jit(solution)/shard_map/ppermute | solution.py:24
  41.5 2.4 %collective-permute-start.9 = (f32[48,128]{1,0:T(8,128)S(1)}, f32[48,128]{1,0:T(8,128)S(1)}, u32[]{:S(2)}, u32[]{:S(2)}) collective-permute-start(f32[48,128]{1,0:T(8,128)S(1)} %get-tuple-element.32.refs_1_.refs_5_), channel_id=1, source_target_pairs={{0,1},{1,0},{2,3},{3,2},{4,5},{5,4},{6,7},{7,6},{8,9},{9,8},{10,11... | collective-permute-start | bytes 73736 | tf_op jit(solution)/shard_map/ppermute | solution.py:24
  43.9 7.2 %copy-start.3 = (f32[8192]{0:T(1024)S(1)}, f32[8192]{0:T(1024)}, u32[]{:S(2)}) copy-start(f32[8192]{0:T(1024)} %param.10) | copy-start | bytes 98308
  46.9 5.4 %collective-permute-start.10 = (f32[32,128]{1,0:T(8,128)S(1)}, f32[32,128]{1,0:T(8,128)S(1)}, u32[]{:S(2)}, u32[]{:S(2)}) collective-permute-start(f32[32,128]{1,0:T(8,128)S(1)} %get-tuple-element.34.refs_1_), channel_id=1, source_target_pairs={{0,6},{1,7},{2,4},{3,5},{4,2},{5,3},{6,0},{7,1},{8,14},{9,15},{10,... | collective-permute-start | bytes 49160 | tf_op jit(solution)/shard_map/ppermute | solution.py:24
  50.4 3.7 %collective-permute-start.11 = (f32[32,128]{1,0:T(8,128)S(1)}, f32[32,128]{1,0:T(8,128)S(1)}, u32[]{:S(2)}, u32[]{:S(2)}) collective-permute-start(f32[32,128]{1,0:T(8,128)S(1)} %get-tuple-element.34.refs_1_), channel_id=1, source_target_pairs={{0,4},{1,5},{2,6},{3,7},{4,0},{5,1},{6,2},{7,3},{8,12},{9,13},{10,... | collective-permute-start | bytes 49160 | tf_op jit(solution)/shard_map/ppermute | solution.py:24
  50.4 3.7 %collective-permute-start.12 = (f32[32,128]{1,0:T(8,128)S(1)}, f32[32,128]{1,0:T(8,128)S(1)}, u32[]{:S(2)}, u32[]{:S(2)}) collective-permute-start(f32[32,128]{1,0:T(8,128)S(1)} %get-tuple-element.34.refs_1_), channel_id=1, source_target_pairs={{0,2},{1,3},{2,0},{3,1},{4,6},{5,7},{6,4},{7,5},{8,10},{9,11},{10,... | collective-permute-start | bytes 49160 | tf_op jit(solution)/shard_map/ppermute | solution.py:24
  56.3 4.7 %collective-permute-start.13 = (f32[32,128]{1,0:T(8,128)S(1)}, f32[32,128]{1,0:T(8,128)S(1)}, u32[]{:S(2)}, u32[]{:S(2)}) collective-permute-start(f32[32,128]{1,0:T(8,128)S(1)} %row_pass.1.refs_1_), channel_id=1, source_target_pairs={{0,8},{1,9},{2,10},{3,11},{4,12},{5,13},{6,14},{7,15},{8,0},{9,1},... | collective-permute-start | bytes 49160 | tf_op jit(solution)/shard_map/ppermute | solution.py:24
  57.5 4.1 %collective-permute-start.14 = (f32[32,128]{1,0:T(8,128)S(1)}, f32[32,128]{1,0:T(8,128)S(1)}, u32[]{:S(2)}, u32[]{:S(2)}) collective-permute-start(f32[32,128]{1,0:T(8,128)S(1)} %row_pass.1.refs_1_), channel_id=1, source_target_pairs={{0,9},{1,8},{2,11},{3,10},{4,13},{5,12},{6,15},{7,14},{8,1},{9,0},... | collective-permute-start | bytes 49160 | tf_op jit(solution)/shard_map/ppermute | solution.py:24
  57.5 4.1 %collective-permute-start.15 = (f32[32,128]{1,0:T(8,128)S(1)}, f32[32,128]{1,0:T(8,128)S(1)}, u32[]{:S(2)}, u32[]{:S(2)}) collective-permute-start(f32[32,128]{1,0:T(8,128)S(1)} %row_pass.1.refs_1_), channel_id=1, source_target_pairs={{0,1},{1,0},{2,3},{3,2},{4,5},{5,4},{6,7},{7,6},{8,9},{9,8},{10,11... | collective-permute-start | bytes 49160 | tf_op jit(solution)/shard_map/ppermute | solution.py:24
  63.6 4.7 %collective-permute-start.16 = (f32[32,128]{1,0:T(8,128)S(1)}, f32[32,128]{1,0:T(8,128)S(1)}, u32[]{:S(2)}, u32[]{:S(2)}) collective-permute-start(f32[32,128]{1,0:T(8,128)S(1)} %get-tuple-element.38.refs_0_), channel_id=1, source_target_pairs={{0,6},{1,7},{2,4},{3,5},{4,2},{5,3},{6,0},{7,1},{8,14},{9,15},{10,... | collective-permute-start | bytes 49160 | tf_op jit(solution)/shard_map/ppermute | solution.py:24
  66.6 3.7 %collective-permute-start.17 = (f32[32,128]{1,0:T(8,128)S(1)}, f32[32,128]{1,0:T(8,128)S(1)}, u32[]{:S(2)}, u32[]{:S(2)}) collective-permute-start(f32[32,128]{1,0:T(8,128)S(1)} %get-tuple-element.38.refs_0_), channel_id=1, source_target_pairs={{0,4},{1,5},{2,6},{3,7},{4,0},{5,1},{6,2},{7,3},{8,12},{9,13},{10,... | collective-permute-start | bytes 49160 | tf_op jit(solution)/shard_map/ppermute | solution.py:24
  66.6 3.7 %collective-permute-start.18 = (f32[32,128]{1,0:T(8,128)S(1)}, f32[32,128]{1,0:T(8,128)S(1)}, u32[]{:S(2)}, u32[]{:S(2)}) collective-permute-start(f32[32,128]{1,0:T(8,128)S(1)} %get-tuple-element.38.refs_0_), channel_id=1, source_target_pairs={{0,2},{1,3},{2,0},{3,1},{4,6},{5,7},{6,4},{7,5},{8,10},{9,11},{10,... | collective-permute-start | bytes 49160 | tf_op jit(solution)/shard_map/ppermute | solution.py:24
  70.4 4.7 %collective-permute-start.19 = (f32[32,128]{1,0:T(8,128)S(1)}, f32[32,128]{1,0:T(8,128)S(1)}, u32[]{:S(2)}, u32[]{:S(2)}) collective-permute-start(f32[32,128]{1,0:T(8,128)S(1)} %finish.1), channel_id=1, source_target_pairs={{0,8},{1,9},{2,10},{3,11},{4,12},{5,13},{6,14},{7,15},{8,0},{9,1},... | collective-permute-start | bytes 49160 | tf_op jit(solution)/shard_map/ppermute | solution.py:24
